TPU v7x, 32 devices: a whole 2x2x4 slice. The times are simulated.
32 devices in a mesh: dp: 4 (over y, core), seq: 8 (over z, x).
Axes of the slice: x: 2, y: 2, z: 4, core: 2. Of those that a mesh axis runs over, the one named last changes fastest.
Arguments:
- tokens: float32 [4, 1024, 1152], P('dp', 'seq'), may hold values from -6 to 6
- cotangent: float32 [4, 1024, 1152], P('dp', 'seq'), may hold values from -6 to 6
- routes: int32 [4, 1024, 1], P('dp', 'seq'), may hold values from 0 to 3; in each aligned block of 128 rows (0 to 127, 128 to 255, ..., all dimensions but the last counted through in order) at most 56 rows name the same one
- mixer_gain: bfloat16 [1152], replicated, may hold values from 0.5 to 1.5
- input_proj: bfloat16 [2, 1152, 2304], P(None, None, ('dp', 'seq')), may hold values from -0.1875 to 0.1875
- conv_weight: bfloat16 [4, 2304], P(None, ('dp', 'seq')), may hold values from -3 to 3
- conv_bias: bfloat16 [2304], P(('dp', 'seq')), may hold values from -1.5 to 1.5
- select_proj: bfloat16 [104, 2304], P(None, ('dp', 'seq')), may hold values from -0.125 to 0.125
- step_proj: bfloat16 [72, 2304], P(None, ('dp', 'seq')), may hold values from -0.75 to 0.75
- step_bias: bfloat16 [2304], P(('dp', 'seq')), may hold values from -5 to -2
- decay_log: bfloat16 [16, 2304], P(None, ('dp', 'seq')), may hold values from -4 to 2
- skip_gain: bfloat16 [2304], P(('dp', 'seq')), may hold values from 0.5 to 1.5
- output_proj: bfloat16 [2304, 1152], P(('dp', 'seq')), may hold values from -0.25 to 0.25
- expert_gain: bfloat16 [1152], replicated, may hold values from 0.5 to 1.5
- router: bfloat16 [4, 1152], replicated, may hold values from -0.125 to 0.125
- expert_up: bfloat16 [1152, 12288], P('seq', 'dp'), may hold values from -0.1875 to 0.1875
- expert_down: bfloat16 [12288, 1152], P('dp', 'seq'), may hold values from -0.21875 to 0.21875
Outputs:
- output: float32 [4, 1024, 1152], P('dp', 'seq')
- input_grad: float32 [4, 1024, 1152], P('dp', 'seq')
- grad_mixer_gain: float32 [1152], replicated
- grad_input_proj: float32 [2, 1152, 2304], P(None, None, ('dp', 'seq'))
- grad_conv_weight: float32 [4, 2304], P(None, ('dp', 'seq'))
- grad_conv_bias: float32 [2304], P(('dp', 'seq'))
- grad_select_proj: float32 [104, 2304], P(None, ('dp', 'seq'))
- grad_step_proj: float32 [72, 2304], P(None, ('dp', 'seq'))
- grad_step_bias: float32 [2304], P(('dp', 'seq'))
- grad_decay_log: float32 [16, 2304], P(None, ('dp', 'seq'))
- grad_skip_gain: float32 [2304], P(('dp', 'seq'))
- grad_output_proj: float32 [2304, 1152], P(('dp', 'seq'))
- grad_expert_gain: float32 [1152], replicated
- grad_router: float32 [4, 1152], replicated
- grad_expert_up: float32 [1152, 12288], P('seq', 'dp')
- grad_expert_down: float32 [12288, 1152], P('dp', 'seq')
Inputs may be any that keep to these rules, and one draw needn't show every extreme that they name: `routes`: among the tokens of one sequence block (128 consecutive tokens of a sequence, starting at a multiple of 128) no expert is the route of more than 56 tokens; in every draw some block sends exactly 56 tokens to one expert.
All inputs are finite; a program needn't handle non-finite values.
Results may differ from a plain program's by a relative error of at most 0.015.
Values may be sent and summed in bfloat16 or wider, within the bound.
A program may use at most 192 MiB of HBM per device.

v0:
```python
import jax
import jax.numpy as jnp
from jax import lax
from jax.sharding import PartitionSpec as P

CAP = 56


HIGHEST = lax.Precision.HIGHEST


def from_behind(value, axis, by):
    size = lax.axis_size(axis)
    pairs = [(i, i + by) for i in range(size) if 0 <= i + by < size]
    return lax.ppermute(value, axis, pairs)


def rms_norm(values, gain):
    return values * lax.rsqrt(jnp.mean(values * values, axis=-1, keepdims=True) + 1e-05) * gain


def gelu_exact(values):
    return jax.nn.gelu(values, approximate=False)


def inner_rows(left, right, precision=None):
    return lax.dot_general(
        left,
        right,
        (((0,), (0,)), ((), ())),
        precision=precision,
        preferred_element_type=jnp.float32,
    )


def outer_cols(left, right, precision=None):
    return lax.dot_general(
        left,
        right,
        (((1,), (1,)), ((), ())),
        precision=precision,
        preferred_element_type=jnp.float32,
    )


def scan_block(length):
    return min(128, max(8, length // 16))


def split_by(values, block):
    return values.reshape(values.shape[0] // block, block, values.shape[-1])


def forward_chain(start, delta, state_in, state_out, conv_act, rates):
    length = delta.shape[0]
    inner = delta.shape[1]
    block = scan_block(length)

    def forward_turn(state_now, pieces):
        block_delta, block_in, block_out, block_act = pieces
        first = state_now
        outs = []
        for index in range(block):
            state_now = (
                jnp.exp(block_delta[index][None, :] * rates) * state_now
                + block_in[index][:, None] * (block_delta[index] * block_act[index])[None, :]
            )
            outs.append(jnp.sum(block_out[index][:, None] * state_now, axis=0))
        return (state_now, (jnp.stack(outs), first))

    final, (scanned, starts) = lax.scan(
        forward_turn,
        start,
        (
            split_by(delta, block),
            split_by(state_in, block),
            split_by(state_out, block),
            split_by(conv_act, block),
        ),
    )
    return (final, scanned.reshape(length, inner), starts)


def backward_chain(after, starts, delta, state_in, state_out, conv_act, grad_mixed, rates):
    length = delta.shape[0]
    inner = delta.shape[1]
    state = rates.shape[0]
    block = scan_block(length)

    def backward_turn(carry, pieces):
        incoming, rate_total = carry
        start, block_delta, block_in, block_out, block_act, block_grad = pieces
        decays = []
        priors = []
        posts = []
        state_now = start
        for index in range(block):
            decay = jnp.exp(block_delta[index][None, :] * rates)
            priors.append(state_now)
            state_now = (
                decay * state_now
                + block_in[index][:, None] * (block_delta[index] * block_act[index])[None, :]
            )
            decays.append(decay)
            posts.append(state_now)
        grad_delta_list = [None] * block
        grad_act_list = [None] * block
        grad_in_list = [None] * block
        grad_out_list = [None] * block
        for index in range(block - 1, -1, -1):
            grad_state = block_out[index][:, None] * block_grad[index][None, :] + incoming
            weighted = grad_state * priors[index] * decays[index]
            input_side = jnp.sum(grad_state * block_in[index][:, None], axis=0)
            grad_delta_list[index] = (
                jnp.sum(weighted * rates, axis=0) + block_act[index] * input_side
            )
            grad_act_list[index] = block_delta[index] * input_side
            grad_in_list[index] = jnp.sum(
                grad_state * (block_delta[index] * block_act[index])[None, :], axis=1
            )
            grad_out_list[index] = jnp.sum(posts[index] * block_grad[index][None, :], axis=1)
            rate_total = rate_total + weighted * block_delta[index][None, :]
            incoming = decays[index] * grad_state
        return (
            (incoming, rate_total),
            (
                jnp.stack(grad_delta_list),
                jnp.stack(grad_act_list),
                jnp.stack(grad_in_list),
                jnp.stack(grad_out_list),
            ),
        )

    begin = (after, jnp.zeros(rates.shape, jnp.float32))
    (unused_start, rate_total), (grad_delta, grad_act, grad_in, grad_out) = lax.scan(
        backward_turn,
        begin,
        (
            starts,
            split_by(delta, block),
            split_by(state_in, block),
            split_by(state_out, block),
            split_by(conv_act, block),
            split_by(grad_mixed, block),
        ),
        reverse=True,
    )
    return (
        grad_delta.reshape(length, inner),
        grad_act.reshape(length, inner),
        grad_in.reshape(length, state),
        grad_out.reshape(length, state),
        rate_total,
    )


def carry_states(through, local, backward):
    empty = jnp.zeros_like(local)
    direction = -1 if backward else 1

    def carry_turn(index, incoming):
        return from_behind(through * incoming + local, "seq", direction)

    return lax.fori_loop(0, lax.axis_size("seq") - 1, carry_turn, empty)


def keep_values(values):
    return values


def edge_forward(values):
    return from_behind(values, "seq", 1)


def edge_backward(values):
    return from_behind(values, "seq", -1)


def chained_start(delta, state_in, state_out, conv_act, rates):
    zero_state = jnp.zeros(rates.shape, jnp.float32)
    local_state, unused_out, unused_starts = forward_chain(
        zero_state, delta, state_in, state_out, conv_act, rates
    )
    through = jnp.exp(rates * jnp.sum(delta, axis=0)[None, :])
    return (carry_states(through, local_state, False), through)


def chained_back(delta, state_out, grad_mixed, rates, through):
    block = scan_block(delta.shape[0])

    def chained_turn(incoming, pieces):
        block_delta, block_out, block_grad = pieces
        for index in range(block - 1, -1, -1):
            grad_state = block_out[index][:, None] * block_grad[index][None, :] + incoming
            incoming = jnp.exp(block_delta[index][None, :] * rates) * grad_state
        return (incoming, None)

    local_grad, unused = lax.scan(
        chained_turn,
        jnp.zeros(rates.shape, jnp.float32),
        (split_by(delta, block), split_by(state_out, block), split_by(grad_mixed, block)),
        reverse=True,
    )
    return carry_states(through, local_grad, True)


def mixer_forward(normed_in, weights, edge_fn, select_fn, start_fn):
    w_input, w_conv, b_conv, w_select, w_step, b_step, w_decay, w_skip = weights
    length = normed_in.shape[0]
    rank = w_step.shape[0]
    state = w_decay.shape[0]
    kernel = w_conv.shape[0]
    conv_input = jnp.dot(normed_in, w_input[0], preferred_element_type=jnp.float32)
    gate_branch = jnp.dot(normed_in, w_input[1], preferred_element_type=jnp.float32)
    edge = edge_fn(conv_input[length - kernel + 1 :])
    extended = jnp.concatenate([edge, conv_input], axis=0)
    conv_taps = w_conv.astype(jnp.float32)
    conv_sum = b_conv.astype(jnp.float32) + sum(
        (conv_taps[k] * extended[k : k + length] for k in range(kernel))
    )
    conv_act, silu_pull_act = jax.vjp(jax.nn.silu, conv_sum)
    conv_low = conv_act.astype(jnp.bfloat16)
    selected = select_fn(outer_cols(conv_low, w_select))
    low_rank = selected[:, :rank]
    state_in = selected[:, rank : rank + state]
    state_out = selected[:, rank + state :]
    step_pre = jnp.dot(low_rank, w_step.astype(jnp.float32), precision=HIGHEST) + b_step.astype(
        jnp.float32
    )
    delta = jax.nn.softplus(step_pre)
    rates = -jnp.exp(w_decay.astype(jnp.float32))
    incoming, through = start_fn(delta, state_in, state_out, conv_act, rates)
    unused_end, scanned, starts = forward_chain(
        incoming, delta, state_in, state_out, conv_act, rates
    )
    mixed = scanned + w_skip.astype(jnp.float32) * conv_act
    silu_gate, silu_pull_gate = jax.vjp(jax.nn.silu, gate_branch)
    mixer_low = (mixed * silu_gate).astype(jnp.bfloat16)
    return (
        extended,
        conv_act,
        silu_pull_act,
        conv_low,
        low_rank,
        state_in,
        state_out,
        step_pre,
        delta,
        rates,
        starts,
        mixed,
        silu_gate,
        silu_pull_gate,
        through,
        mixer_low,
    )


def mixer_backward(grad_y, saved, weights, chain_back, select_back, edge_back):
    (
        extended,
        conv_act,
        silu_pull_act,
        conv_low,
        low_rank,
        state_in,
        state_out,
        step_pre,
        delta,
        rates,
        starts,
        mixed,
        silu_gate,
        silu_pull_gate,
        through,
        mixer_low,
    ) = saved
    w_input, w_conv, b_conv, w_select, w_step, b_step, w_decay, w_skip = weights
    length = grad_y.shape[0]
    kernel = w_conv.shape[0]
    conv_taps = w_conv.astype(jnp.float32)
    grad_mixed = grad_y * silu_gate
    grad_gate_branch = silu_pull_gate(grad_y * mixed)[0]
    grad_skip = jnp.sum(grad_mixed * conv_act, axis=0)
    after = chain_back(delta, state_out, grad_mixed, rates, through)
    grad_delta, grad_act_scan, grad_state_in, grad_state_out, grad_rates = backward_chain(
        after, starts, delta, state_in, state_out, conv_act, grad_mixed, rates
    )
    grad_decay = grad_rates * rates
    grad_conv_act = grad_mixed * w_skip.astype(jnp.float32) + grad_act_scan
    grad_step_pre = grad_delta * jax.nn.sigmoid(step_pre)
    grad_step_bias = jnp.sum(grad_step_pre, axis=0)
    grad_step_w = inner_rows(low_rank, grad_step_pre, HIGHEST)
    grad_low_rank = outer_cols(grad_step_pre, w_step.astype(jnp.float32), HIGHEST)
    summed = select_back((grad_low_rank, grad_state_in, grad_state_out))
    grad_selected = jnp.concatenate([summed[0], summed[1], summed[2]], axis=1).astype(jnp.bfloat16)
    grad_select_w = inner_rows(grad_selected, conv_low)
    grad_conv_act = grad_conv_act + jnp.dot(
        grad_selected, w_select, preferred_element_type=jnp.float32
    )
    grad_conv_sum = silu_pull_act(grad_conv_act)[0]
    edge_grad = edge_back(grad_conv_sum[: kernel - 1])
    later_back = jnp.concatenate([grad_conv_sum, edge_grad], axis=0)
    grad_conv_input = sum(
        (conv_taps[k] * later_back[kernel - 1 - k : kernel - 1 - k + length] for k in range(kernel))
    )
    grad_conv_w = jnp.stack(
        [jnp.sum(grad_conv_sum * extended[k : k + length], axis=0) for k in range(kernel)]
    )
    grad_conv_b = jnp.sum(grad_conv_sum, axis=0)
    return (
        grad_conv_input.astype(jnp.bfloat16),
        grad_gate_branch.astype(jnp.bfloat16),
        (
            grad_conv_w,
            grad_conv_b,
            grad_select_w,
            grad_step_w,
            grad_step_bias,
            grad_decay,
            grad_skip,
        ),
    )


def body(
    tokens,
    cotangent,
    routes,
    mixer_gain,
    input_proj,
    conv_weight,
    conv_bias,
    select_proj,
    step_proj,
    step_bias,
    decay_log,
    skip_gain,
    output_proj,
    expert_gain,
    router,
    expert_up,
    expert_down,
):
    rows = tokens.shape[1]
    width = tokens.shape[2]
    shards = (
        input_proj,
        conv_weight,
        conv_bias,
        select_proj,
        step_proj,
        step_bias,
        decay_log,
        skip_gain,
        output_proj,
    )
    w_up, w_down = (
        lax.all_gather(expert_up, "seq", axis=0, tiled=True),
        lax.all_gather(expert_down, "seq", axis=1, tiled=True),
    )
    experts = router.shape[0]
    copies = lax.axis_size("dp") // experts
    capacity = CAP
    x_in = tokens.reshape(rows, width)
    gain_one = mixer_gain.astype(jnp.float32)
    normed = rms_norm(x_in, gain_one).astype(jnp.bfloat16)
    gathered = (
        lax.all_gather(shards[0], ("dp", "seq"), axis=2, tiled=True),
        lax.all_gather(shards[1], ("dp", "seq"), axis=1, tiled=True),
        lax.all_gather(shards[2], ("dp", "seq"), axis=0, tiled=True),
        lax.all_gather(shards[3], ("dp", "seq"), axis=1, tiled=True),
        lax.all_gather(shards[4], ("dp", "seq"), axis=1, tiled=True),
        lax.all_gather(shards[5], ("dp", "seq"), axis=0, tiled=True),
        lax.all_gather(shards[6], ("dp", "seq"), axis=1, tiled=True),
        lax.all_gather(shards[7], ("dp", "seq"), axis=0, tiled=True),
        lax.all_gather(shards[8], ("dp", "seq"), axis=0, tiled=True),
    )
    saved = mixer_forward(normed, gathered[:8], edge_forward, keep_values, chained_start)
    mixer_low = saved[-1]
    w_output = gathered[8]
    middle = x_in + jnp.dot(mixer_low, w_output, preferred_element_type=jnp.float32)
    gain_two = expert_gain.astype(jnp.float32)
    normed_two = rms_norm(middle, gain_two).astype(jnp.bfloat16)
    probs = jax.nn.softmax(outer_cols(normed_two, router), axis=-1)
    route = routes.reshape(rows)
    chosen = (route[:, None] == lax.broadcasted_iota(jnp.int32, (rows, experts), 1)).astype(
        jnp.float32
    )
    gate = jnp.sum(chosen * probs, axis=1)
    earlier = (
        lax.broadcasted_iota(jnp.int32, (rows, rows), 0)
        > lax.broadcasted_iota(jnp.int32, (rows, rows), 1)
    ).astype(jnp.float32)
    before = jnp.dot(earlier, chosen, precision=HIGHEST)
    position = jnp.sum(before * chosen, axis=1).astype(jnp.int32)
    slot = route * capacity + position
    dispatch_table = (
        slot[None, :] == lax.broadcasted_iota(jnp.int32, (experts * capacity, rows), 0)
    ).astype(jnp.bfloat16)
    buffer = jnp.dot(dispatch_table, normed_two, preferred_element_type=jnp.float32).astype(
        jnp.bfloat16
    )
    send = jnp.repeat(buffer.reshape(experts, capacity, width), copies, axis=0)
    received = lax.all_to_all(send, "dp", split_axis=0, concat_axis=0, tiled=True)
    sources = received.shape[0]
    expert_rows = received.reshape(-1, width)
    expert_pre = jnp.dot(expert_rows, w_up, preferred_element_type=jnp.float32)
    expert_act, gelu_pull = jax.vjp(gelu_exact, expert_pre)
    act_low = expert_act.astype(jnp.bfloat16)
    partial_out = jnp.dot(act_low, w_down, preferred_element_type=jnp.float32).reshape(
        sources, capacity, width
    )
    returned = lax.all_to_all(
        partial_out.astype(jnp.bfloat16), "dp", split_axis=0, concat_axis=0, tiled=True
    ).astype(partial_out.dtype)
    expert_out = jnp.sum(returned.reshape(experts, copies, capacity, width), axis=1).reshape(
        experts * capacity, width
    )
    picked = jnp.take(expert_out, slot, axis=0)
    output = middle + gate[:, None] * picked
    grad_out = cotangent.reshape(rows, width)
    grad_pick = (gate[:, None] * grad_out).astype(jnp.bfloat16)
    grad_gate = jnp.sum(grad_out * picked, axis=1)
    grad_buffer = jnp.dot(dispatch_table, grad_pick, preferred_element_type=jnp.float32).astype(
        jnp.bfloat16
    )
    grad_send = jnp.repeat(grad_buffer.reshape(experts, capacity, width), copies, axis=0)
    grad_rows = lax.all_to_all(grad_send, "dp", split_axis=0, concat_axis=0, tiled=True)
    grad_flat = grad_rows.reshape(-1, width)
    grad_down_w = inner_rows(act_low, grad_flat)
    grad_act = outer_cols(grad_flat, w_down)
    grad_pre = gelu_pull(grad_act)[0].astype(jnp.bfloat16)
    grad_up_w = inner_rows(expert_rows, grad_pre)
    grad_in_rows = outer_cols(grad_pre, w_up).reshape(sources, capacity, width)
    grad_back = lax.all_to_all(
        grad_in_rows.astype(jnp.bfloat16), "dp", split_axis=0, concat_axis=0, tiled=True
    ).astype(grad_in_rows.dtype)
    grad_slots = jnp.sum(grad_back.reshape(experts, copies, capacity, width), axis=1).reshape(
        experts * capacity, width
    )
    grad_logits = gate[:, None] * (chosen - probs) * grad_gate[:, None]
    router_full = router.astype(jnp.float32)
    grad_normed_two = jnp.take(grad_slots, slot, axis=0) + jnp.dot(
        grad_logits, router_full, precision=HIGHEST
    )
    grad_router = inner_rows(grad_logits, normed_two.astype(jnp.float32), HIGHEST)
    unused_two, pull_two = jax.vjp(rms_norm, middle, gain_two)
    grad_middle_norm, grad_gain_two = pull_two(grad_normed_two)
    grad_middle = grad_out + grad_middle_norm
    grad_middle_low = grad_middle.astype(jnp.bfloat16)
    w_input = gathered[0]
    grad_output_w = inner_rows(mixer_low, grad_middle_low)
    grad_y = outer_cols(grad_middle_low, w_output)
    grad_conv_input, grad_gate_branch, mixer_part = mixer_backward(
        grad_y, saved, gathered[:8], chained_back, keep_values, edge_backward
    )
    taps_grad, bias_grad, select_grad, step_grad, shift_grad, decay_grad, skip_grad = mixer_part
    grad_normed = outer_cols(grad_conv_input, w_input[0]) + outer_cols(grad_gate_branch, w_input[1])
    grad_input_w = jnp.stack(
        [inner_rows(normed, grad_conv_input), inner_rows(normed, grad_gate_branch)]
    )
    mixer_grads = (
        lax.psum_scatter(grad_input_w, ("dp", "seq"), scatter_dimension=2, tiled=True),
        lax.psum_scatter(taps_grad, ("dp", "seq"), scatter_dimension=1, tiled=True),
        lax.psum_scatter(bias_grad, ("dp", "seq"), scatter_dimension=0, tiled=True),
        lax.psum_scatter(select_grad, ("dp", "seq"), scatter_dimension=1, tiled=True),
        lax.psum_scatter(step_grad, ("dp", "seq"), scatter_dimension=1, tiled=True),
        lax.psum_scatter(shift_grad, ("dp", "seq"), scatter_dimension=0, tiled=True),
        lax.psum_scatter(decay_grad, ("dp", "seq"), scatter_dimension=1, tiled=True),
        lax.psum_scatter(skip_grad, ("dp", "seq"), scatter_dimension=0, tiled=True),
        lax.psum_scatter(grad_output_w, ("dp", "seq"), scatter_dimension=0, tiled=True),
    )
    unused_one, pull_one = jax.vjp(rms_norm, x_in, gain_one)
    grad_in_norm, grad_gain_one = pull_one(grad_normed)
    grad_tokens = grad_middle + grad_in_norm
    expert_grads = (
        lax.psum_scatter(
            grad_up_w.astype(jnp.bfloat16), "seq", scatter_dimension=0, tiled=True
        ).astype(jnp.float32),
        lax.psum_scatter(
            grad_down_w.astype(jnp.bfloat16), "seq", scatter_dimension=1, tiled=True
        ).astype(jnp.float32),
    )
    small_sums = lax.psum((grad_gain_one, grad_gain_two, grad_router), ("dp", "seq"))
    return (
        output.reshape(tokens.shape),
        grad_tokens.reshape(tokens.shape),
        small_sums[0],
        mixer_grads[0],
        mixer_grads[1],
        mixer_grads[2],
        mixer_grads[3],
        mixer_grads[4],
        mixer_grads[5],
        mixer_grads[6],
        mixer_grads[7],
        mixer_grads[8],
        small_sums[1],
        small_sums[2],
        expert_grads[0],
        expert_grads[1],
    )


def solution(mesh):
    placed = (
        P("dp", "seq", None),
        P("dp", "seq", None),
        P("dp", "seq", None),
        P(),
        P(None, None, ("dp", "seq")),
        P(None, ("dp", "seq")),
        P(("dp", "seq")),
        P(None, ("dp", "seq")),
        P(None, ("dp", "seq")),
        P(("dp", "seq")),
        P(None, ("dp", "seq")),
        P(("dp", "seq")),
        P(("dp", "seq"), None),
        P(),
        P(),
        P("seq", "dp"),
        P("dp", "seq"),
    )
    return jax.shard_map(
        body,
        mesh=mesh,
        in_specs=placed,
        out_specs=(
            P("dp", "seq", None),
            P("dp", "seq", None),
            P(),
            P(None, None, ("dp", "seq")),
            P(None, ("dp", "seq")),
            P(("dp", "seq")),
            P(None, ("dp", "seq")),
            P(None, ("dp", "seq")),
            P(("dp", "seq")),
            P(None, ("dp", "seq")),
            P(("dp", "seq")),
            P(("dp", "seq"), None),
            P(),
            P(),
            P("seq", "dp"),
            P("dp", "seq"),
        ),
        check_vma=False,
    )
```

profile of v0, /device:TPU:31, one launch (start us, length us, event | category | flops | bytes accessed | tf_op | source)
XLA Modules:
  0.0 2081.3 jit_solution(14161114678847000698)
XLA Ops:
  10.2 68.7 %all_gather.38 = bf16[72,2304]{0,1:T(8,128)(2,1)S(1)} all-gather(bf16[72,72]{0,1:T(8,128)(2,1)S(1)} %copy.69), channel_id=1, replica_groups=mesh['dp'=4,'seq'=8] {'dp','seq'}, dimensions={1}, use_global_device_ids=true | all-gather | bytes 342144 | tf_op jit(solution)/shard_map/all_gather | solution.py:373
  78.9 70.1 %all_gather.37 = bf16[104,2304]{0,1:T(8,128)(2,1)S(1)} all-gather(bf16[104,72]{0,1:T(8,128)(2,1)S(1)} %copy-done.67), channel_id=1, replica_groups=mesh['dp'=4,'seq'=8] {'dp','seq'}, dimensions={1}, use_global_device_ids=true | all-gather | bytes 494208 | tf_op jit(solution)/shard_map/all_gather | solution.py:372
  149.7 65.1 %all-gather.1 = bf16[32,72,4]{1,2,0:T(4,128)(2,1)S(1)} all-gather(bf16[1,72,4]{1,2,0:T(4,128)(2,1)S(1)} %bitcast.439), channel_id=1, replica_groups=mesh['dp'=4,'seq'=8] {'dp','seq'}, dimensions={0}, use_global_device_ids=true | all-gather | bytes 19008 | tf_op jit(solution)/shard_map/all_gather | solution.py:370
  215.0 68.3 %all-gather = bf16[32,72,16]{1,2,0:T(8,128)(2,1)S(1)} all-gather(bf16[1,72,16]{1,2,0:T(8,128)(2,1)S(1)} %bitcast.438), channel_id=1, replica_groups=mesh['dp'=4,'seq'=8] {'dp','seq'}, dimensions={0}, use_global_device_ids=true | all-gather | bytes 76032 | tf_op jit(solution)/shard_map/all_gather | solution.py:375
  291.9 43.3 %all-reduce.14 = (bf16[2304]{0:T(1024)(128)(2,1)S(1)}, bf16[2304]{0:T(1024)(128)(2,1)S(1)}, bf16[2304]{0:T(1024)(128)(2,1)S(1)}) all-reduce(bf16[2304]{0:T(1024)(128)(2,1)S(1)} %dynamic-update-slice.2, bf16[2304]{0:T(1024)(128)(2,1)S(1)} %dynamic-update-slice.1, ...), channel_id=1, replica_groups=mesh['dp'=4,'seq'=8] {'dp','seq'}, use_global_device_ids=true, to_apply=%add.2 | all-reduce | flops 6912 | bytes 27648
  335.7 4.5 fusion.138
  344.3 52.1 %while.88 = (s32[]{:T(128)}, f32[16,2304]{1,0:T(8,128)S(1)}, f32[16,8,2304]{2,1,0:T(8,128)}, f32[16,2304]{1,0:T(8,128)S(1)}, f32[16,8,16]{2,1,0:T(8,128)}, /*ind...) while((s32[]{:T(128)}, f32[16,2304]{1,0:T(8,128)S(1)}, ...), condition=%wide.region_3.4_spmd.clone, body=%wide.region_2.3_spmd.clone.sunk | while | flops 1234954 | bytes 1108759 | solution.py:71
  397.2 49.4 %while.85 = (s32[]{:T(128)}, f32[16,2304]{1,0:T(8,128)S(1)}, f32[16,2304]{1,0:T(8,128)S(1)}, f32[16,2304]{1,0:T(8,128)S(1)}, s32[]{:T(128)}) while((s32[]{:T(128)}, f32[16,2304]{1,0:T(8,128)S(1)}, f32[16,2304]{1,0:T(8,128)S(1)}, f32[16,2304]{1,0:T(8,128)S(1)}, s32[]{:T(128)}) %tuple.410), condition=%wide.region_5.6_spmd, body=%wide.region_4.5_spmd.sunk | while | flops 73730 | bytes 1179749 | solution.py:164
  398.5 4.6 collective-permute-done
  404.5 5.2 collective-permute-done
  411.0 5.5 collective-permute-done
  417.8 5.5 collective-permute-done
  424.6 5.5 collective-permute-done
  431.4 6.7 collective-permute-done
  439.5 7.1 collective-permute-done
  447.8 85.2 %while.86 = (s32[]{:T(128)}, f32[16,2304]{1,0:T(8,128)S(1)}, f32[16,8,2304]{2,1,0:T(8,128)}, f32[16,16,2304]{2,1,0:T(8,128)}, f32[16,8,2304]{2,1,0:T(8,128)}, /*...) while((s32[]{:T(128)}, f32[16,2304]{1,0:T(8,128)S(1)}, ...), condition=%wide.region_15.16_spmd, body=%wide.region_6.15_spmd.sunk | while | flops 2654217 | bytes 2770605 | solution.py:71
  532.9 5.8 multiply_convert_fusion.1
  543.8 12.7 all-to-all-start
  557.9 5.4 all-to-all-done
  563.3 5.6 all-to-all-start.2
  569.0 6.5 fusion.145
  575.7 11.2 add_convert_fusion
  590.5 5.4 all-to-all-start.1
  595.9 6.6 convolution_convert_fusion.2
  602.7 6.0 all-to-all-start.3
  623.2 4.2 fusion.113
  630.3 50.9 %while.89 = (s32[]{:T(128)}, f32[16,2304]{1,0:T(8,128)S(1)}, f32[16,8,2304]{2,1,0:T(8,128)}, f32[16,2304]{1,0:T(8,128)S(1)}, f32[16,8,16]{2,1,0:T(8,128)}, /*ind...) while((s32[]{:T(128)}, f32[16,2304]{1,0:T(8,128)S(1)}, ...), condition=%wide.region_24.26_spmd.clone, body=%wide.region_23.25_spmd.clone.sunk | while | flops 1216523 | bytes 887595 | solution.py:198
  681.2 46.6 %while.87 = (s32[]{:T(128)}, f32[16,2304]{1,0:T(8,128)S(1)}, f32[16,2304]{1,0:T(8,128)S(1)}, f32[16,2304]{1,0:T(8,128)S(1)}, s32[]{:T(128)}) while((s32[]{:T(128)}, f32[16,2304]{1,0:T(8,128)S(1)}, f32[16,2304]{1,0:T(8,128)S(1)}, f32[16,2304]{1,0:T(8,128)S(1)}, s32[]{:T(128)}) %tuple.452), condition=%wide.region_26.28_spmd, body=%wide.region_25.27_spmd.sunk | while | flops 73730 | bytes 1179749 | solution.py:164
  681.3 4.5 collective-permute-start.1
  688.4 4.1 collective-permute-start.1
  706.7 4.7 collective-permute-start.1
  713.5 4.7 collective-permute-start.1
  720.4 4.7 collective-permute-start.1
  731.3 299.6 %while.90 = (s32[]{:T(128)}, f32[16,2304]{1,0:T(8,128)S(1)}, f32[16,2304]{1,0:T(8,128)S(1)}, f32[16,8,2304]{2,1,0:T(8,128)}, f32[16,8,2304]{2,1,0:T(8,128)}, /*i...) while((s32[]{:T(128)}, f32[16,2304]{1,0:T(8,128)S(1)}, ...), condition=%wide.region_60.62_spmd.clone, body=%wide.region_27.61_spmd.clone.sunk | while | flops 8441611 | bytes 6761259 | solution.py:135
  1039.2 5.1 collective-permute-start.3
  1045.1 5.8 convolution_bitcast_fusion
  1053.1 5.6 convolution_bitcast_fusion.1
  1062.1 15.8 pad_maximum_fusion
  1077.8 34.1 %copy.74 = f32[2,1152,2304]{1,0,2:T(2,128)} copy(f32[2,1152,2304]{2,1,0:T(8,128)} %pad_maximum_fusion) | data formatting | bytes 42467328 | tf_op jit(solution)/shard_map/stack | solution.py:460
  1113.0 6.3 convolution_convert_fusion.1
  1120.3 6.2 convolution_convert_fusion
  1130.4 5.6 fusion.111
  1137.6 58.3 %all-reduce.18.cloned.1.call-done = (f32[1152]{0:T(1024)}, f32[4,2304]{1,0:T(4,128)}, f32[2304]{0:T(1024)}, f32[2304]{0:T(1024)}, f32[2304]{0:T(1024)}, /*index=5*/f32[1152]{0:T(1024)}, f32[4,1152]{1,0:T(4,128)}) async-done(((f32[1152]{0:T(1024)}, f32[4,2304]{1,0:T(4,128)}, f32[2304]{0:T(1024)}, f32[2304]{0:T(1024)}, f32[2304]{0:T(1024)}, /*index=5*/f32[1152]{0:T(1024)}, f32[4,1152]{1,0:T(4,128)}), ...) | async-done | bytes 92176 | tf_op jit(solution)/shard_map/psum | solution.py:485
  1201.0 359.8 %all-reduce.20.cloned.1.call-done = (f32[2,1152,2304]{1,0,2:T(2,128)}, f32[72,2304]{1,0:T(8,128)}, f32[16,2304]{1,0:T(8,128)}) async-done(((f32[2,1152,2304]{1,0,2:T(2,128)}, f32[72,2304]{1,0:T(8,128)}, f32[16,2304]{1,0:T(8,128)}), (f32[2,1152,2304]{1,0,2:T(2,128)}, f32[72,2304]{1,0:T(8,128)}, f32[16,2304]{1,0:T(8,128)})) %all-reduce.20.cloned.1.call-update) | async-done | bytes 22044688
  1565.6 127.6 %reduce-scatter.12.cloned.1.call-done = bf16[144,3072]{1,0:T(8,128)(2,1)} async-done(((bf16[1152,3072]{1,0:T(8,128)(2,1)}), bf16[144,3072]{1,0:T(8,128)(2,1)}) %reduce-scatter.12.cloned.1.call-update) | async-done | bytes 884752 | tf_op jit(solution)/shard_map/reduce_scatter | solution.py:478
  1695.8 129.6 %reduce-scatter.14.cloned.1.call-done = bf16[3072,144]{0,1:T(8,128)(2,1)} async-done(((bf16[3072,1152]{0,1:T(8,128)(2,1)}), bf16[3072,144]{0,1:T(8,128)(2,1)}) %reduce-scatter.14.cloned.1.call-update) | async-done | bytes 884752 | tf_op jit(solution)/shard_map/reduce_scatter | solution.py:481
  1828.0 97.2 %reduce-scatter.16.cloned.1.call-done = f32[104,72]{0,1:T(8,128)} async-done(((f32[104,2304]{0,1:T(8,128)}), f32[104,72]{0,1:T(8,128)}) %reduce-scatter.16.cloned.1.call-update) | async-done | bytes 29968
  1925.3 147.1 %reduce-scatter.18.cloned.1.call-done = f32[72,1152]{1,0:T(8,128)} async-done(((f32[2304,1152]{1,0:T(8,128)}), f32[72,1152]{1,0:T(8,128)}) %reduce-scatter.18.cloned.1.call-update) | async-done | bytes 331792
  (1945 shorter events, 600.6 us)
Async XLA Ops:
  7.2 549.3 %copy-start = (bf16[4,1152]{1,0:T(4,128)(2,1)S(1)}, bf16[4,1152]{1,0:T(4,128)(2,1)}, u32[]{:S(2)}) copy-start(bf16[4,1152]{1,0:T(4,128)(2,1)} %param.45) | copy-start | bytes 27652
  7.2 277.0 %all-gather.7.cloned.1.call-start = ((), (), s32[]{:S(2)}) async-start(), calls=%async_computation.8 | async-start | bytes 10948608 | tf_op jit(solution)/shard_map/all_gather | solution.py:369
  7.9 530.8 %all-gather.9.cloned.1.call-start = ((), (), s32[]{:S(2)}) async-start(), calls=%async_computation.9 | async-start | bytes 5474304 | tf_op jit(solution)/shard_map/all_gather | solution.py:377
  8.7 560.2 %all-gather.11.cloned.1.call-start = ((), (), s32[]{:S(2)}) async-start(), calls=%async_computation.10 | async-start | bytes 7962624 | tf_op jit(solution)/shard_map/all_gather | solution.py:359
  9.4 139.5 %copy-start.84 = (bf16[1152]{0:T(1024)(128)(2,1)S(1)}, bf16[1152]{0:T(1024)(128)(2,1)}, u32[]{:S(2)}) copy-start(bf16[1152]{0:T(1024)(128)(2,1)} %param.34) | copy-start | bytes 6916
  9.4 139.5 %copy-start.2 = (f32[1,128,1152]{2,1,0:T(8,128)S(1)}, f32[1,128,1152]{2,1,0:T(8,128)}, u32[]{:S(2)}) copy-start(f32[1,128,1152]{2,1,0:T(8,128)} %param.31) | copy-start | bytes 1769476
  9.5 140.2 %copy-start.89 = (bf16[4,72]{1,0:T(4,128)(2,1)S(1)}, bf16[4,72]{1,0:T(4,128)(2,1)}, u32[]{:S(2)}) copy-start(bf16[4,72]{1,0:T(4,128)(2,1)} %param.36) | copy-start | bytes 1732
  9.5 566.0 %all-gather.13.cloned.1.call-start = ((), (), s32[]{:S(2)}) async-start(), calls=%async_computation.11 | async-start | bytes 7962624 | tf_op jit(solution)/shard_map/all_gather | solution.py:360
  10.1 205.0 %copy-start.85 = (bf16[16,72]{1,0:T(8,128)(2,1)S(1)}, bf16[16,72]{1,0:T(8,128)(2,1)}, u32[]{:S(2)}) copy-start(bf16[16,72]{1,0:T(8,128)(2,1)} %param.41) | copy-start | bytes 6916
  78.9 262.4 %copy-start.6 = (bf16[72,2304]{0,1:T(8,128)(2,1)}, bf16[72,2304]{0,1:T(8,128)(2,1)S(1)}, u32[]{:S(2)}) copy-start(bf16[72,2304]{0,1:T(8,128)(2,1)S(1)} %all_gather.38) | copy-start | bytes 995332
  78.9 204.6 %copy-start.76 = (s32[1,128,1]{1,2,0:T(1,128)S(1)}, s32[1,128,1]{1,2,0:T(1,128)}, u32[]{:S(2)}) copy-start(s32[1,128,1]{1,2,0:T(1,128)} %param.33) | copy-start | bytes 1540
  148.9 191.3 %copy-start.30 = (bf16[104,2304]{0,1:T(8,128)(2,1)}, bf16[104,2304]{0,1:T(8,128)(2,1)S(1)}, u32[]{:S(2)}) copy-start(bf16[104,2304]{0,1:T(8,128)(2,1)S(1)} %all_gather.37) | copy-start | bytes 1437700
  148.9 384.0 %copy-start.31 = (f32[1152]{0:T(1024)}, f32[1152]{0:T(1024)S(1)}, u32[]{:S(2)}) copy-start(f32[1152]{0:T(1024)S(1)} %convert_element_type.111) | copy-start | bytes 13828
  149.6 383.3 %copy-start.74 = (f32[128]{0:T(128)}, f32[128]{0:T(128)S(1)}, u32[]{:S(2)}) copy-start(f32[128]{0:T(128)S(1)} %fusion.130) | copy-start | bytes 1540
  215.0 120.7 %copy-start.41 = (f32[2304]{0:T(1024)}, f32[2304]{0:T(1024)S(1)}, u32[]{:S(2)}) copy-start(f32[2304]{0:T(1024)S(1)} %get-tuple-element.878) | copy-start | bytes 27652
  289.3 46.3 %collective-permute-start.2 = (f32[3,2304]{1,0:T(4,128)S(1)}, f32[3,2304]{1,0:T(4,128)S(1)}, u32[]{:S(2)}, u32[]{:S(2)}) collective-permute-start(f32[3,2304]{1,0:T(4,128)S(1)} %slice.1115), channel_id=1, source_target_pairs={{0,1},{1,2},{2,3},{3,4},{4,5},{5,6},{6,7},{8,9},{9,10},{10,11},{11... | collective-permute-start | bytes 82952 | tf_op jit(solution)/shard_map/ppermute | solution.py:15
  335.3 197.6 %copy-start.64 = (f32[2304]{0:T(1024)}, f32[2304]{0:T(1024)S(1)}, u32[]{:S(2)}) copy-start(f32[2304]{0:T(1024)S(1)} %convert_element_type.116) | copy-start | bytes 27652
  335.6 206.9 %copy-start.37 = (f32[1152]{0:T(1024)}, f32[1152]{0:T(1024)S(1)}, u32[]{:S(2)}) copy-start(f32[1152]{0:T(1024)S(1)} %convert_element_type.118) | copy-start | bytes 13828
  397.2 5.9 collective-permute-start
  403.2 6.5 collective-permute-start
  409.7 6.8 collective-permute-start
  416.5 6.8 collective-permute-start
  423.3 6.8 collective-permute-start
  430.1 8.0 collective-permute-start
  438.2 8.4 collective-permute-start
  543.8 19.5 all-to-all-start
  563.3 12.4 all-to-all-start.2
  590.5 12.2 all-to-all-start.1
  602.7 13.0 all-to-all-start.3
  608.8 587.1 %all-reduce.18.cloned.1.call-start = ((), (), s32[]{:S(2)}) async-start(), calls=%async_computation.16 | async-start | bytes 217088 | tf_op jit(solution)/shard_map/psum | solution.py:485
  681.3 7.1 collective-permute-start.1
  688.4 6.2 collective-permute-start.1
  694.7 5.9 collective-permute-start.1
  700.6 6.1 collective-permute-start.1
  706.7 6.8 collective-permute-start.1
  713.5 6.8 collective-permute-start.1
  720.4 7.5 collective-permute-start.1
  731.3 299.6 %copy-start.4 = (f32[128,2304]{1,0:T(8,128)S(1)}, f32[128,2304]{1,0:T(8,128)}, u32[]{:S(2)}) copy-start(f32[128,2304]{1,0:T(8,128)} %copy-done.3) | copy-start | bytes 3538948
  1039.2 11.8 collective-permute-start.3
  1062.0 498.7 %all-reduce.20.cloned.1.call-start = ((), (), s32[]{:S(2)}) async-start(), calls=%async_computation.17 | async-start | bytes 44089344
  1112.0 581.2 %reduce-scatter.12.cloned.1.call-start = ((), (), s32[]{:S(2)}) async-start(), calls=%async_computation.12 | async-start | bytes 7962624 | tf_op jit(solution)/shard_map/reduce_scatter | solution.py:478
  1119.3 706.1 %reduce-scatter.14.cloned.1.call-start = ((), (), s32[]{:S(2)}) async-start(), calls=%async_computation.13 | async-start | bytes 7962624 | tf_op jit(solution)/shard_map/reduce_scatter | solution.py:481
  1126.6 798.7 %reduce-scatter.16.cloned.1.call-start = ((), (), s32[]{:S(2)}) async-start(), calls=%async_computation.14 | async-start | bytes 1216512
  1129.4 943.0 %reduce-scatter.18.cloned.1.call-start = ((), (), s32[]{:S(2)}) async-start(), calls=%async_computation.15 | async-start | bytes 10948608
  1693.2 381.0 %copy-start.1 = (bf16[4,1152]{1,0:T(4,128)(2,1)S(1)}, bf16[4,1152]{1,0:T(4,128)(2,1)}, u32[]{:S(2)}) copy-start(bf16[4,1152]{1,0:T(4,128)(2,1)} %param.45) | copy-start | bytes 27652
  1695.8 376.6 %copy-start.80 = (f32[1152]{0:T(1024)S(1)}, f32[1152]{0:T(1024)}, u32[]{:S(2)}) copy-start(f32[1152]{0:T(1024)} %get-tuple-element.2007) | copy-start | bytes 13828
  1695.8 377.2 %copy-start.79 = (f32[1152]{0:T(1024)S(1)}, f32[1152]{0:T(1024)}, u32[]{:S(2)}) copy-start(f32[1152]{0:T(1024)} %get-tuple-element.2017) | copy-start | bytes 13828
  1695.8 377.8 %copy-start.69 = (f32[4,1152]{1,0:T(4,128)S(1)}, f32[4,1152]{1,0:T(4,128)}, u32[]{:S(2)}) copy-start(f32[4,1152]{1,0:T(4,128)} %get-tuple-element.2018) | copy-start | bytes 55300
  (308 other events, 1965.0 us)
Sparse Core Ops, SparseCore 0:
  11.0 93.8 all-gather.6
  107.7 65.9 all-gather.8
  175.9 108.7 all-gather.10
  286.7 108.3 all-gather.12
  1062.2 133.6 all-reduce.17
  1203.9 356.8 all-reduce.19
  1564.4 128.7 reduce-scatter.11
  1697.4 128.0 reduce-scatter.13
  1831.1 94.0 reduce-scatter.15
  1931.8 140.6 reduce-scatter.17
where the time goes:
time: 2110 us; the launch traced here: 2080 us
  waiting for transfers between devices  988 us (47%)
  local copies, waits for them, and re-layouts  350 us (17%)
  blocking collectives  316 us (15%)
  other arithmetic  237 us (11%)
  matrix products  90.5 us (4%)
  starting transfers between devices  76.8 us (4%)
    unnamed x13, waiting for transfers between devices  607 us
    reduce_scatter x1, waiting for transfers between devices, body(): lax.psum_scatter(grad_down_w.astype(jnp.bfloat16), 'seq', scatter_dimensi...  130 us
    reduce_scatter x1, waiting for transfers between devices, body(): lax.psum_scatter(grad_up_w.astype(jnp.bfloat16), 'seq', scatter_dimension...  128 us
    all_gather x1, blocking collectives, body(): lax.all_gather(shards[3], ('dp', 'seq'), axis=1, tiled=True)  70.1 us
    slice x32, local copies, waits for them, and re-layouts, forward_turn(): block_act[index]  69 us
    all_gather x1, blocking collectives, body(): lax.all_gather(shards[4], ('dp', 'seq'), axis=1, tiled=True)  68.7 us
    all_gather x1, blocking collectives, body(): lax.all_gather(shards[6], ('dp', 'seq'), axis=1, tiled=True)  68.3 us
    all_gather x1, blocking collectives, body(): lax.all_gather(shards[1], ('dp', 'seq'), axis=1, tiled=True)  65.1 us
  transfers between devices with their start and end apart: 30, of which 24 were waited for; matrix products, arithmetic and copies ran while one was open for 13% of the time, Pallas kernels for 0%

commit v1 on v0

--- a/solution.py
+++ b/solution.py
@@ -1,6 +1,7 @@
 import jax
 import jax.numpy as jnp
 from jax import lax
+from jax.experimental import pallas as pl
 from jax.sharding import PartitionSpec as P
 
 CAP = 56
@@ -13,6 +14,16 @@
     size = lax.axis_size(axis)
     pairs = [(i, i + by) for i in range(size) if 0 <= i + by < size]
     return lax.ppermute(value, axis, pairs)
+
+
+def copy_kernel(from_ref, to_ref):
+    to_ref[...] = from_ref[...]
+
+
+def copied(values):
+    return pl.pallas_call(
+        copy_kernel, out_shape=jax.ShapeDtypeStruct(values.shape, values.dtype)
+    )(values)
 
 
 def rms_norm(values, gain):
@@ -362,7 +373,7 @@
     experts = router.shape[0]
     copies = lax.axis_size("dp") // experts
     capacity = CAP
-    x_in = tokens.reshape(rows, width)
+    x_in = copied(tokens.reshape(rows, width))
     gain_one = mixer_gain.astype(jnp.float32)
     normed = rms_norm(x_in, gain_one).astype(jnp.bfloat16)
     gathered = (

time: 2110 us -> 2050 us (0.972)
  local copies, waits for them, and re-layouts: 350 us -> 295 us
    dynamic_slice x80, local copies, waits for them, and re-layouts: 54.8 us -> 0.69 us  [forward_chain(): lax.scan(forward_turn, start, (split_by(delta, block), split_by(state_in,...]
  transfers between devices with their start and end apart: 30 -> 30, of which waited for: 24 -> 24; matrix products, arithmetic and copies ran while one was open for 13% -> 12% of each run, Pallas kernels for 0% -> 0%
where the time goes in v1:
time: 2050 us; the launch traced here: 2030 us
  waiting for transfers between devices  989 us (48%)
  blocking collectives  315 us (15%)
  local copies, waits for them, and re-layouts  295 us (14%)
  other arithmetic  238 us (12%)
  matrix products  91 us (4%)
  starting transfers between devices  76.2 us (4%)
    unnamed x13, waiting for transfers between devices  607 us
    reduce_scatter x1, waiting for transfers between devices, body(): lax.psum_scatter(grad_down_w.astype(jnp.bfloat16), 'seq', scatter_dimensi...  130 us
    reduce_scatter x1, waiting for transfers between devices, body(): lax.psum_scatter(grad_up_w.astype(jnp.bfloat16), 'seq', scatter_dimension...  128 us
    all_gather x1, blocking collectives, body(): lax.all_gather(shards[3], ('dp', 'seq'), axis=1, tiled=True)  69.7 us
    all_gather x1, blocking collectives, body(): lax.all_gather(shards[4], ('dp', 'seq'), axis=1, tiled=True)  69.2 us
    slice x32, local copies, waits for them, and re-layouts, forward_turn(): block_act[index]  69.1 us
    all_gather x1, blocking collectives, body(): lax.all_gather(shards[6], ('dp', 'seq'), axis=1, tiled=True)  68.1 us
    all_gather x1, blocking collectives, body(): lax.all_gather(shards[1], ('dp', 'seq'), axis=1, tiled=True)  65.3 us
  transfers between devices with their start and end apart: 30, of which 24 were waited for; matrix products, arithmetic and copies ran while one was open for 12% of the time, Pallas kernels for 0%

profile of v1, /device:TPU:31, one launch (start us, length us, event | category | flops | bytes accessed | tf_op | source)
XLA Modules:
  0.0 2031.1 jit_solution(17083831369040411693)
XLA Ops:
  12.1 69.2 %all_gather.38 = bf16[72,2304]{0,1:T(8,128)(2,1)S(1)} all-gather(bf16[72,72]{0,1:T(8,128)(2,1)S(1)} %copy.69), channel_id=1, replica_groups=mesh['dp'=4,'seq'=8] {'dp','seq'}, dimensions={1}, use_global_device_ids=true | all-gather | bytes 342144 | tf_op jit(solution)/shard_map/all_gather | solution.py:384
  81.3 69.7 %all_gather.37 = bf16[104,2304]{0,1:T(8,128)(2,1)S(1)} all-gather(bf16[104,72]{0,1:T(8,128)(2,1)S(1)} %copy-done.64), channel_id=1, replica_groups=mesh['dp'=4,'seq'=8] {'dp','seq'}, dimensions={1}, use_global_device_ids=true | all-gather | bytes 494208 | tf_op jit(solution)/shard_map/all_gather | solution.py:383
  151.2 65.3 %all-gather.1 = bf16[32,72,4]{1,2,0:T(4,128)(2,1)S(1)} all-gather(bf16[1,72,4]{1,2,0:T(4,128)(2,1)S(1)} %bitcast.422), channel_id=1, replica_groups=mesh['dp'=4,'seq'=8] {'dp','seq'}, dimensions={0}, use_global_device_ids=true | all-gather | bytes 19008 | tf_op jit(solution)/shard_map/all_gather | solution.py:381
  216.7 68.1 %all-gather = bf16[32,72,16]{1,2,0:T(8,128)(2,1)S(1)} all-gather(bf16[1,72,16]{1,2,0:T(8,128)(2,1)S(1)} %bitcast.421), channel_id=1, replica_groups=mesh['dp'=4,'seq'=8] {'dp','seq'}, dimensions={0}, use_global_device_ids=true | all-gather | bytes 76032 | tf_op jit(solution)/shard_map/all_gather | solution.py:386
  285.8 4.2 fusion.65
  293.7 42.8 %all-reduce.14 = (bf16[2304]{0:T(1024)(128)(2,1)S(1)}, bf16[2304]{0:T(1024)(128)(2,1)S(1)}, bf16[2304]{0:T(1024)(128)(2,1)S(1)}) all-reduce(bf16[2304]{0:T(1024)(128)(2,1)S(1)} %dynamic-update-slice.2, bf16[2304]{0:T(1024)(128)(2,1)S(1)} %dynamic-update-slice.1, ...), channel_id=1, replica_groups=mesh['dp'=4,'seq'=8] {'dp','seq'}, use_global_device_ids=true, to_apply=%add.2 | all-reduce | flops 6912 | bytes 27648
  336.9 4.5 fusion.133
  344.9 41.7 %while.88 = (s32[]{:T(128)}, f32[16,2304]{1,0:T(8,128)S(1)}, f32[16,8,2304]{2,1,0:T(8,128)}, f32[16,2304]{1,0:T(8,128)S(1)}, f32[16,8,16]{2,1,0:T(8,128)S(1)}, /...) while((s32[]{:T(128)}, f32[16,2304]{1,0:T(8,128)S(1)}, ...), condition=%wide.region_3.4_spmd.clone, body=%wide.region_2.3_spmd.clone.sunk | while | flops 1234954 | bytes 1108759 | solution.py:82
  386.7 51.4 %while.85 = (s32[]{:T(128)}, f32[16,2304]{1,0:T(8,128)S(1)}, f32[16,2304]{1,0:T(8,128)S(1)}, f32[16,2304]{1,0:T(8,128)S(1)}, s32[]{:T(128)}) while((s32[]{:T(128)}, f32[16,2304]{1,0:T(8,128)S(1)}, f32[16,2304]{1,0:T(8,128)S(1)}, f32[16,2304]{1,0:T(8,128)S(1)}, s32[]{:T(128)}) %tuple.410), condition=%wide.region_5.6_spmd, body=%wide.region_4.5_spmd.sunk | while | flops 73730 | bytes 1179749 | solution.py:175
  388.1 5.0 collective-permute-done
  394.4 9.7 collective-permute-done
  405.4 5.2 collective-permute-done
  411.9 5.5 collective-permute-done
  418.7 5.5 collective-permute-done
  425.6 5.5 collective-permute-done
  432.4 5.7 collective-permute-done
  439.3 74.4 %while.86 = (s32[]{:T(128)}, f32[16,2304]{1,0:T(8,128)S(1)}, f32[16,8,2304]{2,1,0:T(8,128)}, f32[16,16,2304]{2,1,0:T(8,128)}, f32[16,8,2304]{2,1,0:T(8,128)}, /*...) while((s32[]{:T(128)}, f32[16,2304]{1,0:T(8,128)S(1)}, ...), condition=%wide.region_15.16_spmd, body=%wide.region_6.15_spmd.sunk | while | flops 2654217 | bytes 2770605 | solution.py:82
  513.7 5.8 multiply_convert_fusion.1
  524.6 11.5 all-to-all-start
  538.1 4.8 all-to-all-done
  542.9 6.2 all-to-all-start.2
  549.2 6.5 fusion.140
  556.0 11.1 add_convert_fusion
  570.8 5.4 all-to-all-start.1
  576.2 6.6 convolution_convert_fusion.2
  583.0 6.0 all-to-all-start.3
  603.5 4.2 fusion.110
  610.6 40.6 %while.89 = (s32[]{:T(128)}, f32[16,2304]{1,0:T(8,128)S(1)}, f32[16,8,2304]{2,1,0:T(8,128)}, f32[16,2304]{1,0:T(8,128)S(1)}, f32[16,8,16]{2,1,0:T(8,128)S(1)}, /...) while((s32[]{:T(128)}, f32[16,2304]{1,0:T(8,128)S(1)}, ...), condition=%wide.region_24.26_spmd.clone, body=%wide.region_23.25_spmd.clone.sunk | while | flops 1216523 | bytes 887595 | solution.py:209
  651.2 46.6 %while.87 = (s32[]{:T(128)}, f32[16,2304]{1,0:T(8,128)S(1)}, f32[16,2304]{1,0:T(8,128)S(1)}, f32[16,2304]{1,0:T(8,128)S(1)}, s32[]{:T(128)}) while((s32[]{:T(128)}, f32[16,2304]{1,0:T(8,128)S(1)}, f32[16,2304]{1,0:T(8,128)S(1)}, f32[16,2304]{1,0:T(8,128)S(1)}, s32[]{:T(128)}) %tuple.452), condition=%wide.region_26.28_spmd, body=%wide.region_25.27_spmd.sunk | while | flops 73730 | bytes 1179749 | solution.py:175
  651.2 4.6 collective-permute-start.1
  676.7 4.7 collective-permute-start.1
  683.5 4.7 collective-permute-start.1
  690.3 4.7 collective-permute-start.1
  701.2 278.7 %while.90 = (s32[]{:T(128)}, f32[16,2304]{1,0:T(8,128)S(1)}, f32[16,2304]{1,0:T(8,128)S(1)}, f32[16,8,2304]{2,1,0:T(8,128)}, f32[16,8,2304]{2,1,0:T(8,128)}, /*i...) while((s32[]{:T(128)}, f32[16,2304]{1,0:T(8,128)S(1)}, ...), condition=%wide.region_60.62_spmd.clone, body=%wide.region_27.61_spmd.clone.sunk | while | flops 8441611 | bytes 6761103 | solution.py:146
  988.2 5.2 collective-permute-start.3
  994.1 5.9 convolution_bitcast_fusion
  1002.1 5.6 convolution_bitcast_fusion.1
  1011.8 15.8 pad_maximum_fusion
  1027.6 34.1 %copy.74 = f32[2,1152,2304]{1,0,2:T(2,128)} copy(f32[2,1152,2304]{2,1,0:T(8,128)} %pad_maximum_fusion) | data formatting | bytes 42467328 | tf_op jit(solution)/shard_map/stack | solution.py:471
  1062.7 6.3 convolution_convert_fusion.1
  1070.4 5.9 convolution_convert_fusion
  1080.2 5.6 fusion.108
  1087.8 57.9 %all-reduce.18.cloned.1.call-done = (f32[1152]{0:T(1024)}, f32[4,2304]{1,0:T(4,128)}, f32[2304]{0:T(1024)}, f32[2304]{0:T(1024)}, f32[2304]{0:T(1024)}, /*index=5*/f32[1152]{0:T(1024)}, f32[4,1152]{1,0:T(4,128)}) async-done(((f32[1152]{0:T(1024)}, f32[4,2304]{1,0:T(4,128)}, f32[2304]{0:T(1024)}, f32[2304]{0:T(1024)}, f32[2304]{0:T(1024)}, /*index=5*/f32[1152]{0:T(1024)}, f32[4,1152]{1,0:T(4,128)}), ...) | async-done | bytes 92176 | tf_op jit(solution)/shard_map/psum | solution.py:496
  1150.8 359.8 %all-reduce.20.cloned.1.call-done = (f32[2,1152,2304]{1,0,2:T(2,128)}, f32[72,2304]{1,0:T(8,128)}, f32[16,2304]{1,0:T(8,128)}) async-done(((f32[2,1152,2304]{1,0,2:T(2,128)}, f32[72,2304]{1,0:T(8,128)}, f32[16,2304]{1,0:T(8,128)}), (f32[2,1152,2304]{1,0,2:T(2,128)}, f32[72,2304]{1,0:T(8,128)}, f32[16,2304]{1,0:T(8,128)})) %all-reduce.20.cloned.1.call-update) | async-done | bytes 22044688
  1515.4 127.6 %reduce-scatter.12.cloned.1.call-done = bf16[144,3072]{1,0:T(8,128)(2,1)} async-done(((bf16[1152,3072]{1,0:T(8,128)(2,1)}), bf16[144,3072]{1,0:T(8,128)(2,1)}) %reduce-scatter.12.cloned.1.call-update) | async-done | bytes 884752 | tf_op jit(solution)/shard_map/reduce_scatter | solution.py:489
  1645.6 129.6 %reduce-scatter.14.cloned.1.call-done = bf16[3072,144]{0,1:T(8,128)(2,1)} async-done(((bf16[3072,1152]{0,1:T(8,128)(2,1)}), bf16[3072,144]{0,1:T(8,128)(2,1)}) %reduce-scatter.14.cloned.1.call-update) | async-done | bytes 884752 | tf_op jit(solution)/shard_map/reduce_scatter | solution.py:492
  1777.8 97.2 %reduce-scatter.16.cloned.1.call-done = f32[104,72]{0,1:T(8,128)} async-done(((f32[104,2304]{0,1:T(8,128)}), f32[104,72]{0,1:T(8,128)}) %reduce-scatter.16.cloned.1.call-update) | async-done | bytes 29968
  1875.0 147.1 %reduce-scatter.18.cloned.1.call-done = f32[72,1152]{1,0:T(8,128)} async-done(((f32[2304,1152]{1,0:T(8,128)}), f32[72,1152]{1,0:T(8,128)}) %reduce-scatter.18.cloned.1.call-update) | async-done | bytes 331792
  (1909 shorter events, 549.7 us)
Async XLA Ops:
  7.2 528.9 %copy-start = (bf16[4,1152]{1,0:T(4,128)(2,1)S(1)}, bf16[4,1152]{1,0:T(4,128)(2,1)}, u32[]{:S(2)}) copy-start(bf16[4,1152]{1,0:T(4,128)(2,1)} %param.45) | copy-start | bytes 27652
  7.2 278.6 %all-gather.7.cloned.1.call-start = ((), (), s32[]{:S(2)}) async-start(), calls=%async_computation.8 | async-start | bytes 10948608 | tf_op jit(solution)/shard_map/all_gather | solution.py:380
  7.9 511.5 %all-gather.9.cloned.1.call-start = ((), (), s32[]{:S(2)}) async-start(), calls=%async_computation.9 | async-start | bytes 5474304 | tf_op jit(solution)/shard_map/all_gather | solution.py:388
  8.7 540.5 %all-gather.11.cloned.1.call-start = ((), (), s32[]{:S(2)}) async-start(), calls=%async_computation.10 | async-start | bytes 7962624 | tf_op jit(solution)/shard_map/all_gather | solution.py:370
  9.4 546.3 %all-gather.13.cloned.1.call-start = ((), (), s32[]{:S(2)}) async-start(), calls=%async_computation.11 | async-start | bytes 7962624 | tf_op jit(solution)/shard_map/all_gather | solution.py:371
  10.0 141.0 %copy-start.80 = (bf16[1152]{0:T(1024)(128)(2,1)S(1)}, bf16[1152]{0:T(1024)(128)(2,1)}, u32[]{:S(2)}) copy-start(bf16[1152]{0:T(1024)(128)(2,1)} %param.34) | copy-start | bytes 6916
  11.9 139.1 %copy-start.2 = (f32[128,1152]{1,0:T(8,128)S(1)}, f32[128,1152]{1,0:T(8,128)}, u32[]{:S(2)}) copy-start(f32[128,1152]{1,0:T(8,128)} %shard_map.288) | copy-start | bytes 1769476
  11.9 139.2 %copy-start.85 = (bf16[4,72]{1,0:T(4,128)(2,1)S(1)}, bf16[4,72]{1,0:T(4,128)(2,1)}, u32[]{:S(2)}) copy-start(bf16[4,72]{1,0:T(4,128)(2,1)} %param.36) | copy-start | bytes 1732
  12.0 204.8 %copy-start.81 = (bf16[16,72]{1,0:T(8,128)(2,1)S(1)}, bf16[16,72]{1,0:T(8,128)(2,1)}, u32[]{:S(2)}) copy-start(bf16[16,72]{1,0:T(8,128)(2,1)} %param.41) | copy-start | bytes 6916
  81.3 261.1 %copy-start.7 = (bf16[72,2304]{0,1:T(8,128)(2,1)}, bf16[72,2304]{0,1:T(8,128)(2,1)S(1)}, u32[]{:S(2)}) copy-start(bf16[72,2304]{0,1:T(8,128)(2,1)S(1)} %all_gather.38) | copy-start | bytes 995332
  81.3 203.6 %copy-start.70 = (s32[1,128,1]{1,2,0:T(1,128)S(1)}, s32[1,128,1]{1,2,0:T(1,128)}, u32[]{:S(2)}) copy-start(s32[1,128,1]{1,2,0:T(1,128)} %param.33) | copy-start | bytes 1540
  151.0 190.4 %copy-start.31 = (bf16[104,2304]{0,1:T(8,128)(2,1)}, bf16[104,2304]{0,1:T(8,128)(2,1)S(1)}, u32[]{:S(2)}) copy-start(bf16[104,2304]{0,1:T(8,128)(2,1)S(1)} %all_gather.37) | copy-start | bytes 1437700
  151.0 134.7 %copy-start.45 = (f32[1152]{0:T(1024)}, f32[1152]{0:T(1024)S(1)}, u32[]{:S(2)}) copy-start(f32[1152]{0:T(1024)S(1)} %convert_element_type.105) | copy-start | bytes 13828
  151.2 133.7 %copy-start.88 = (f32[128]{0:T(128)}, f32[128]{0:T(128)S(1)}, u32[]{:S(2)}) copy-start(f32[128]{0:T(128)S(1)} %multiply_reduce_fusion.50) | copy-start | bytes 1540
  151.2 138.8 %copy-start.83 = (f32[128]{0:T(128)}, f32[128]{0:T(128)S(1)}, u32[]{:S(2)}) copy-start(f32[128]{0:T(128)S(1)} %fusion.127) | copy-start | bytes 1540
  285.7 227.9 %copy-start.20 = (bf16[128,1152]{1,0:T(8,128)(2,1)}, bf16[128,1152]{1,0:T(8,128)(2,1)S(1)}, u32[]{:S(2)}) copy-start(bf16[128,1152]{1,0:T(8,128)(2,1)S(1)} %multiply_convert_fusion.3) | copy-start | bytes 884740
  291.0 45.8 %collective-permute-start.2 = (f32[3,2304]{1,0:T(4,128)S(1)}, f32[3,2304]{1,0:T(4,128)S(1)}, u32[]{:S(2)}, u32[]{:S(2)}) collective-permute-start(f32[3,2304]{1,0:T(4,128)S(1)} %slice.1115), channel_id=1, source_target_pairs={{0,1},{1,2},{2,3},{3,4},{4,5},{5,6},{6,7},{8,9},{9,10},{10,11},{11... | collective-permute-start | bytes 82952 | tf_op jit(solution)/shard_map/ppermute | solution.py:16
  336.5 177.1 %copy-start.61 = (f32[2304]{0:T(1024)}, f32[2304]{0:T(1024)S(1)}, u32[]{:S(2)}) copy-start(f32[2304]{0:T(1024)S(1)} %convert_element_type.109) | copy-start | bytes 27652
  386.8 6.3 collective-permute-start
  393.1 11.0 collective-permute-start
  404.1 6.5 collective-permute-start
  410.6 6.8 collective-permute-start
  417.4 6.8 collective-permute-start
  424.3 6.8 collective-permute-start
  431.1 7.0 collective-permute-start
  524.6 18.3 all-to-all-start
  542.9 13.1 all-to-all-start.2
  570.8 12.2 all-to-all-start.1
  583.0 13.0 all-to-all-start.3
  589.0 556.6 %all-reduce.18.cloned.1.call-start = ((), (), s32[]{:S(2)}) async-start(), calls=%async_computation.16 | async-start | bytes 217088 | tf_op jit(solution)/shard_map/psum | solution.py:496
  651.2 7.1 collective-permute-start.1
  658.4 6.2 collective-permute-start.1
  664.6 5.9 collective-permute-start.1
  670.5 6.1 collective-permute-start.1
  676.7 6.8 collective-permute-start.1
  683.5 6.8 collective-permute-start.1
  690.3 7.4 collective-permute-start.1
  701.2 278.7 %copy-start.4 = (f32[128,2304]{1,0:T(8,128)S(1)}, f32[128,2304]{1,0:T(8,128)}, u32[]{:S(2)}) copy-start(f32[128,2304]{1,0:T(8,128)} %copy-done.3) | copy-start | bytes 3538948
  988.2 11.8 collective-permute-start.3
  1011.8 498.8 %all-reduce.20.cloned.1.call-start = ((), (), s32[]{:S(2)}) async-start(), calls=%async_computation.17 | async-start | bytes 44089344
  1061.7 581.3 %reduce-scatter.12.cloned.1.call-start = ((), (), s32[]{:S(2)}) async-start(), calls=%async_computation.12 | async-start | bytes 7962624 | tf_op jit(solution)/shard_map/reduce_scatter | solution.py:489
  1069.1 706.2 %reduce-scatter.14.cloned.1.call-start = ((), (), s32[]{:S(2)}) async-start(), calls=%async_computation.13 | async-start | bytes 7962624 | tf_op jit(solution)/shard_map/reduce_scatter | solution.py:492
  1076.3 798.7 %reduce-scatter.16.cloned.1.call-start = ((), (), s32[]{:S(2)}) async-start(), calls=%async_computation.14 | async-start | bytes 1216512
  1079.1 943.1 %reduce-scatter.18.cloned.1.call-start = ((), (), s32[]{:S(2)}) async-start(), calls=%async_computation.15 | async-start | bytes 10948608
  1643.0 381.0 %copy-start.1 = (bf16[4,1152]{1,0:T(4,128)(2,1)S(1)}, bf16[4,1152]{1,0:T(4,128)(2,1)}, u32[]{:S(2)}) copy-start(bf16[4,1152]{1,0:T(4,128)(2,1)} %param.45) | copy-start | bytes 27652
  1645.6 376.6 %copy-start.74 = (f32[1152]{0:T(1024)S(1)}, f32[1152]{0:T(1024)}, u32[]{:S(2)}) copy-start(f32[1152]{0:T(1024)} %get-tuple-element.2007) | copy-start | bytes 13828
  1645.6 377.2 %copy-start.73 = (f32[1152]{0:T(1024)S(1)}, f32[1152]{0:T(1024)}, u32[]{:S(2)}) copy-start(f32[1152]{0:T(1024)} %get-tuple-element.2017) | copy-start | bytes 13828
  1645.6 377.8 %copy-start.66 = (f32[4,1152]{1,0:T(4,128)S(1)}, f32[4,1152]{1,0:T(4,128)}, u32[]{:S(2)}) copy-start(f32[4,1152]{1,0:T(4,128)} %get-tuple-element.2018) | copy-start | bytes 55300
  (289 other events, 1878.7 us)
Sparse Core Ops, SparseCore 0:
  10.9 93.1 all-gather.6
  107.0 67.1 all-gather.8
  176.4 108.7 all-gather.10
  287.2 109.5 all-gather.12
  1011.9 133.7 all-reduce.17
  1153.7 356.8 all-reduce.19
  1514.2 128.7 reduce-scatter.11
  1647.1 128.0 reduce-scatter.13
  1780.9 94.0 reduce-scatter.15
  1881.5 140.6 reduce-scatter.17

commit v2 on v0

v2 whole, which is shorter than its diff:
```python
import functools
import math

import jax
import jax.numpy as jnp
from jax import lax
from jax.experimental import pallas as pl
from jax.experimental.pallas import tpu as pltpu
from jax.sharding import PartitionSpec as P

CAP = 56
LANES = 128
TIME_BLOCK = 128
LOG2E = math.log2(math.e)

HIGHEST = lax.Precision.HIGHEST


def rms_norm(values, gain):
    return values * lax.rsqrt(jnp.mean(values * values, axis=-1, keepdims=True) + 1e-05) * gain


def gelu_exact(values):
    return jax.nn.gelu(values, approximate=False)


def inner_rows(left, right, precision=None):
    return lax.dot_general(
        left,
        right,
        (((0,), (0,)), ((), ())),
        precision=precision,
        preferred_element_type=jnp.float32,
    )


def outer_cols(left, right, precision=None):
    return lax.dot_general(
        left,
        right,
        (((1,), (1,)), ((), ())),
        precision=precision,
        preferred_element_type=jnp.float32,
    )


def sublane_sums(parts):
    row = lax.broadcasted_iota(jnp.int32, parts[0].shape, 0)
    low4 = row < 4
    low2 = (row % 4) < 2
    low1 = (row % 2) < 1
    quads = []
    for k in range(4):
        a, b = parts[k], parts[k + 4]
        quads.append(jnp.where(low4, a, b) + pltpu.roll(jnp.where(low4, b, a), 4, 0))
    pairs = []
    for k in range(2):
        a, b = quads[k], quads[k + 2]
        pairs.append(
            jnp.where(low2, a, b) + jnp.where(low2, pltpu.roll(a, 6, 0), pltpu.roll(b, 2, 0))
        )
    a, b = pairs
    return jnp.where(low1, a, b) + jnp.where(low1, pltpu.roll(a, 7, 0), pltpu.roll(b, 1, 0))


def lane_column(block, k):
    return jnp.broadcast_to(block[:, k : k + 1], block.shape)


MESH = pl.DeviceIdType.MESH
VMEM_LIMIT = 56 * 1024 * 1024


def dot_nn(left, right, precision=None):
    return lax.dot_general(
        left, right, (((1,), (0,)), ((), ())), precision=precision,
        preferred_element_type=jnp.float32,
    )


def place():
    own, line = lax.axis_index("seq"), lax.axis_index("dp")
    return line, own, own // 2, lax.rem(own, 2)


def remote(source, target, send_sem, recv_sem, line, position):
    return pltpu.make_async_remote_copy(
        src_ref=source,
        dst_ref=target,
        send_sem=send_sem,
        recv_sem=recv_sem,
        device_id=(line, position),
        device_id_type=MESH,
    )


def greet(count, lines=1):
    line, own, _, _ = place()
    barrier = pltpu.get_barrier_semaphore()
    for k in range(1, count):
        pl.semaphore_signal(
            barrier, inc=1, device_id=(line, lax.rem(own + k, count)), device_id_type=MESH
        )
    for k in range(1, lines):
        pl.semaphore_signal(
            barrier, inc=1, device_id=(lax.rem(line + k, lines), own), device_id_type=MESH
        )
    pl.semaphore_wait(barrier, count - 1 + lines - 1)


def sigmoid(values):
    return 1.0 / (1.0 + jnp.exp(-values))


def softplus(values):
    return jnp.maximum(values, 0.0) + jnp.log1p(jnp.exp(-jnp.abs(values)))


class Cuts:
    def __init__(self, picks, rank, state, kernel):
        self.picks, self.rank, self.state, self.kernel = picks, rank, state, kernel
        self.step = picks
        self.decay = self.step + rank
        self.taps = self.decay + state
        self.conv_bias = self.taps + kernel
        self.step_bias = self.conv_bias + 1
        self.skip = self.step_bias + 1
        self.rows = self.skip + 1


def front_kernel(
    count, lines, cuts,
    normed_ref, packed_ref,
    all_ref, weights_ref, small_ref, ext_ref, sum_ref, act_ref, gate_ref, selected_ref,
    part_ref, partial_ref,
    send_w, recv_w, send_hi, recv_hi, send_x, recv_x, send_rs, recv_rs, send_ag, recv_ag,
):
    line, own, high, low = place()
    half = count // 2
    rows, width = normed_ref.shape
    shard = packed_ref.shape[0]
    inner = weights_ref.shape[0]
    kernel = cuts.kernel
    partner = 2 * high + 1 - low
    greet(count, lines)

    copies = []
    shard_rows = pl.ds(pl.multiple_of(line * shard, 16), shard)
    for k in range(1, half):
        copy = remote(
            normed_ref, all_ref.at[own], send_hi.at[k], recv_hi.at[k],
            line, 2 * lax.rem(high + k, half) + low,
        )
        copy.start()
        copies.append(copy)
    copy = remote(normed_ref, all_ref.at[own], send_x.at[0], recv_x.at[0], line, partner)
    copy.start()
    copies.append(copy)
    for k in range(1, lines):
        copy = remote(
            packed_ref, weights_ref.at[shard_rows], send_w.at[k], recv_w.at[k],
            lax.rem(line + k, lines), own,
        )
        copy.start()
        copies.append(copy)
    all_ref[own] = normed_ref[...]
    weights_ref[shard_rows, :] = packed_ref[...]
    if lines * shard < inner:
        weights_ref[lines * shard :, :] = jnp.zeros(
            (inner - lines * shard, weights_ref.shape[1]), weights_ref.dtype
        )
    ext_ref[0:8, :] = jnp.zeros((8, inner), jnp.float32)
    for k in range(1, half):
        block = 2 * lax.rem(high - k + half, half) + low
        remote(
            normed_ref, all_ref.at[block], send_hi.at[k], recv_hi.at[k], line, partner
        ).wait_recv()
        copy = remote(
            all_ref.at[block], all_ref.at[block], send_x.at[k], recv_x.at[k], line, partner
        )
        copy.start()
        copies.append(copy)
    for k in range(1, lines):
        from_line = lax.rem(line - k + lines, lines)
        there = pl.ds(pl.multiple_of(from_line * shard, 16), shard)
        remote(
            packed_ref, weights_ref.at[there], send_w.at[k], recv_w.at[k], from_line, own
        ).wait_recv()
    small_ref[...] = weights_ref[:, 3 * width :].astype(jnp.float32).T
    for k in range(half):
        block = 2 * lax.rem(high - k + half, half) + 1 - low
        remote(
            normed_ref, all_ref.at[block], send_x.at[k], recv_x.at[k], line, partner
        ).wait_recv()

    def project(b, carry):
        start = pl.multiple_of(b * rows, rows)
        block = all_ref[b]
        ext_ref[pl.ds(pl.multiple_of(start + 8, 8), rows), :] = outer_cols(
            block, weights_ref[:, :width]
        )
        gate_ref[pl.ds(start, rows), :] = outer_cols(block, weights_ref[:, width : 2 * width])
        return carry

    lax.fori_loop(0, count, project, 0)

    def convolve(b, carry):
        start = pl.multiple_of(b * rows, rows)
        window = ext_ref[pl.ds(start, rows + 8), :]
        total = small_ref[cuts.conv_bias : cuts.conv_bias + 1, :]
        for k in range(kernel):
            tap = small_ref[cuts.taps + k : cuts.taps + k + 1, :]
            total = total + tap * window[9 - kernel + k : 9 - kernel + k + rows]
        act = total * sigmoid(total)
        sum_ref[pl.ds(start, rows), :] = total
        act_ref[pl.ds(start, rows), :] = act
        part_ref[b] = outer_cols(
            small_ref[: cuts.picks, :].astype(jnp.bfloat16), act.astype(jnp.bfloat16)
        )
        return carry

    lax.fori_loop(0, count, convolve, 0)

    for k in range(1, count):
        there = lax.rem(own + k, count)
        copy = remote(
            part_ref.at[there], partial_ref.at[k], send_rs.at[k], recv_rs.at[k], line, there
        )
        copy.start()
        copies.append(copy)
    total = part_ref[own]
    for k in range(1, count):
        remote(
            part_ref.at[own], partial_ref.at[k], send_rs.at[k], recv_rs.at[k], line, partner
        ).wait_recv()
        total = total + partial_ref[k]
    selected_ref[own] = total
    for k in range(1, count):
        copy = remote(
            selected_ref.at[own], selected_ref.at[own], send_ag.at[k], recv_ag.at[k],
            line, lax.rem(own + k, count),
        )
        copy.start()
        copies.append(copy)
    for k in range(1, count):
        block = lax.rem(own - k + count, count)
        remote(
            selected_ref.at[block], selected_ref.at[block], send_ag.at[k], recv_ag.at[k],
            line, partner,
        ).wait_recv()
    for copy in copies:
        copy.wait_send()


def front(count, lines, cuts, normed, packed):
    rows, width = normed.shape
    shard, columns = packed.shape
    inner = -(-lines * shard // LANES) * LANES
    length = count * rows
    half = count // 2
    small = columns - 3 * width
    vmem = pl.BlockSpec(memory_space=pltpu.VMEM)

    def f32(*shape):
        return jax.ShapeDtypeStruct(shape, jnp.float32)

    dma = pltpu.SemaphoreType.DMA
    return pl.pallas_call(
        functools.partial(front_kernel, count, lines, cuts),
        in_specs=[vmem] * 2,
        out_specs=[vmem] * 8,
        out_shape=[
            jax.ShapeDtypeStruct((count, rows, width), jnp.bfloat16),
            jax.ShapeDtypeStruct((inner, columns), jnp.bfloat16),
            f32(small, inner),
            f32(length + 8, inner),
            f32(length, inner),
            f32(length, inner),
            f32(length, inner),
            f32(count, cuts.picks, rows),
        ],
        scratch_shapes=[
            pltpu.VMEM((count, cuts.picks, rows), jnp.float32),
            pltpu.VMEM((count, cuts.picks, rows), jnp.float32),
            dma((lines,)), dma((lines,)), dma((half,)), dma((half,)), dma((half,)), dma((half,)),
            dma((count,)), dma((count,)), dma((count,)), dma((count,)),
        ],
        compiler_params=pltpu.CompilerParams(
            collective_id=0, has_side_effects=True, vmem_limit_bytes=VMEM_LIMIT
        ),
        cost_estimate=pl.CostEstimate(
            flops=4 * length * width * inner,
            bytes_accessed=20 * length * inner,
            transcendentals=length * inner,
        ),
        name="front",
    )(normed, packed)


class Relay:
    def __init__(self, count, part, across, along, send_x, recv_x, send_hi, recv_hi):
        self.line, self.own, self.high, self.low = place()
        self.half = count // 2
        self.part, self.across, self.along = part, across, along
        self.send_x, self.recv_x, self.send_hi, self.recv_hi = send_x, recv_x, send_hi, recv_hi
        self.partner = 2 * self.high + 1 - self.low

    def over(self, block):
        i = block // 2
        return remote(
            self.part.at[block], self.across.at[i], self.send_x.at[i], self.recv_x.at[i],
            self.line, self.partner,
        )

    def on(self, block):
        i = block // 2
        k = lax.rem(i - self.high + self.half, self.half)
        return remote(
            self.part.at[block], self.along.at[k], self.send_hi.at[k], self.recv_hi.at[k],
            self.line, 2 * i + self.low,
        )

    def made(self, block):
        @pl.when(lax.rem(block, 2) != self.low)
        def _():
            self.over(block).start()

    def pass_on(self, block):
        @pl.when((lax.rem(block, 2) == self.low) & (block // 2 != self.high))
        def _():
            self.over(block).wait_recv()
            both = self.part[block].astype(jnp.float32) + self.across[block // 2].astype(
                jnp.float32
            )
            self.part[block] = both.astype(jnp.bfloat16)
            self.on(block).start()

    def finish(self):
        self.over(self.own).wait_recv()
        total = self.part[self.own].astype(jnp.float32) + self.across[self.high].astype(
            jnp.float32
        )
        for k in range(1, self.half):
            block = 2 * lax.rem(self.high + k, self.half) + self.low
            self.on(block).wait_recv()
            total = total + self.along[k].astype(jnp.float32)
        for i in range(self.half):
            self.over(2 * i + 1 - self.low).wait_send()
        for k in range(1, self.half):
            self.on(2 * lax.rem(self.high + k, self.half) + self.low).wait_send()
        return total

    @staticmethod
    def scratch(count, rows, width):
        half = count // 2
        dma = pltpu.SemaphoreType.DMA
        return [
            pltpu.VMEM((count, rows, width), jnp.bfloat16),
            pltpu.VMEM((half, rows, width), jnp.bfloat16),
            pltpu.VMEM((half, rows, width), jnp.bfloat16),
            dma((half,)), dma((half,)), dma((half,)), dma((half,)),
        ]


def scan_forward_kernel(
    count, cuts,
    act_ref, gate_ref, selected_ref, small_ref, output_ref,
    pre_ref, mixed_ref, mixer_low_ref, prior_ref, end_ref, summed_ref,
    state_ref, delta_ref, scanned_ref, *relay_refs,
):
    steps, inner = act_ref.shape
    tiles = inner // LANES
    state = cuts.state
    halves = state // 8
    step = pl.program_id(0)
    relay = Relay(count, *relay_refs)

    @pl.when(step == 0)
    def _():
        greet(count)
        state_ref[...] = jnp.zeros_like(state_ref)

    rates2 = -LOG2E * jnp.exp(small_ref[cuts.decay : cuts.decay + state, :])
    pre = inner_rows(
        selected_ref[0, : cuts.rank, :],
        small_ref[cuts.step : cuts.step + cuts.rank, :],
        HIGHEST,
    ) + small_ref[cuts.step_bias : cuts.step_bias + 1, :]
    pre_ref[...] = pre
    delta_ref[...] = softplus(pre)
    in_rows = cuts.rank
    out_rows = cuts.rank + state

    def group(g, states):
        states = [list(s) for s in states]
        base = pl.multiple_of(g * 8, 8)
        shift = lax.rem(steps - base, steps)
        b_cols = [
            pltpu.roll(selected_ref[0, in_rows + 8 * i : in_rows + 8 * i + 8, :], shift, 1)
            for i in range(halves)
        ]
        c_cols = [
            pltpu.roll(selected_ref[0, out_rows + 8 * i : out_rows + 8 * i + 8, :], shift, 1)
            for i in range(halves)
        ]
        d8 = delta_ref[pl.ds(base, 8), :]
        du8 = d8 * act_ref[pl.ds(base, 8), :]
        parts = [[None] * 8 for _ in range(tiles)]
        for k in range(8):
            b_now = [lane_column(b, k) for b in b_cols]
            c_now = [lane_column(c, k) for c in c_cols]
            for j in range(tiles):
                cols = slice(j * LANES, (j + 1) * LANES)
                d = jnp.broadcast_to(d8[k : k + 1, cols], (8, LANES))
                du = jnp.broadcast_to(du8[k : k + 1, cols], (8, LANES))
                total = None
                for i in range(halves):
                    old = states[j][i]
                    prior_ref[base + k, 8 * i : 8 * i + 8, cols] = old
                    new = jnp.exp2(d * rates2[8 * i : 8 * i + 8, cols]) * old + b_now[i] * du
                    states[j][i] = new
                    term = c_now[i] * new
                    total = term if total is None else total + term
                parts[j][k] = total
        for j in range(tiles):
            scanned_ref[pl.ds(base, 8), j * LANES : (j + 1) * LANES] = sublane_sums(parts[j])
        return tuple(tuple(s) for s in states)

    first = tuple(
        tuple(
            state_ref[8 * i : 8 * i + 8, j * LANES : (j + 1) * LANES] for i in range(halves)
        )
        for j in range(tiles)
    )
    last = lax.fori_loop(0, steps // 8, group, first)
    for j in range(tiles):
        for i in range(halves):
            state_ref[8 * i : 8 * i + 8, j * LANES : (j + 1) * LANES] = last[j][i]
    end_ref[...] = state_ref[...]

    mixed = scanned_ref[...] + small_ref[cuts.skip : cuts.skip + 1, :] * act_ref[...]
    gate = gate_ref[...]
    low = (mixed * (gate * sigmoid(gate))).astype(jnp.bfloat16)
    mixed_ref[...] = mixed
    mixer_low_ref[...] = low
    relay.part[step] = dot_nn(low, output_ref[...]).astype(jnp.bfloat16)
    relay.made(step)

    @pl.when(step >= 2)
    def _():
        relay.pass_on(step - 2)

    @pl.when(step == count - 1)
    def _():
        relay.pass_on(step - 1)
        relay.pass_on(step)
        summed_ref[...] = relay.finish()


def scan_forward(count, cuts, width, act, gate, selected, small, weights):
    length, inner = act.shape
    state = cuts.state
    block = length // count
    rows = pl.BlockSpec((block, inner), lambda t: (t, 0))
    whole = pl.BlockSpec((state, inner), lambda t: (0, 0))
    return pl.pallas_call(
        functools.partial(scan_forward_kernel, count, cuts),
        grid=(count,),
        in_specs=[
            rows,
            rows,
            pl.BlockSpec((1, cuts.picks, block), lambda t: (t, 0, 0)),
            pl.BlockSpec(small.shape, lambda t: (0, 0)),
            pl.BlockSpec((inner, width), lambda t: (0, 2)),
        ],
        out_specs=[
            rows,
            rows,
            rows,
            pl.BlockSpec((block, state, inner), lambda t: (t, 0, 0)),
            whole,
            pl.BlockSpec((block, width), lambda t: (0, 0)),
        ],
        out_shape=[
            jax.ShapeDtypeStruct((length, inner), jnp.float32),
            jax.ShapeDtypeStruct((length, inner), jnp.float32),
            jax.ShapeDtypeStruct((length, inner), jnp.bfloat16),
            jax.ShapeDtypeStruct((length, state, inner), jnp.float32),
            jax.ShapeDtypeStruct((state, inner), jnp.float32),
            jax.ShapeDtypeStruct((block, width), jnp.float32),
        ],
        scratch_shapes=[
            pltpu.VMEM((state, inner), jnp.float32),
            pltpu.VMEM((block, inner), jnp.float32),
            pltpu.VMEM((block, inner), jnp.float32),
            *Relay.scratch(count, block, width),
        ],
        compiler_params=pltpu.CompilerParams(
            collective_id=1, has_side_effects=True, vmem_limit_bytes=VMEM_LIMIT
        ),
        cost_estimate=pl.CostEstimate(
            flops=8 * length * state * inner,
            bytes_accessed=4 * length * inner * (state + 6),
            transcendentals=length * state * inner,
        ),
        name="scan_forward",
    )(act, gate, selected, small, weights)


def scan_backward_kernel(
    count, cuts,
    own_ref, act_ref, gate_ref, mixed_ref, pre_ref, selected_ref, small_ref, output_ref,
    prior_ref, end_ref,
    grad_gate_ref, grad_act_ref, grad_step_ref, rate_total_ref, rows_ref, grad_selected_ref,
    all_out_ref,
    incoming_ref, post_ref, delta_ref, grad_ref, grad_delta_ref, all_ref,
    part_ref, partial_ref, total_ref,
    send_hi, recv_hi, send_x, recv_x, send_rs, recv_rs, send_ag, recv_ag,
):
    steps, inner = act_ref.shape
    tiles = inner // LANES
    state = cuts.state
    halves = state // 8
    lane = lax.broadcasted_iota(jnp.int32, (8, steps), 1)
    line, own, high, low = place()
    half = count // 2
    partner = 2 * high + 1 - low
    index = pl.program_id(0)
    now = count - 1 - index

    def along(k):
        return remote(
            own_ref, all_ref.at[own], send_hi.at[k], recv_hi.at[high], line,
            2 * lax.rem(high + k, half) + low,
        )

    def across(block):
        i = block // 2
        return remote(
            all_ref.at[block], all_ref.at[block], send_x.at[i], recv_x.at[i], line, partner
        )

    def came_along(block):
        i = block // 2
        return remote(
            all_ref.at[block], all_ref.at[block], send_hi.at[0], recv_hi.at[i], line, partner
        )

    def hand_over(block):
        @pl.when((lax.rem(block, 2) == low) & (block // 2 != high))
        def _():
            came_along(block).wait_recv()
            across(block).start()

    @pl.when(index == 0)
    def _():
        greet(count)
        all_ref[own] = own_ref[...]
        incoming_ref[...] = jnp.zeros_like(incoming_ref)
        post_ref[...] = end_ref[...]
        rate_total_ref[...] = jnp.zeros_like(rate_total_ref)
        grad_step_ref[...] = jnp.zeros_like(grad_step_ref)
        rows_ref[...] = jnp.zeros_like(rows_ref)

    @pl.when(index == jnp.maximum(count - 3 - own, 0))
    def _():
        for k in range(1, half):
            along(k).start()
        across(own).start()

    @pl.when(index == 0)
    def _():
        hand_over(now)
        hand_over(now - 1)

    @pl.when(lax.rem(now, 2) != low)
    def _():
        across(now).wait_recv()

    gate = gate_ref[...]
    gate_sig = sigmoid(gate)
    grad_y = outer_cols(all_ref[now], output_ref[...])
    grad_gate_ref[...] = (
        grad_y * mixed_ref[...] * (gate_sig * (1.0 + gate * (1.0 - gate_sig)))
    ).astype(jnp.bfloat16)
    grad_mixed = grad_y * (gate * gate_sig)
    grad_ref[...] = grad_mixed
    delta_ref[...] = softplus(pre_ref[...])
    rows_ref[1:2, :] += jnp.sum(grad_mixed * act_ref[...], axis=0, keepdims=True)
    rates2 = -LOG2E * jnp.exp(small_ref[cuts.decay : cuts.decay + state, :])
    in_rows = cuts.rank
    out_rows = cuts.rank + state

    def tile_of(ref):
        return tuple(
            tuple(ref[8 * i : 8 * i + 8, j * LANES : (j + 1) * LANES] for i in range(halves))
            for j in range(tiles)
        )

    def group(turn, carry):
        incoming, posts, rate_total, in_acc, out_acc = carry
        incoming = [list(s) for s in incoming]
        posts = [list(s) for s in posts]
        rate_total = [list(s) for s in rate_total]
        in_acc, out_acc = list(in_acc), list(out_acc)
        base = pl.multiple_of((steps // 8 - 1 - turn) * 8, 8)
        shift = lax.rem(steps - base, steps)
        b_cols = [
            pltpu.roll(selected_ref[0, in_rows + 8 * i : in_rows + 8 * i + 8, :], shift, 1)
            for i in range(halves)
        ]
        c_cols = [
            pltpu.roll(selected_ref[0, out_rows + 8 * i : out_rows + 8 * i + 8, :], shift, 1)
            for i in range(halves)
        ]
        d8 = delta_ref[pl.ds(base, 8), :]
        u8 = act_ref[pl.ds(base, 8), :]
        du8 = d8 * u8
        g8 = grad_ref[pl.ds(base, 8), :]
        rate_parts = [[None] * 8 for _ in range(tiles)]
        side_parts = [[None] * 8 for _ in range(tiles)]
        for k in range(7, -1, -1):
            b_now = [lane_column(b, k) for b in b_cols]
            c_now = [lane_column(c, k) for c in c_cols]
            in_sum = [None] * halves
            out_sum = [None] * halves
            for j in range(tiles):
                cols = slice(j * LANES, (j + 1) * LANES)
                d = jnp.broadcast_to(d8[k : k + 1, cols], (8, LANES))
                du = jnp.broadcast_to(du8[k : k + 1, cols], (8, LANES))
                gm = jnp.broadcast_to(g8[k : k + 1, cols], (8, LANES))
                rate_part = None
                side_part = None
                for i in range(halves):
                    prior = prior_ref[base + k, 8 * i : 8 * i + 8, cols]
                    rates = rates2[8 * i : 8 * i + 8, cols]
                    grad_state = c_now[i] * gm + incoming[j][i]
                    passed = jnp.exp2(d * rates) * grad_state
                    incoming[j][i] = passed
                    weighted = passed * prior
                    term = weighted * rates
                    rate_part = term if rate_part is None else rate_part + term
                    term = grad_state * b_now[i]
                    side_part = term if side_part is None else side_part + term
                    term = grad_state * du
                    in_sum[i] = term if in_sum[i] is None else in_sum[i] + term
                    term = posts[j][i] * gm
                    out_sum[i] = term if out_sum[i] is None else out_sum[i] + term
                    rate_total[j][i] = rate_total[j][i] + weighted * d
                    posts[j][i] = prior
                rate_parts[j][k] = rate_part
                side_parts[j][k] = side_part
            here = lane == base + k
            for i in range(halves):
                in_acc[i] = jnp.where(here, jnp.sum(in_sum[i], axis=1, keepdims=True), in_acc[i])
                out_acc[i] = jnp.where(here, jnp.sum(out_sum[i], axis=1, keepdims=True), out_acc[i])
        for j in range(tiles):
            cols = slice(j * LANES, (j + 1) * LANES)
            side = sublane_sums(side_parts[j])
            grad_delta_ref[pl.ds(base, 8), cols] = (
                sublane_sums(rate_parts[j]) * (1.0 / LOG2E) + u8[:, cols] * side
            )
            grad_act_ref[pl.ds(base, 8), cols] = d8[:, cols] * side
        return (
            tuple(tuple(s) for s in incoming),
            tuple(tuple(s) for s in posts),
            tuple(tuple(s) for s in rate_total),
            tuple(in_acc),
            tuple(out_acc),
        )

    empty = tuple(jnp.zeros((8, steps), jnp.float32) for _ in range(halves))
    incoming, posts, rate_total, in_acc, out_acc = lax.fori_loop(
        0,
        steps // 8,
        group,
        (tile_of(incoming_ref), tile_of(post_ref), tile_of(rate_total_ref), empty, empty),
    )
    for i in range(halves):
        part_ref[now, in_rows + 8 * i : in_rows + 8 * i + 8, :] = in_acc[i]
        part_ref[now, out_rows + 8 * i : out_rows + 8 * i + 8, :] = out_acc[i]
        for j in range(tiles):
            cols = slice(j * LANES, (j + 1) * LANES)
            incoming_ref[8 * i : 8 * i + 8, cols] = incoming[j][i]
            post_ref[8 * i : 8 * i + 8, cols] = posts[j][i]
            rate_total_ref[8 * i : 8 * i + 8, cols] = rate_total[j][i]

    grad_act_ref[...] += grad_ref[...] * small_ref[cuts.skip : cuts.skip + 1, :]
    grad_pre = grad_delta_ref[...] * sigmoid(pre_ref[...])
    rows_ref[0:1, :] += jnp.sum(grad_pre, axis=0, keepdims=True)
    grad_step_ref[...] += dot_nn(selected_ref[0, : cuts.rank, :], grad_pre, HIGHEST)
    part_ref[now, : cuts.rank, :] = outer_cols(
        small_ref[cuts.step : cuts.step + cuts.rank, :], grad_pre, HIGHEST
    )

    def partial_to(block):
        return remote(
            part_ref.at[block], partial_ref.at[own], send_rs.at[block], recv_rs.at[own], line, block
        )

    @pl.when(now != own)
    def _():
        partial_to(now).start()

    def total_to(k):
        return remote(
            total_ref.at[own], total_ref.at[own], send_ag.at[k], recv_ag.at[own], line,
            lax.rem(own + k, count),
        )

    @pl.when(now >= 2)
    def _():
        hand_over(now - 2)

    @pl.when(index == jnp.minimum(count - 1 - own + 2, count - 1))
    def _():
        total = part_ref[own]
        for k in range(1, count):
            there = lax.rem(own + k, count)
            remote(
                part_ref.at[own], partial_ref.at[there], send_rs.at[own], recv_rs.at[there],
                line, there,
            ).wait_recv()
            total = total + partial_ref[there]
        total_ref[own] = total
        for k in range(1, count):
            total_to(k).start()

    @pl.when(index == count - 1)
    def _():
        for k in range(1, count):
            there = lax.rem(own + k, count)
            remote(
                total_ref.at[there], total_ref.at[there], send_ag.at[k], recv_ag.at[there],
                line, there,
            ).wait_recv()
        grad_selected_ref[...] = total_ref[...]
        all_out_ref[...] = all_ref[...]
        for k in range(1, half):
            along(k).wait_send()
        for i in range(half):
            across(2 * i + low).wait_send()
        for k in range(1, count):
            partial_to(lax.rem(own + k, count)).wait_send()
            total_to(k).wait_send()


def scan_backward(count, cuts, grad_low, act, gate, mixed, pre, selected, small, weights, priors, end):
    length, inner = act.shape
    state = cuts.state
    block = length // count
    width = grad_low.shape[1]
    half = count // 2

    def back(t):
        return count - 1 - t

    rows = pl.BlockSpec((block, inner), lambda t: (back(t), 0))
    whole = pl.BlockSpec((state, inner), lambda t: (0, 0))
    dma = pltpu.SemaphoreType.DMA
    picked = (count, cuts.picks, block)
    return pl.pallas_call(
        functools.partial(scan_backward_kernel, count, cuts),
        grid=(count,),
        in_specs=[
            pl.BlockSpec((block, width), lambda t: (0, 0)),
            rows,
            rows,
            rows,
            rows,
            pl.BlockSpec((1, cuts.picks, block), lambda t: (back(t), 0, 0)),
            pl.BlockSpec(small.shape, lambda t: (0, 0)),
            pl.BlockSpec((inner, width), lambda t: (0, 2)),
            pl.BlockSpec((block, state, inner), lambda t: (back(t), 0, 0)),
            whole,
        ],
        out_specs=[
            rows,
            rows,
            pl.BlockSpec((cuts.rank, inner), lambda t: (0, 0)),
            whole,
            pl.BlockSpec((8, inner), lambda t: (0, 0)),
            pl.BlockSpec(picked, lambda t: (0, 0, 0)),
            pl.BlockSpec((count, block, width), lambda t: (0, 0, 0)),
        ],
        out_shape=[
            jax.ShapeDtypeStruct((length, inner), jnp.bfloat16),
            jax.ShapeDtypeStruct((length, inner), jnp.float32),
            jax.ShapeDtypeStruct((cuts.rank, inner), jnp.float32),
            jax.ShapeDtypeStruct((state, inner), jnp.float32),
            jax.ShapeDtypeStruct((8, inner), jnp.float32),
            jax.ShapeDtypeStruct(picked, jnp.float32),
            jax.ShapeDtypeStruct((count, block, width), jnp.bfloat16),
        ],
        scratch_shapes=[
            pltpu.VMEM((state, inner), jnp.float32),
            pltpu.VMEM((state, inner), jnp.float32),
            pltpu.VMEM((block, inner), jnp.float32),
            pltpu.VMEM((block, inner), jnp.float32),
            pltpu.VMEM((block, inner), jnp.float32),
            pltpu.VMEM((count, block, width), jnp.bfloat16),
            pltpu.VMEM(picked, jnp.float32),
            pltpu.VMEM(picked, jnp.float32),
            pltpu.VMEM(picked, jnp.float32),
            dma((half,)), dma((half,)), dma((half,)), dma((half,)),
            dma((count,)), dma((count,)), dma((count,)), dma((count,)),
        ],
        compiler_params=pltpu.CompilerParams(
            collective_id=2, has_side_effects=True, vmem_limit_bytes=VMEM_LIMIT
        ),
        cost_estimate=pl.CostEstimate(
            flops=20 * length * state * inner,
            bytes_accessed=4 * length * inner * (state + 6),
            transcendentals=length * state * inner,
        ),
        name="scan_backward",
    )(grad_low, act, gate, mixed, pre, selected, small, weights, priors, end)


def back_kernel(
    count, cuts, width,
    grad_selected_ref, small_ref, conv_w_ref, gate_w_ref, ext_ref, sum_ref, grad_act_ref, grad_gate_ref,
    summed_ref, grad_conv_ref, grad_select_ref, rows_ref,
    grad_sum_ref, *relay_refs,
):
    relay = Relay(count, *relay_refs)
    length, inner = sum_ref.shape
    rows = length // count
    kernel = cuts.kernel
    greet(count)
    grad_select_ref[...] = jnp.zeros_like(grad_select_ref)
    rows_ref[...] = jnp.zeros_like(rows_ref)
    grad_sum_ref[length:, :] = jnp.zeros((8, inner), jnp.float32)
    select = small_ref[: cuts.picks, :].astype(jnp.bfloat16)

    def first(b, carry):
        start = pl.multiple_of(b * rows, rows)
        grad_selected = grad_selected_ref[b].astype(jnp.bfloat16)
        total = sum_ref[pl.ds(start, rows), :]
        sig = sigmoid(total)
        grad_act = grad_act_ref[pl.ds(start, rows), :] + inner_rows(grad_selected, select)
        grad_sum = grad_act * (sig * (1.0 + total * (1.0 - sig)))
        grad_sum_ref[pl.ds(start, rows), :] = grad_sum
        grad_select_ref[...] += dot_nn(grad_selected, (total * sig).astype(jnp.bfloat16))
        window = ext_ref[pl.ds(start, rows + 8), :]
        for k in range(kernel):
            rows_ref[k : k + 1, :] += jnp.sum(
                grad_sum * window[9 - kernel + k : 9 - kernel + k + rows], axis=0, keepdims=True
            )
        rows_ref[kernel : kernel + 1, :] += jnp.sum(grad_sum, axis=0, keepdims=True)
        return carry

    lax.fori_loop(0, count, first, 0)

    def order(j):
        return j // 2 + lax.rem(j, 2) * (count // 2)

    def second(j, carry):
        b = order(j)
        start = pl.multiple_of(b * rows, rows)
        window = grad_sum_ref[pl.ds(start, rows + 8), :]
        grad_conv = None
        for k in range(kernel):
            tap = small_ref[cuts.taps + k : cuts.taps + k + 1, :]
            term = tap * window[kernel - 1 - k : kernel - 1 - k + rows]
            grad_conv = term if grad_conv is None else grad_conv + term
        grad_conv = grad_conv.astype(jnp.bfloat16)
        grad_conv_ref[pl.ds(start, rows), :] = grad_conv
        relay.part[b] = (
            dot_nn(grad_conv, conv_w_ref[...])
            + dot_nn(grad_gate_ref[pl.ds(start, rows), :], gate_w_ref[...])
        ).astype(jnp.bfloat16)
        relay.made(b)
        return carry

    lax.fori_loop(0, count, second, 0)

    def third(j, carry):
        relay.pass_on(order(j))
        return carry

    lax.fori_loop(0, count, third, 0)
    summed_ref[...] = relay.finish()


def back(count, cuts, width, grad_selected, small, weights, ext, conv_sum, grad_act, grad_gate):
    length, inner = conv_sum.shape
    rows = length // count

    def full(shape):
        return pl.BlockSpec(shape, lambda i: (0,) * len(shape))

    return pl.pallas_call(
        functools.partial(back_kernel, count, cuts, width),
        grid=(1,),
        in_specs=[
            full(grad_selected.shape),
            full(small.shape),
            pl.BlockSpec((inner, width), lambda i: (0, 0)),
            pl.BlockSpec((inner, width), lambda i: (0, 1)),
            full(ext.shape),
            full(conv_sum.shape),
            full(grad_act.shape),
            full(grad_gate.shape),
        ],
        out_specs=[
            full((rows, width)),
            full((length, inner)),
            full((cuts.picks, inner)),
            full((8, inner)),
        ],
        out_shape=[
            jax.ShapeDtypeStruct((rows, width), jnp.float32),
            jax.ShapeDtypeStruct((length, inner), jnp.bfloat16),
            jax.ShapeDtypeStruct((cuts.picks, inner), jnp.float32),
            jax.ShapeDtypeStruct((8, inner), jnp.float32),
        ],
        scratch_shapes=[
            pltpu.VMEM((length + 8, inner), jnp.float32),
            *Relay.scratch(count, rows, width),
        ],
        compiler_params=pltpu.CompilerParams(
            collective_id=3, has_side_effects=True, vmem_limit_bytes=VMEM_LIMIT
        ),
        cost_estimate=pl.CostEstimate(
            flops=4 * length * width * inner,
            bytes_accessed=20 * length * inner,
            transcendentals=length * inner,
        ),
        name="back",
    )(grad_selected, small, weights, weights, ext, conv_sum, grad_act, grad_gate)


def body(
    tokens,
    cotangent,
    routes,
    mixer_gain,
    input_proj,
    conv_weight,
    conv_bias,
    select_proj,
    step_proj,
    step_bias,
    decay_log,
    skip_gain,
    output_proj,
    expert_gain,
    router,
    expert_up,
    expert_down,
):
    rows = tokens.shape[1]
    width = tokens.shape[2]
    shard = input_proj.shape[2]
    rank = step_proj.shape[0]
    state = decay_log.shape[0]
    kernel = conv_weight.shape[0]
    picks = select_proj.shape[0]
    count = lax.axis_size("seq")
    lines = lax.axis_size("dp")
    shard_rows = -(-shard // 16) * 16
    cuts = Cuts(picks, rank, state, kernel)

    x_in = tokens.reshape(rows, width)
    gain_one = mixer_gain.astype(jnp.float32)
    normed = rms_norm(x_in, gain_one).astype(jnp.bfloat16)

    small = jnp.concatenate(
        [
            select_proj,
            step_proj,
            decay_log,
            conv_weight,
            conv_bias[None, :],
            step_bias[None, :],
            skip_gain[None, :],
        ],
        axis=0,
    )
    small_pad = -(-cuts.rows // LANES) * LANES
    small = jnp.pad(small, ((0, small_pad - cuts.rows), (0, 0)))
    packed = jnp.concatenate(
        [input_proj.reshape(2 * width, shard).T, output_proj, small.T], axis=1
    )
    packed = jnp.pad(packed, ((0, shard_rows - shard), (0, 0)))
    w_up, w_down = (
        lax.all_gather(expert_up, "seq", axis=0, tiled=True),
        lax.all_gather(expert_down, "seq", axis=1, tiled=True),
    )
    (normed_all, weights, small_all, conv_ext, conv_sum, conv_act, gate_branch, selected) = front(
        count, lines, cuts, normed, packed
    )
    pre, mixed, mixer_low, priors, end, mixer_out = scan_forward(
        count, cuts, width, conv_act, gate_branch, selected, small_all, weights
    )
    middle = x_in + mixer_out

    experts = router.shape[0]
    copies = lax.axis_size("dp") // experts
    capacity = CAP
    gain_two = expert_gain.astype(jnp.float32)
    normed_two = rms_norm(middle, gain_two).astype(jnp.bfloat16)
    probs = jax.nn.softmax(outer_cols(normed_two, router), axis=-1)
    route = routes.reshape(rows)
    chosen = (route[:, None] == lax.broadcasted_iota(jnp.int32, (rows, experts), 1)).astype(
        jnp.float32
    )
    gate = jnp.sum(chosen * probs, axis=1)
    earlier = (
        lax.broadcasted_iota(jnp.int32, (rows, rows), 0)
        > lax.broadcasted_iota(jnp.int32, (rows, rows), 1)
    ).astype(jnp.float32)
    before = jnp.dot(earlier, chosen, precision=HIGHEST)
    position = jnp.sum(before * chosen, axis=1).astype(jnp.int32)
    slot = route * capacity + position
    dispatch_table = (
        slot[None, :] == lax.broadcasted_iota(jnp.int32, (experts * capacity, rows), 0)
    ).astype(jnp.bfloat16)
    buffer = jnp.dot(dispatch_table, normed_two, preferred_element_type=jnp.float32).astype(
        jnp.bfloat16
    )
    send = jnp.repeat(buffer.reshape(experts, capacity, width), copies, axis=0)
    received = lax.all_to_all(send, "dp", split_axis=0, concat_axis=0, tiled=True)
    sources = received.shape[0]
    expert_rows = received.reshape(-1, width)
    expert_pre = jnp.dot(expert_rows, w_up, preferred_element_type=jnp.float32)
    expert_act, gelu_pull = jax.vjp(gelu_exact, expert_pre)
    act_low = expert_act.astype(jnp.bfloat16)
    partial_out = jnp.dot(act_low, w_down, preferred_element_type=jnp.float32).reshape(
        sources, capacity, width
    )
    returned = lax.all_to_all(
        partial_out.astype(jnp.bfloat16), "dp", split_axis=0, concat_axis=0, tiled=True
    ).astype(partial_out.dtype)
    expert_out = jnp.sum(returned.reshape(experts, copies, capacity, width), axis=1).reshape(
        experts * capacity, width
    )
    picked = jnp.take(expert_out, slot, axis=0)
    output = middle + gate[:, None] * picked
    grad_out = cotangent.reshape(rows, width)
    grad_pick = (gate[:, None] * grad_out).astype(jnp.bfloat16)
    grad_gate = jnp.sum(grad_out * picked, axis=1)
    grad_buffer = jnp.dot(dispatch_table, grad_pick, preferred_element_type=jnp.float32).astype(
        jnp.bfloat16
    )
    grad_send = jnp.repeat(grad_buffer.reshape(experts, capacity, width), copies, axis=0)
    grad_rows = lax.all_to_all(grad_send, "dp", split_axis=0, concat_axis=0, tiled=True)
    grad_flat = grad_rows.reshape(-1, width)
    grad_down_w = inner_rows(act_low, grad_flat)
    grad_act = outer_cols(grad_flat, w_down)
    grad_pre = gelu_pull(grad_act)[0].astype(jnp.bfloat16)
    grad_up_w = inner_rows(expert_rows, grad_pre)
    grad_in_rows = outer_cols(grad_pre, w_up).reshape(sources, capacity, width)
    grad_back = lax.all_to_all(
        grad_in_rows.astype(jnp.bfloat16), "dp", split_axis=0, concat_axis=0, tiled=True
    ).astype(grad_in_rows.dtype)
    grad_slots = jnp.sum(grad_back.reshape(experts, copies, capacity, width), axis=1).reshape(
        experts * capacity, width
    )
    grad_logits = gate[:, None] * (chosen - probs) * grad_gate[:, None]
    router_full = router.astype(jnp.float32)
    grad_normed_two = jnp.take(grad_slots, slot, axis=0) + jnp.dot(
        grad_logits, router_full, precision=HIGHEST
    )
    grad_router = inner_rows(grad_logits, normed_two.astype(jnp.float32), HIGHEST)
    unused_two, pull_two = jax.vjp(rms_norm, middle, gain_two)
    grad_middle_norm, grad_gain_two = pull_two(grad_normed_two)
    grad_middle = grad_out + grad_middle_norm
    grad_middle_low = grad_middle.astype(jnp.bfloat16)

    (grad_gate_branch, grad_act, grad_step_w, rate_total, scan_rows, grad_selected, grad_middle_all) = (
        scan_backward(
            count, cuts, grad_middle_low, conv_act, gate_branch, mixed, pre, selected, small_all,
            weights, priors, end,
        )
    )
    grad_normed, grad_conv_input, grad_select_w, conv_rows = back(
        count, cuts, width, grad_selected, small_all, weights, conv_ext, conv_sum, grad_act,
        grad_gate_branch,
    )
    grad_decay = rate_total * -jnp.exp(small_all[cuts.decay : cuts.decay + state])
    normed_rows = normed_all.reshape(-1, width)
    grad_output_w = inner_rows(mixer_low, grad_middle_all.reshape(-1, width))
    grad_conv_w = inner_rows(grad_conv_input, normed_rows)
    grad_gate_w = inner_rows(grad_gate_branch, normed_rows)
    grad_small = jnp.concatenate(
        [
            grad_select_w,
            grad_step_w,
            grad_decay,
            conv_rows[: kernel + 1],
            scan_rows[:2],
            jnp.zeros((small_pad - cuts.rows, grad_decay.shape[1]), jnp.float32),
        ],
        axis=0,
    )
    grad_packed = jnp.concatenate(
        [part.astype(jnp.bfloat16) for part in (grad_conv_w, grad_gate_w, grad_output_w, grad_small.T)],
        axis=1,
    )
    grad_shard = lax.psum_scatter(
        grad_packed[: lines * shard_rows], "dp", scatter_dimension=0, tiled=True
    )[:shard].astype(jnp.float32)
    grad_input_w = grad_shard[:, : 2 * width].T.reshape(2, width, shard)
    small_shard = grad_shard[:, 3 * width :].T
    cut = 0
    small_grads = []
    for number in (picks, rank, state, kernel, 1, 1, 1):
        small_grads.append(small_shard[cut : cut + number])
        cut += number

    grad_gain_one = (
        jnp.sum(
            weights[:, :width].astype(jnp.float32) * grad_conv_w
            + weights[:, width : 2 * width].astype(jnp.float32) * grad_gate_w,
            axis=0,
        )
        / gain_one
    )
    unused_one, pull_one = jax.vjp(lambda v: rms_norm(v, gain_one), x_in)
    grad_tokens = grad_middle + pull_one(grad_normed)[0]
    expert_grads = (
        lax.psum_scatter(
            grad_up_w.astype(jnp.bfloat16), "seq", scatter_dimension=0, tiled=True
        ).astype(jnp.float32),
        lax.psum_scatter(
            grad_down_w.astype(jnp.bfloat16), "seq", scatter_dimension=1, tiled=True
        ).astype(jnp.float32),
    )
    small_sums = lax.psum(
        jnp.concatenate([grad_gain_one[None], grad_gain_two[None], grad_router], axis=0),
        ("dp", "seq"),
    )
    return (
        output.reshape(tokens.shape),
        grad_tokens.reshape(tokens.shape),
        small_sums[0],
        grad_input_w,
        small_grads[3],
        small_grads[4].reshape(shard),
        small_grads[0],
        small_grads[1],
        small_grads[5].reshape(shard),
        small_grads[2],
        small_grads[6].reshape(shard),
        grad_shard[:, 2 * width : 3 * width],
        small_sums[1],
        small_sums[2:],
        expert_grads[0],
        expert_grads[1],
    )


def solution(mesh):
    both = ("dp", "seq")
    placed = (
        P("dp", "seq", None),
        P("dp", "seq", None),
        P("dp", "seq", None),
        P(),
        P(None, None, both),
        P(None, both),
        P(both),
        P(None, both),
        P(None, both),
        P(both),
        P(None, both),
        P(both),
        P(both, None),
        P(),
        P(),
        P("seq", "dp"),
        P("dp", "seq"),
    )
    return jax.shard_map(
        body,
        mesh=mesh,
        in_specs=placed,
        out_specs=(
            P("dp", "seq", None),
            P("dp", "seq", None),
            P(),
            P(None, None, both),
            P(None, both),
            P(both),
            P(None, both),
            P(None, both),
            P(both),
            P(None, both),
            P(both),
            P(both, None),
            P(),
            P(),
            P("seq", "dp"),
            P("dp", "seq"),
        ),
        check_vma=False,
    )
```

time: 2110 us -> 851 us (0.40); the launches traced: 2080 us -> 846 us
  waiting for transfers between devices: 988 us -> 279 us
  Pallas kernels: 0 us -> 386 us
  local copies, waits for them, and re-layouts: 350 us -> 20.8 us
  blocking collectives: 316 us -> 41.9 us
  other arithmetic: 237 us -> 30.9 us
  starting transfers between devices: 76.8 us -> 22.2 us
  matrix products: 90.5 us -> 50.7 us
    unnamed x13 -> x5, waiting for transfers between devices: 607 us -> 1.43 us
    pallas_call x0 -> x4, Pallas kernels: none -> 386 us  [the longest x1 127 us: scan_backward(): pl.pallas_call(functools.partial(scan_backward_kernel, count, cuts), grid...]
    all_gather x4 -> x0, blocking collectives: 272 us -> none  [the longest x1 70.1 us: body(): lax.all_gather(shards[3], ('dp', 'seq'), axis=1, tiled=True)]
    slice x102 -> x11, local copies, waits for them, and re-layouts: 181 us -> 5.05 us  [the longest x5 1.58 us: body(): small_grads.append(small_shard[cut:cut + number])]
    reduce_sum x99 -> x1, other arithmetic: 106 us -> 0.15 us  [rms_norm(): values * lax.rsqrt(jnp.mean(values * values, axis=-1, keepdims=True) + 1e...]
    add x79 -> x0, other arithmetic: 64.1 us -> none  [the longest x32 37 us: backward_turn(): jnp.sum(weighted * rates, axis=0) + block_act[index] * input_side]
    psum x1 -> x0, waiting for transfers between devices: 58.3 us -> none  [body(): lax.psum((grad_gain_one, grad_gain_two, grad_router), ('dp', 'seq'))]
    ppermute x16 -> x0, waiting for transfers between devices: 55.7 us -> none  [from_behind(): return lax.ppermute(value, axis, pairs)]
  transfers between devices with their start and end apart: 30 -> 9, of which waited for: 24 -> 7; matrix products, arithmetic and copies ran while one was open for 13% -> 6% of each run, Pallas kernels for 0% -> 25%
where the time goes in v2:
time: 851 us; the launch traced here: 846 us
  Pallas kernels  386 us (45%)
  waiting for transfers between devices  279 us (33%)
  matrix products  50.7 us (6%)
  blocking collectives  41.9 us (5%)
  other arithmetic  30.9 us (4%)
  starting transfers between devices  22.2 us (3%)
  local copies, waits for them, and re-layouts  20.8 us (2%)
  between operations  14.2 us (2%)
    reduce_scatter x1, waiting for transfers between devices, body(): lax.psum_scatter(grad_up_w.astype(jnp.bfloat16), 'seq', scatter_dimension...  129 us
    pallas_call x1, Pallas kernels, scan_backward(): pl.pallas_call(functools.partial(scan_backward_kernel, count, cuts), grid...  127 us
    pallas_call x1, Pallas kernels, front(): pl.pallas_call(functools.partial(front_kernel, count, lines, cuts), in_sp...  125 us
    reduce_scatter x1, waiting for transfers between devices, body(): lax.psum_scatter(grad_down_w.astype(jnp.bfloat16), 'seq', scatter_dimensi...  107 us
    pallas_call x1, Pallas kernels, scan_forward(): pl.pallas_call(functools.partial(scan_forward_kernel, count, cuts), grid=...  86.7 us
    pallas_call x1, Pallas kernels, back(): pl.pallas_call(functools.partial(back_kernel, count, cuts, width), grid=(...  47.9 us
    psum x1, blocking collectives, body(): lax.psum(jnp.concatenate([grad_gain_one[None], grad_gain_two[None], grad_...  41.9 us
    all_gather x1, waiting for transfers between devices, body(): lax.all_gather(expert_down, 'seq', axis=1, tiled=True)  31.9 us
  transfers between devices with their start and end apart: 9, of which 7 were waited for; matrix products, arithmetic and copies ran while one was open for 6% of the time, Pallas kernels for 25%

profile of v2, /device:TPU:31, one launch (start us, length us, event | category | flops | bytes accessed | tf_op | source)
XLA Modules:
  0.0 846.4 jit_solution(9362003270744933320)
XLA Ops:
  10.1 0.8 copy.48
  11.6 0.8 copy.46
  13.2 0.8 copy.47
  14.8 1.0 copy.58
  15.8 0.8 concatenate.16
  16.8 0.9 fusion.11.packed_ref
  17.6 0.8 fusion.19.normed_ref
  18.5 124.6 %front.1 = (bf16[8,128,1152]{2,1,0:T(8,128)(2,1)}, bf16[384,3712]{1,0:T(8,128)(2,1)}, f32[256,384]{1,0:T(8,128)}, f32[1032,384]{1,0:T(8,128)}, f32[1024,384]{1,0...) custom-call(bf16[128,1152]{1,0:T(8,128)(2,1)} %fusion.19.normed_ref, ...), custom_call_target="tpu_custom_call" | custom-call | flops 1811939328 | bytes 7864320 | tf_op jit(solution)/shard_map/front/pallas_call | solution.py:268
  143.1 86.7 %scan_forward.1 = (f32[1024,384]{1,0:T(8,128)}, f32[1024,384]{1,0:T(8,128)}, bf16[1024,384]{1,0:T(8,128)(2,1)}, f32[1024,16,384]{2,1,0:T(8,128)}, f32[16,384]{1,0:T(8,128)}, /*index=5*/f32[128,1152]{1,0:T(8,128)}) custom-call(f32[1024,384]{1,0:T(8,128)} %get-tuple-element.42.act_ref, f32[1024,384]{1,0:T(8,128)} %get-tuple-element.43.gate_ref, ...), custom_call_target="tpu_custom_call" | custom-call | flops 50331648 | bytes 34603008 | tf_op jit(solution)/shard_map/scan_forward/pallas_call | solution.py:466
  229.9 1.5 multiply_reduce_fusion.2
  231.6 1.1 convolution_convert_fusion.6
  232.7 6.8 all-to-all-start
  239.8 1.1 convolution_convert_fusion.5
  240.9 5.5 all-to-all-done
  246.4 5.2 all-to-all-start.2
  251.7 6.6 fusion.43
  258.5 31.9 %all-gather.5.cloned.1.call-done = bf16[3072,1152]{0,1:T(8,128)(2,1)} async-done(((bf16[3072,144]{0,1:T(8,128)(2,1)}), bf16[3072,1152]{0,1:T(8,128)(2,1)}) %all-gather.5.cloned.1.call-update) | async-done | bytes 7077904 | tf_op jit(solution)/shard_map/all_gather | solution.py:989
  290.4 11.1 %add_convert_fusion = (bf16[224,3072]{1,0:T(8,128)(2,1)}, f32[224,3072]{1,0:T(8,128)S(1)}) fusion(f32[224,3072]{1,0:T(8,128)} %fusion.43, bf16[224,1152]{1,0:T(8,128)(2,1)S(1)} %bitcast.94, bf16[3072,1152]{0,1:T(8,128)(2,1)} %all-gather.5.cloned.1.call-done), kind=kOutput, calls=%fused_computation.7 | convolution fusion | flops 1634992128 | bytes 14475264 | tf_op jit(solution)/shard_map/dot_general | solution.py:38
  301.9 3.1 convolution_convert_fusion.4
  305.1 4.0 all-to-all-start.1
  309.1 6.6 convolution_convert_fusion.3
  315.9 6.0 all-to-all-start.3
  321.9 1.1 bitcast_convert_fusion.1
  323.1 1.7 gather_fusion
  324.7 4.2 all-to-all-done.3
  328.9 1.1 bitcast_convert_fusion
  330.0 1.7 gather_fusion.1
  331.7 2.1 fusion.16
  334.5 0.9 fusion.37
  335.5 127.3 %scan_backward.1 = (bf16[1024,384]{1,0:T(8,128)(2,1)}, f32[1024,384]{1,0:T(8,128)}, f32[72,384]{1,0:T(8,128)}, f32[16,384]{1,0:T(8,128)}, f32[8,384]{1,0:T(8,128...) custom-call(bf16[128,1152]{1,0:T(8,128)(2,1)} %get-tuple-element.106.own_ref, ...), custom_call_target="tpu_custom_call" | custom-call | flops 125829120 | bytes 34603008 | tf_op jit(solution)/shard_map/scan_backward/pallas_call | solution.py:762
  464.3 47.9 %back.1 = (f32[128,1152]{1,0:T(8,128)}, bf16[1024,384]{1,0:T(8,128)(2,1)}, f32[104,384]{1,0:T(8,128)}, f32[8,384]{1,0:T(8,128)}) custom-call(f32[8,104,128]{2,1,0:T(8,128)} %get-tuple-element.52.grad_selected_ref, f32[256,384]{1,0:T(8,128)} %get-tuple-element.45.small_ref, bf16[384,3712]{1,0:T(8,128)(2,1)} %get-tuple-element.46.output_ref.conv_w_ref.gate_w_ref, ...), custom_call_target="tpu_custom_call" | custom-call | flops 1811939328 | bytes 7864320 | tf_op jit(solution)/shard_map/back/pallas_call | solution.py:893
  512.9 0.9 convert.21
  514.2 0.8 copy.52
  515.1 3.0 fusion.44
  518.1 2.5 convolution_convert_fusion.2
  520.7 3.0 fusion.41
  523.7 11.1 %pad_maximum_fusion = bf16[320,3712]{1,0:T(8,128)(2,1)} fusion(bf16[384,256]{1,0:T(8,128)(2,1)S(1)} %copy-done.17, bf16[384,1152]{1,0:T(8,128)(2,1)S(1)} %convolution_convert_fusion.2, bf16[384,1152]{1,0:T(8,128)(2,1)S(1)} %get-tuple-element.118, bf16[384,1152]{1,0:T(8,128)(2,1)S(1)} %get-tuple-element.116), kind=kLoop, calls=%fused_computation.27 | loop fusion | flops 9502720 | bytes 5226496 | tf_op jit(solution)/shard_map/concatenate | solution.py:1098
  534.9 5.0 convolution_convert_fusion
  539.9 1.0 copy-done.8
  540.9 6.3 convolution_convert_fusion.1
  548.2 41.9 %psum.7 = f32[6,1152]{1,0:T(8,128)S(1)} all-reduce(f32[6,1152]{1,0:T(8,128)S(1)} %pad_maximum_fusion.3), channel_id=1, replica_groups=mesh['dp'=4,'seq'=8] {'dp','seq'}, use_global_device_ids=true, to_apply=%region_11.13 | all-reduce | flops 6912 | bytes 55296 | tf_op jit(solution)/shard_map/psum | solution.py:1131
  591.5 1.0 fusion.14
  592.5 1.1 slice_convert_fusion
  597.4 0.9 copy.60
  599.0 106.8 %reduce-scatter.8.cloned.1.call-done = bf16[3072,144]{0,1:T(8,128)(2,1)} async-done(((bf16[3072,1152]{0,1:T(8,128)(2,1)}), bf16[3072,144]{0,1:T(8,128)(2,1)}) %reduce-scatter.8.cloned.1.call-update) | async-done | bytes 884752 | tf_op jit(solution)/shard_map/reduce_scatter | solution.py:1127
  705.7 2.6 convert_element_type.122
  708.3 129.1 %reduce-scatter.6.cloned.1.call-done = bf16[144,3072]{1,0:T(8,128)(2,1)} async-done(((bf16[1152,3072]{1,0:T(8,128)(2,1)}), bf16[144,3072]{1,0:T(8,128)(2,1)}) %reduce-scatter.6.cloned.1.call-update) | async-done | bytes 884752 | tf_op jit(solution)/shard_map/reduce_scatter | solution.py:1124
  837.3 2.6 convert_element_type.120
  (107 shorter events, 17.1 us)
Async XLA Ops:
  7.2 232.3 %copy-start = (bf16[4,1152]{1,0:T(4,128)(2,1)S(1)}, bf16[4,1152]{1,0:T(4,128)(2,1)}, u32[]{:S(2)}) copy-start(bf16[4,1152]{1,0:T(4,128)(2,1)} %param.33) | copy-start | bytes 27652
  7.2 9.4 %copy-start.2 = (f32[1,128,1152]{2,1,0:T(8,128)S(1)}, f32[1,128,1152]{2,1,0:T(8,128)}, u32[]{:S(2)}) copy-start(f32[1,128,1152]{2,1,0:T(8,128)} %param.19) | copy-start | bytes 1769476
  7.2 9.6 %copy-start.18 = (bf16[72,1152]{1,0:T(8,128)(2,1)S(1)}, bf16[72,1152]{1,0:T(8,128)(2,1)}, u32[]{:S(2)}) copy-start(bf16[72,1152]{1,0:T(8,128)(2,1)} %param.31) | copy-start | bytes 497668
  7.2 244.4 %all-gather.3.cloned.1.call-start = ((), (), s32[]{:S(2)}) async-start(), calls=%async_computation.7 | async-start | bytes 7962624 | tf_op jit(solution)/shard_map/all_gather | solution.py:988
  8.0 282.4 %all-gather.5.cloned.1.call-start = ((), (), s32[]{:S(2)}) async-start(), calls=%async_computation.8 | async-start | bytes 7962624 | tf_op jit(solution)/shard_map/all_gather | solution.py:989
  143.1 86.7 %copy-start.21 = (s32[1,128,1]{1,2,0:T(1,128)S(1)}, s32[1,128,1]{1,2,0:T(1,128)}, u32[]{:S(2)}) copy-start(s32[1,128,1]{1,2,0:T(1,128)} %param.21) | copy-start | bytes 1540
  229.7 10.0 %copy-start.5 = (f32[1,128,1152]{2,1,0:T(8,128)S(1)}, f32[1,128,1152]{2,1,0:T(8,128)}, u32[]{:S(2)}) copy-start(f32[1,128,1152]{2,1,0:T(8,128)} %param.20) | copy-start | bytes 1769476
  232.7 13.8 %all-to-all-start = ((bf16[4,56,1152]{2,1,0:T(8,128)(2,1)}), bf16[4,56,1152]{2,1,0:T(8,128)(2,1)S(1)}, u32[]{:S(2)}, u32[]{:S(2)}) async-start(bf16[4,56,1152]{2,1,0:T(8,128)(2,1)} %bitcast.7), calls=%async_computation | async-start | bytes 1032192 | tf_op jit(solution)/shard_map/all_to_all | solution.py:1024
  246.4 11.8 %copy-start.7 = (bf16[4,56,1152]{2,1,0:T(8,128)(2,1)}, bf16[4,56,1152]{2,1,0:T(8,128)(2,1)S(1)}, u32[]{:S(2)}) copy-start(bf16[4,56,1152]{2,1,0:T(8,128)(2,1)S(1)} %all-to-all-done) | copy-start | bytes 1548292
  246.4 12.1 %all-to-all-start.2 = ((bf16[4,56,1152]{2,1,0:T(8,128)(2,1)}), bf16[4,56,1152]{2,1,0:T(8,128)(2,1)S(1)}, u32[]{:S(2)}, u32[]{:S(2)}) async-start(bf16[4,56,1152]{2,1,0:T(8,128)(2,1)} %bitcast.96), calls=%async_computation.2 | async-start | bytes 1032192 | tf_op jit(solution)/shard_map/all_to_all | solution.py:1048
  258.5 42.9 %copy-start.14 = (bf16[4,56,1152]{2,1,0:T(8,128)(2,1)}, bf16[4,56,1152]{2,1,0:T(8,128)(2,1)S(1)}, u32[]{:S(2)}) copy-start(bf16[4,56,1152]{2,1,0:T(8,128)(2,1)S(1)} %all-to-all-done.2) | copy-start | bytes 1548292
  290.4 11.1 %copy-start.9 = (f32[224,3072]{1,0:T(8,128)S(1)}, f32[224,3072]{1,0:T(8,128)}, u32[]{:S(2)}) copy-start(f32[224,3072]{1,0:T(8,128)} %fusion.43) | copy-start | bytes 8257540
  290.4 11.5 %copy-start.22 = (bf16[3072,1152]{0,1:T(8,128)(2,1)S(1)}, bf16[3072,1152]{0,1:T(8,128)(2,1)}, u32[]{:S(2)}) copy-start(bf16[3072,1152]{0,1:T(8,128)(2,1)} %all-gather.5.cloned.1.call-done) | copy-start | bytes 21233668
  301.9 3.2 copy-start.3
  305.1 10.9 %all-to-all-start.1 = ((bf16[4,56,1152]{2,1,0:T(8,128)(2,1)}), bf16[4,56,1152]{2,1,0:T(8,128)(2,1)S(1)}, u32[]{:S(2)}, u32[]{:S(2)}) async-start(bf16[4,56,1152]{2,1,0:T(8,128)(2,1)} %bitcast.9), calls=%async_computation.1 | async-start | bytes 1032192 | tf_op jit(solution)/shard_map/all_to_all | solution.py:1033
  315.9 6.0 copy-start.16
  315.9 13.0 %all-to-all-start.3 = ((bf16[4,56,1152]{2,1,0:T(8,128)(2,1)}), bf16[4,56,1152]{2,1,0:T(8,128)(2,1)}, u32[]{:S(2)}, u32[]{:S(2)}) async-start(bf16[4,56,1152]{2,1,0:T(8,128)(2,1)} %bitcast.15), calls=%async_computation.3 | async-start | bytes 1032192 | tf_op jit(solution)/shard_map/all_to_all | solution.py:1055
  321.9 270.6 %reduce-scatter.4.cloned.1.call-start = ((), (), s32[]{:S(2)}) async-start(), calls=%async_computation.9 | async-start | bytes 2969600 | tf_op jit(solution)/shard_map/reduce_scatter | solution.py:1102
  331.7 2.1 copy-start.13
  464.3 48.6 %copy-start.19 = (f32[72,384]{1,0:T(8,128)S(1)}, f32[72,384]{1,0:T(8,128)}, u32[]{:S(2)}) copy-start(f32[72,384]{1,0:T(8,128)} %get-tuple-element.63) | copy-start | bytes 331780
  464.3 50.8 %copy-start.6 = (bf16[1024,384]{1,0:T(8,128)(2,1)S(1)}, bf16[1024,384]{1,0:T(8,128)(2,1)}, u32[]{:S(2)}) copy-start(bf16[1024,384]{1,0:T(8,128)(2,1)} %get-tuple-element.56.grad_gate_ref) | copy-start | bytes 2359300
  515.1 3.1 copy-start.11
  518.1 2.5 copy-start.10
  518.1 2.5 copy-start.23
  520.7 3.0 copy-start.17
  523.7 11.2 %copy-start.4 = (bf16[224,3072]{1,0:T(8,128)(2,1)S(1)}, bf16[224,3072]{1,0:T(8,128)(2,1)}, u32[]{:S(2)}) copy-start(bf16[224,3072]{1,0:T(8,128)(2,1)} %copy-done.3) | copy-start | bytes 4128772
  523.7 11.2 %copy-start.15 = (bf16[4,56,1152]{2,1,0:T(8,128)(2,1)S(1)}, bf16[4,56,1152]{2,1,0:T(8,128)(2,1)}, u32[]{:S(2)}) copy-start(bf16[4,56,1152]{2,1,0:T(8,128)(2,1)} %copy-done.14) | copy-start | bytes 1548292
  534.8 170.9 %reduce-scatter.8.cloned.1.call-start = ((), (), s32[]{:S(2)}) async-start(), calls=%async_computation.11 | async-start | bytes 7962624 | tf_op jit(solution)/shard_map/reduce_scatter | solution.py:1127
  539.9 1.0 copy-start.8
  539.9 297.5 %reduce-scatter.6.cloned.1.call-start = ((), (), s32[]{:S(2)}) async-start(), calls=%async_computation.10 | async-start | bytes 7962624 | tf_op jit(solution)/shard_map/reduce_scatter | solution.py:1124
  547.2 0.7 copy-start.20
  547.2 44.1 %copy-start.12 = (f32[128,1152]{1,0:T(8,128)S(1)}, f32[128,1152]{1,0:T(8,128)}, u32[]{:S(2)}) copy-start(f32[128,1152]{1,0:T(8,128)} %get-tuple-element.57) | copy-start | bytes 1769476
  597.3 242.5 %copy-start.1 = (bf16[4,1152]{1,0:T(4,128)(2,1)S(1)}, bf16[4,1152]{1,0:T(4,128)(2,1)}, u32[]{:S(2)}) copy-start(bf16[4,1152]{1,0:T(4,128)(2,1)} %param.33) | copy-start | bytes 27652
Sparse Core Ops, SparseCore 0:
  10.2 148.8 all-gather.2
  161.3 128.9 all-gather.4
  534.9 38.5 reduce-scatter.3
  577.6 128.1 reduce-scatter.7
  709.3 128.0 reduce-scatter.5

commit v3 on v2

--- a/solution.py
+++ b/solution.py
@@ -298,26 +298,34 @@
 
 
 class Relay:
-    def __init__(self, count, part, across, along, send_x, recv_x, send_hi, recv_hi):
-        self.line, self.own, self.high, self.low = place()
+    def __init__(self, axis, count, part, across, along, send_x, recv_x, send_hi, recv_hi):
+        self.axis = axis
+        self.own = lax.axis_index(axis)
+        self.other = lax.axis_index("dp" if axis == "seq" else "seq")
+        self.high, self.low = self.own // 2, lax.rem(self.own, 2)
         self.half = count // 2
         self.part, self.across, self.along = part, across, along
         self.send_x, self.recv_x, self.send_hi, self.recv_hi = send_x, recv_x, send_hi, recv_hi
         self.partner = 2 * self.high + 1 - self.low
 
+    def remote(self, source, target, send_sem, recv_sem, position):
+        if self.axis == "seq":
+            return remote(source, target, send_sem, recv_sem, self.other, position)
+        return remote(source, target, send_sem, recv_sem, position, self.other)
+
     def over(self, block):
         i = block // 2
-        return remote(
+        return self.remote(
             self.part.at[block], self.across.at[i], self.send_x.at[i], self.recv_x.at[i],
-            self.line, self.partner,
+            self.partner,
         )
 
     def on(self, block):
         i = block // 2
         k = lax.rem(i - self.high + self.half, self.half)
-        return remote(
+        return self.remote(
             self.part.at[block], self.along.at[k], self.send_hi.at[k], self.recv_hi.at[k],
-            self.line, 2 * i + self.low,
+            2 * i + self.low,
         )
 
     def made(self, block):
@@ -373,7 +381,7 @@
     state = cuts.state
     halves = state // 8
     step = pl.program_id(0)
-    relay = Relay(count, *relay_refs)
+    relay = Relay("seq", count, *relay_refs)
 
     @pl.when(step == 0)
     def _():
@@ -818,18 +826,24 @@
 
 
 def back_kernel(
-    count, cuts, width,
-    grad_selected_ref, small_ref, conv_w_ref, gate_w_ref, ext_ref, sum_ref, grad_act_ref, grad_gate_ref,
-    summed_ref, grad_conv_ref, grad_select_ref, rows_ref,
-    grad_sum_ref, *relay_refs,
+    count, lines, cuts,
+    grad_selected_ref, small_ref, weights_ref, ext_ref, sum_ref, grad_act_ref, grad_gate_ref,
+    mixer_low_ref, normed_ref, grad_middle_ref, grad_step_ref, rate_total_ref, scan_rows_ref,
+    vectors_ref,
+    summed_ref, shard_ref, totals_ref,
+    grad_sum_ref, grad_conv_ref, grad_small_ref, ours_ref, theirs_ref,
+    send_v, recv_v, send_u, recv_u, *relay_refs,
 ):
-    relay = Relay(count, *relay_refs)
+    relay = Relay("seq", count, *relay_refs[:7])
+    spread = Relay("dp", lines, *relay_refs[7:])
+    line, own, _, _ = place()
     length, inner = sum_ref.shape
+    width = normed_ref.shape[1]
     rows = length // count
     kernel = cuts.kernel
-    greet(count)
-    grad_select_ref[...] = jnp.zeros_like(grad_select_ref)
-    rows_ref[...] = jnp.zeros_like(rows_ref)
+    shard = shard_ref.shape[0]
+    greet(count, lines)
+    grad_small_ref[...] = jnp.zeros_like(grad_small_ref)
     grad_sum_ref[length:, :] = jnp.zeros((8, inner), jnp.float32)
     select = small_ref[: cuts.picks, :].astype(jnp.bfloat16)
 
@@ -841,13 +855,17 @@
         grad_act = grad_act_ref[pl.ds(start, rows), :] + inner_rows(grad_selected, select)
         grad_sum = grad_act * (sig * (1.0 + total * (1.0 - sig)))
         grad_sum_ref[pl.ds(start, rows), :] = grad_sum
-        grad_select_ref[...] += dot_nn(grad_selected, (total * sig).astype(jnp.bfloat16))
+        grad_small_ref[: cuts.picks, :] += dot_nn(
+            grad_selected, (total * sig).astype(jnp.bfloat16)
+        )
         window = ext_ref[pl.ds(start, rows + 8), :]
         for k in range(kernel):
-            rows_ref[k : k + 1, :] += jnp.sum(
+            row = slice(cuts.taps + k, cuts.taps + k + 1)
+            grad_small_ref[row, :] += jnp.sum(
                 grad_sum * window[9 - kernel + k : 9 - kernel + k + rows], axis=0, keepdims=True
             )
-        rows_ref[kernel : kernel + 1, :] += jnp.sum(grad_sum, axis=0, keepdims=True)
+        row = slice(cuts.conv_bias, cuts.conv_bias + 1)
+        grad_small_ref[row, :] += jnp.sum(grad_sum, axis=0, keepdims=True)
         return carry
 
     lax.fori_loop(0, count, first, 0)
@@ -867,68 +885,118 @@
         grad_conv = grad_conv.astype(jnp.bfloat16)
         grad_conv_ref[pl.ds(start, rows), :] = grad_conv
         relay.part[b] = (
-            dot_nn(grad_conv, conv_w_ref[...])
-            + dot_nn(grad_gate_ref[pl.ds(start, rows), :], gate_w_ref[...])
+            dot_nn(grad_conv, weights_ref[:, :width])
+            + dot_nn(grad_gate_ref[pl.ds(start, rows), :], weights_ref[:, width : 2 * width])
         ).astype(jnp.bfloat16)
         relay.made(b)
         return carry
 
     lax.fori_loop(0, count, second, 0)
 
-    def third(j, carry):
-        relay.pass_on(order(j))
-        return carry
-
-    lax.fori_loop(0, count, third, 0)
+    decay = slice(cuts.decay, cuts.decay + cuts.state)
+    grad_small_ref[cuts.step : cuts.step + cuts.rank, :] = grad_step_ref[...]
+    grad_small_ref[decay, :] = -rate_total_ref[...] * jnp.exp(small_ref[decay, :])
+    grad_small_ref[cuts.step_bias : cuts.step_bias + 2, :] = scan_rows_ref[0:2, :]
+    small_t = grad_small_ref[...].T
+    for d in range(lines):
+        spread.part[d, :, 3 * width :] = small_t[d * shard : (d + 1) * shard].astype(jnp.bfloat16)
+    chunk = width // 3
+    ours_ref[...] = vectors_ref[...]
+    for left_ref, right_ref, place_at in (
+        (mixer_low_ref, grad_middle_ref, 2 * width),
+        (grad_conv_ref, normed_ref, 0),
+        (grad_gate_ref, normed_ref, width),
+    ):
+
+        def columns(c, carry, left_ref=left_ref, right_ref=right_ref, place_at=place_at):
+            here = pl.ds(pl.multiple_of(c * chunk, chunk), chunk)
+            there = pl.ds(pl.multiple_of(place_at + c * chunk, chunk), chunk)
+            grad = inner_rows(left_ref[...], right_ref[:, here])
+            if place_at < 2 * width:
+                ours_ref[0:1, here] += jnp.sum(
+                    weights_ref[:, there].astype(jnp.float32) * grad, axis=0, keepdims=True
+                )
+            low = grad.astype(jnp.bfloat16)
+            for d in range(lines):
+                spread.part[d, :, there] = low[d * shard : (d + 1) * shard]
+            return carry
+
+        lax.fori_loop(0, 3, columns, 0)
+        if place_at == 2 * width:
+            lax.fori_loop(0, count, lambda j, carry: (relay.pass_on(order(j)), carry)[1], 0)
+    for d in range(lines):
+        spread.made(d)
+
+    def sum_over(size, axis, send, recv):
+        here = own if axis == "seq" else line
+
+        def copy(k, slot):
+            there = lax.rem(here + k, size)
+            target = (line, there) if axis == "seq" else (there, own)
+            return remote(ours_ref, theirs_ref.at[slot], send.at[k], recv.at[k], *target)
+
+        base = 0 if axis == "seq" else count
+        for k in range(1, size):
+            copy(k, base + k).start()
+        total = ours_ref[...]
+        for k in range(1, size):
+            copy(k, base + k).wait_recv()
+            total = total + theirs_ref[base + k]
+        for k in range(1, size):
+            copy(k, base + k).wait_send()
+        return total
+
+    ours_ref[...] = sum_over(count, "seq", send_v, recv_v)
+    for d in range(lines):
+        spread.pass_on(d)
+    totals_ref[...] = sum_over(lines, "dp", send_u, recv_u)
     summed_ref[...] = relay.finish()
-
-
-def back(count, cuts, width, grad_selected, small, weights, ext, conv_sum, grad_act, grad_gate):
+    shard_ref[...] = spread.finish()
+
+
+def back(
+    count, lines, shard, cuts, grad_selected, small, weights, ext, conv_sum, grad_act, grad_gate,
+    mixer_low, normed, grad_middle, grad_step, rate_total, scan_rows, vectors,
+):
     length, inner = conv_sum.shape
+    width = normed.shape[1]
+    columns = weights.shape[1]
     rows = length // count
-
-    def full(shape):
-        return pl.BlockSpec(shape, lambda i: (0,) * len(shape))
-
+    vmem = pl.BlockSpec(memory_space=pltpu.VMEM)
+    dma = pltpu.SemaphoreType.DMA
+    args = (
+        grad_selected, small, weights, ext, conv_sum, grad_act, grad_gate, mixer_low, normed,
+        grad_middle, grad_step, rate_total, scan_rows, vectors,
+    )
     return pl.pallas_call(
-        functools.partial(back_kernel, count, cuts, width),
-        grid=(1,),
-        in_specs=[
-            full(grad_selected.shape),
-            full(small.shape),
-            pl.BlockSpec((inner, width), lambda i: (0, 0)),
-            pl.BlockSpec((inner, width), lambda i: (0, 1)),
-            full(ext.shape),
-            full(conv_sum.shape),
-            full(grad_act.shape),
-            full(grad_gate.shape),
-        ],
-        out_specs=[
-            full((rows, width)),
-            full((length, inner)),
-            full((cuts.picks, inner)),
-            full((8, inner)),
-        ],
+        functools.partial(back_kernel, count, lines, cuts),
+        in_specs=[vmem] * len(args),
+        out_specs=[vmem] * 3,
         out_shape=[
             jax.ShapeDtypeStruct((rows, width), jnp.float32),
-            jax.ShapeDtypeStruct((length, inner), jnp.bfloat16),
-            jax.ShapeDtypeStruct((cuts.picks, inner), jnp.float32),
-            jax.ShapeDtypeStruct((8, inner), jnp.float32),
+            jax.ShapeDtypeStruct((shard, columns), jnp.float32),
+            jax.ShapeDtypeStruct(vectors.shape, jnp.float32),
         ],
         scratch_shapes=[
             pltpu.VMEM((length + 8, inner), jnp.float32),
+            pltpu.VMEM((length, inner), jnp.bfloat16),
+            pltpu.VMEM(small.shape, jnp.float32),
+            pltpu.VMEM(vectors.shape, jnp.float32),
+            pltpu.VMEM((count + lines, *vectors.shape), jnp.float32),
+            dma((count,)), dma((count,)), dma((lines,)), dma((lines,)),
             *Relay.scratch(count, rows, width),
+            *Relay.scratch(lines, shard, columns),
         ],
         compiler_params=pltpu.CompilerParams(
             collective_id=3, has_side_effects=True, vmem_limit_bytes=VMEM_LIMIT
         ),
         cost_estimate=pl.CostEstimate(
-            flops=4 * length * width * inner,
-            bytes_accessed=20 * length * inner,
+            flops=10 * length * width * inner,
+            bytes_accessed=30 * length * inner,
             transcendentals=length * inner,
         ),
         name="back",
-    )(grad_selected, small, weights, weights, ext, conv_sum, grad_act, grad_gate)
+    )(*args)
 
 
 def body(
@@ -1069,39 +1137,37 @@
     grad_middle = grad_out + grad_middle_norm
     grad_middle_low = grad_middle.astype(jnp.bfloat16)
 
+    grad_middle_low, grad_up_low, grad_down_low = lax.optimization_barrier(
+        (grad_middle_low, grad_up_w.astype(jnp.bfloat16), grad_down_w.astype(jnp.bfloat16))
+    )
+    expert_grads = (
+        lax.psum_scatter(grad_up_low, "seq", scatter_dimension=0, tiled=True).astype(jnp.float32),
+        lax.psum_scatter(grad_down_low, "seq", scatter_dimension=1, tiled=True).astype(
+            jnp.float32
+        ),
+    )
+
     (grad_gate_branch, grad_act, grad_step_w, rate_total, scan_rows, grad_selected, grad_middle_all) = (
         scan_backward(
             count, cuts, grad_middle_low, conv_act, gate_branch, mixed, pre, selected, small_all,
             weights, priors, end,
         )
     )
-    grad_normed, grad_conv_input, grad_select_w, conv_rows = back(
-        count, cuts, width, grad_selected, small_all, weights, conv_ext, conv_sum, grad_act,
-        grad_gate_branch,
-    )
-    grad_decay = rate_total * -jnp.exp(small_all[cuts.decay : cuts.decay + state])
-    normed_rows = normed_all.reshape(-1, width)
-    grad_output_w = inner_rows(mixer_low, grad_middle_all.reshape(-1, width))
-    grad_conv_w = inner_rows(grad_conv_input, normed_rows)
-    grad_gate_w = inner_rows(grad_gate_branch, normed_rows)
-    grad_small = jnp.concatenate(
+    vectors = jnp.concatenate(
         [
-            grad_select_w,
-            grad_step_w,
-            grad_decay,
-            conv_rows[: kernel + 1],
-            scan_rows[:2],
-            jnp.zeros((small_pad - cuts.rows, grad_decay.shape[1]), jnp.float32),
+            jnp.zeros((1, width), jnp.float32),
+            grad_gain_two[None],
+            grad_router,
+            jnp.zeros((6 - experts, width), jnp.float32),
         ],
         axis=0,
     )
-    grad_packed = jnp.concatenate(
-        [part.astype(jnp.bfloat16) for part in (grad_conv_w, grad_gate_w, grad_output_w, grad_small.T)],
-        axis=1,
-    )
-    grad_shard = lax.psum_scatter(
-        grad_packed[: lines * shard_rows], "dp", scatter_dimension=0, tiled=True
-    )[:shard].astype(jnp.float32)
+    grad_normed, grad_shard, totals = back(
+        count, lines, shard_rows, cuts, grad_selected, small_all, weights, conv_ext, conv_sum,
+        grad_act, grad_gate_branch, mixer_low, normed_all.reshape(-1, width),
+        grad_middle_all.reshape(-1, width), grad_step_w, rate_total, scan_rows, vectors,
+    )
+    grad_shard = grad_shard[:shard]
     grad_input_w = grad_shard[:, : 2 * width].T.reshape(2, width, shard)
     small_shard = grad_shard[:, 3 * width :].T
     cut = 0
@@ -1109,33 +1175,12 @@
     for number in (picks, rank, state, kernel, 1, 1, 1):
         small_grads.append(small_shard[cut : cut + number])
         cut += number
-
-    grad_gain_one = (
-        jnp.sum(
-            weights[:, :width].astype(jnp.float32) * grad_conv_w
-            + weights[:, width : 2 * width].astype(jnp.float32) * grad_gate_w,
-            axis=0,
-        )
-        / gain_one
-    )
     unused_one, pull_one = jax.vjp(lambda v: rms_norm(v, gain_one), x_in)
     grad_tokens = grad_middle + pull_one(grad_normed)[0]
-    expert_grads = (
-        lax.psum_scatter(
-            grad_up_w.astype(jnp.bfloat16), "seq", scatter_dimension=0, tiled=True
-        ).astype(jnp.float32),
-        lax.psum_scatter(
-            grad_down_w.astype(jnp.bfloat16), "seq", scatter_dimension=1, tiled=True
-        ).astype(jnp.float32),
-    )
-    small_sums = lax.psum(
-        jnp.concatenate([grad_gain_one[None], grad_gain_two[None], grad_router], axis=0),
-        ("dp", "seq"),
-    )
     return (
         output.reshape(tokens.shape),
         grad_tokens.reshape(tokens.shape),
-        small_sums[0],
+        totals[0] / gain_one,
         grad_input_w,
         small_grads[3],
         small_grads[4].reshape(shard),
@@ -1145,8 +1190,8 @@
         small_grads[2],
         small_grads[6].reshape(shard),
         grad_shard[:, 2 * width : 3 * width],
-        small_sums[1],
-        small_sums[2:],
+        totals[1],
+        totals[2 : 2 + experts],
         expert_grads[0],
         expert_grads[1],
     )

time: 851 us -> 717 us (0.84)
  waiting for transfers between devices: 279 us -> 86.1 us
  Pallas kernels: 386 us -> 500 us
  blocking collectives: 41.9 us -> 0 us
  other arithmetic: 30.9 us -> 15.8 us
  local copies, waits for them, and re-layouts: 20.8 us -> 34.7 us
  matrix products: 50.7 us -> 41 us
    reduce_scatter x3 -> x1, waiting for transfers between devices: 236 us -> 42 us  [body(): lax.psum_scatter(grad_up_low, 'seq', scatter_dimension=0, tiled=True)]
    pallas_call x1, Pallas kernels: 47.9 us -> 116 us  [back(): pl.pallas_call(functools.partial(back_kernel, count, lines, cuts), in_spe...]
    pallas_call x1, Pallas kernels: 127 us -> 173 us  [scan_backward(): pl.pallas_call(functools.partial(scan_backward_kernel, count, cuts), grid...]
    psum x1 -> x0, blocking collectives: 41.9 us -> none  [body(): lax.psum(jnp.concatenate([grad_gain_one[None], grad_gain_two[None], grad_...]
    unnamed x54 -> x35, local copies, waits for them, and re-layouts: 6.11 us -> 17.9 us
    concatenate x2 -> x1, other arithmetic: 11.1 us -> 0.7 us  [body(): jnp.concatenate([jnp.zeros((1, width), jnp.float32), grad_gain_two[None],...]
    dot_general x6 -> x3, matrix products: 20.1 us -> 10.3 us  [inner_rows(): lax.dot_general(left, right, (((0,), (0,)), ((), ())), precision=precisio...]
  transfers between devices with their start and end apart: 9 -> 8, of which waited for: 7 -> 5; matrix products, arithmetic and copies ran while one was open for 6% -> 7% of each run, Pallas kernels for 25% -> 70%
where the time goes in v3:
time: 717 us; the launch traced here: 712 us
  Pallas kernels  500 us (70%)
  waiting for transfers between devices  86.1 us (12%)
  matrix products  41 us (6%)
  local copies, waits for them, and re-layouts  34.7 us (5%)
  starting transfers between devices  20.2 us (3%)
  other arithmetic  15.8 us (2%)
  between operations  14 us (2%)
    pallas_call x1, Pallas kernels, scan_backward(): pl.pallas_call(functools.partial(scan_backward_kernel, count, cuts), grid...  173 us
    pallas_call x1, Pallas kernels, front(): pl.pallas_call(functools.partial(front_kernel, count, lines, cuts), in_sp...  125 us
    pallas_call x1, Pallas kernels, back(): pl.pallas_call(functools.partial(back_kernel, count, lines, cuts), in_spe...  116 us
    pallas_call x1, Pallas kernels, scan_forward(): pl.pallas_call(functools.partial(scan_forward_kernel, count, cuts), grid=...  86.9 us
    reduce_scatter x1, waiting for transfers between devices, body(): lax.psum_scatter(grad_up_low, 'seq', scatter_dimension=0, tiled=True)  42 us
    all_gather x1, waiting for transfers between devices, body(): lax.all_gather(expert_down, 'seq', axis=1, tiled=True)  32.2 us
    unnamed x35, local copies, waits for them, and re-layouts  17.9 us
    dot_general x3, matrix products, outer_cols(): lax.dot_general(left, right, (((1,), (1,)), ((), ())), precision=precisio...  17.9 us
  transfers between devices with their start and end apart: 8, of which 5 were waited for; matrix products, arithmetic and copies ran while one was open for 7% of the time, Pallas kernels for 70%

profile of v3, /device:TPU:31, one launch (start us, length us, event | category | flops | bytes accessed | tf_op | source)
XLA Modules:
  0.0 712.1 jit_solution(11069458498685751531)
XLA Ops:
  10.1 0.8 copy.60
  10.9 0.8 copy.61
  11.6 0.8 copy.58
  12.4 0.8 copy.62
  13.2 0.8 copy.59
  14.0 0.8 copy.63
  14.8 1.0 copy.72
  15.8 0.8 concatenate.9
  16.8 0.9 fusion.11.packed_ref
  17.6 0.8 fusion.19.normed_ref
  18.5 124.6 %front.1 = (bf16[8,128,1152]{2,1,0:T(8,128)(2,1)}, bf16[384,3712]{1,0:T(8,128)(2,1)}, f32[256,384]{1,0:T(8,128)}, f32[1032,384]{1,0:T(8,128)}, f32[1024,384]{1,0...) custom-call(bf16[128,1152]{1,0:T(8,128)(2,1)} %fusion.19.normed_ref, ...), custom_call_target="tpu_custom_call" | custom-call | flops 1811939328 | bytes 7864320 | tf_op jit(solution)/shard_map/front/pallas_call | solution.py:268
  143.1 86.9 %scan_forward.1 = (f32[1024,384]{1,0:T(8,128)}, f32[1024,384]{1,0:T(8,128)}, bf16[1024,384]{1,0:T(8,128)(2,1)}, f32[1024,16,384]{2,1,0:T(8,128)}, f32[16,384]{1,0:T(8,128)}, /*index=5*/f32[128,1152]{1,0:T(8,128)}) custom-call(f32[1024,384]{1,0:T(8,128)} %get-tuple-element.44.act_ref, f32[1024,384]{1,0:T(8,128)} %get-tuple-element.45.gate_ref, ...), custom_call_target="tpu_custom_call" | custom-call | flops 50331648 | bytes 34603008 | tf_op jit(solution)/shard_map/scan_forward/pallas_call | solution.py:474
  230.2 1.5 multiply_reduce_fusion.2
  231.8 1.1 convolution_convert_fusion.5
  232.9 6.5 all-to-all-start
  239.7 1.1 convolution_convert_fusion.4
  240.9 5.5 all-to-all-done
  246.4 5.2 all-to-all-start.2
  251.6 6.6 fusion.42
  258.5 32.2 %all-gather.5.cloned.1.call-done = bf16[3072,1152]{0,1:T(8,128)(2,1)} async-done(((bf16[3072,144]{0,1:T(8,128)(2,1)}), bf16[3072,1152]{0,1:T(8,128)(2,1)}) %all-gather.5.cloned.1.call-update) | async-done | bytes 7077904 | tf_op jit(solution)/shard_map/all_gather | solution.py:1057
  290.7 11.1 %add_convert_fusion = (bf16[224,3072]{1,0:T(8,128)(2,1)}, f32[224,3072]{1,0:T(8,128)S(1)}) fusion(f32[224,3072]{1,0:T(8,128)} %fusion.42, bf16[224,1152]{1,0:T(8,128)(2,1)S(1)} %bitcast.88, bf16[3072,1152]{0,1:T(8,128)(2,1)} %all-gather.5.cloned.1.call-done), kind=kOutput, calls=%fused_computation.6 | convolution fusion | flops 1634992128 | bytes 14475264 | tf_op jit(solution)/shard_map/dot_general | solution.py:38
  302.2 5.1 convolution_convert_fusion
  307.3 3.1 convolution_convert_fusion.3
  310.4 4.0 all-to-all-start.1
  314.4 6.7 convolution_convert_fusion.2
  321.1 5.0 convolution_convert_fusion.1
  326.1 4.4 all-to-all-start.3
  330.5 1.1 bitcast_convert_fusion.1
  331.6 1.7 gather_fusion
  333.2 4.2 all-to-all-done.3
  337.4 1.1 bitcast_convert_fusion
  338.5 1.7 gather_fusion.1
  340.2 2.1 fusion.16
  343.0 0.9 fusion.37
  344.0 10.3 %copy.69 = bf16[3072,1152]{0,1:T(8,128)(2,1)} copy(bf16[3072,1152]{1,0:T(8,128)(2,1)} %convolution_convert_fusion) | data formatting | bytes 14155776
  355.0 172.8 %scan_backward.1 = (bf16[1024,384]{1,0:T(8,128)(2,1)}, f32[1024,384]{1,0:T(8,128)}, f32[72,384]{1,0:T(8,128)}, f32[16,384]{1,0:T(8,128)}, f32[8,384]{1,0:T(8,128...) custom-call(bf16[128,1152]{1,0:T(8,128)(2,1)} %get-tuple-element.50.own_ref, ...), custom_call_target="tpu_custom_call" | custom-call | flops 125829120 | bytes 34603008 | tf_op jit(solution)/shard_map/scan_backward/pallas_call | solution.py:770
  528.7 116.1 %back.1 = (f32[128,1152]{1,0:T(8,128)}, f32[80,3712]{1,0:T(8,128)}, f32[8,1152]{1,0:T(8,128)}) custom-call(f32[8,104,128]{2,1,0:T(8,128)} %get-tuple-element.55.grad_selected_ref, f32[256,384]{1,0:T(8,128)} %get-tuple-element.47.small_ref, bf16[384,3712]{1,0:T(8,128)(2,1)} %get-tuple-element.48.output_ref.weights_ref, ...), custom_call_target="tpu_custom_call" | custom-call | flops 4529848320 | bytes 11796480 | tf_op jit(solution)/shard_map/back/pallas_call | solution.py:971
  644.8 1.0 slice_bitcast_fusion
  646.6 1.7 slice.53
  648.3 1.2 slice.44
  649.5 1.4 slice.55
  652.9 0.9 copy.74
  653.8 1.5 slice_reduce_fusion.3
  656.8 1.0 fusion.14
  657.8 1.6 copy.70
  659.4 1.6 copy.68
  661.0 42.0 %reduce-scatter.5.cloned.1.call-done = bf16[144,3072]{1,0:T(8,128)(2,1)} async-done(((bf16[1152,3072]{1,0:T(8,128)(2,1)}), bf16[144,3072]{1,0:T(8,128)(2,1)}) %reduce-scatter.5.cloned.1.call-update) | async-done | bytes 884752 | tf_op jit(solution)/shard_map/reduce_scatter | solution.py:1144
  703.0 2.6 convert_element_type.92
  (73 shorter events, 11.1 us)
Async XLA Ops:
  7.2 232.2 %copy-start = (bf16[4,1152]{1,0:T(4,128)(2,1)S(1)}, bf16[4,1152]{1,0:T(4,128)(2,1)}, u32[]{:S(2)}) copy-start(bf16[4,1152]{1,0:T(4,128)(2,1)} %param.33) | copy-start | bytes 27652
  7.2 9.4 %copy-start.1 = (f32[1,128,1152]{2,1,0:T(8,128)S(1)}, f32[1,128,1152]{2,1,0:T(8,128)}, u32[]{:S(2)}) copy-start(f32[1,128,1152]{2,1,0:T(8,128)} %param.19) | copy-start | bytes 1769476
  7.2 9.6 %copy-start.8 = (bf16[72,1152]{1,0:T(8,128)(2,1)S(1)}, bf16[72,1152]{1,0:T(8,128)(2,1)}, u32[]{:S(2)}) copy-start(bf16[72,1152]{1,0:T(8,128)(2,1)} %param.31) | copy-start | bytes 497668
  7.2 244.4 %all-gather.3.cloned.1.call-start = ((), (), s32[]{:S(2)}) async-start(), calls=%async_computation.6 | async-start | bytes 7962624 | tf_op jit(solution)/shard_map/all_gather | solution.py:1056
  8.0 282.7 %all-gather.5.cloned.1.call-start = ((), (), s32[]{:S(2)}) async-start(), calls=%async_computation.7 | async-start | bytes 7962624 | tf_op jit(solution)/shard_map/all_gather | solution.py:1057
  143.1 87.0 %copy-start.10 = (s32[1,128,1]{1,2,0:T(1,128)S(1)}, s32[1,128,1]{1,2,0:T(1,128)}, u32[]{:S(2)}) copy-start(s32[1,128,1]{1,2,0:T(1,128)} %param.21) | copy-start | bytes 1540
  230.0 9.7 %copy-start.2 = (f32[1,128,1152]{2,1,0:T(8,128)S(1)}, f32[1,128,1152]{2,1,0:T(8,128)}, u32[]{:S(2)}) copy-start(f32[1,128,1152]{2,1,0:T(8,128)} %param.20) | copy-start | bytes 1769476
  232.9 13.4 %all-to-all-start = ((bf16[4,56,1152]{2,1,0:T(8,128)(2,1)}), bf16[4,56,1152]{2,1,0:T(8,128)(2,1)S(1)}, u32[]{:S(2)}, u32[]{:S(2)}) async-start(bf16[4,56,1152]{2,1,0:T(8,128)(2,1)} %bitcast.7), calls=%async_computation | async-start | bytes 1032192 | tf_op jit(solution)/shard_map/all_to_all | solution.py:1092
  246.4 12.1 %all-to-all-start.2 = ((bf16[4,56,1152]{2,1,0:T(8,128)(2,1)}), bf16[4,56,1152]{2,1,0:T(8,128)(2,1)S(1)}, u32[]{:S(2)}, u32[]{:S(2)}) async-start(bf16[4,56,1152]{2,1,0:T(8,128)(2,1)} %bitcast.90), calls=%async_computation.2 | async-start | bytes 1032192 | tf_op jit(solution)/shard_map/all_to_all | solution.py:1116
  290.7 11.1 %copy-start.3 = (f32[224,3072]{1,0:T(8,128)S(1)}, f32[224,3072]{1,0:T(8,128)}, u32[]{:S(2)}) copy-start(f32[224,3072]{1,0:T(8,128)} %fusion.42) | copy-start | bytes 8257540
  301.7 5.5 slice-start
  302.2 5.1 slice-start.1
  310.4 15.7 %all-to-all-start.1 = ((bf16[4,56,1152]{2,1,0:T(8,128)(2,1)}), bf16[4,56,1152]{2,1,0:T(8,128)(2,1)S(1)}, u32[]{:S(2)}, u32[]{:S(2)}) async-start(bf16[4,56,1152]{2,1,0:T(8,128)(2,1)} %bitcast.95), calls=%async_computation.1 | async-start | bytes 1032192 | tf_op jit(solution)/shard_map/all_to_all | solution.py:1101
  314.4 6.7 copy-start.7
  326.1 4.4 copy-start.6
  326.1 11.3 %all-to-all-start.3 = ((bf16[4,56,1152]{2,1,0:T(8,128)(2,1)}), bf16[4,56,1152]{2,1,0:T(8,128)(2,1)}, u32[]{:S(2)}, u32[]{:S(2)}) async-start(bf16[4,56,1152]{2,1,0:T(8,128)(2,1)} %bitcast.94), calls=%async_computation.3 | async-start | bytes 1032192 | tf_op jit(solution)/shard_map/all_to_all | solution.py:1123
  330.5 327.3 %reduce-scatter.7.cloned.1.call-start = ((), (), s32[]{:S(2)}) async-start(), calls=%async_computation.9 | async-start | bytes 7962624
  340.2 2.1 copy-start.5
  354.3 348.7 %reduce-scatter.5.cloned.1.call-start = ((), (), s32[]{:S(2)}) async-start(), calls=%async_computation.8 | async-start | bytes 7962624 | tf_op jit(solution)/shard_map/reduce_scatter | solution.py:1144
  644.8 11.2 %copy-start.4 = (f32[128,1152]{1,0:T(8,128)S(1)}, f32[128,1152]{1,0:T(8,128)}, u32[]{:S(2)}) copy-start(f32[128,1152]{1,0:T(8,128)} %get-tuple-element.66) | copy-start | bytes 1769476
  644.8 11.4 %copy-start.9 = (bf16[1152]{0:T(1024)(128)(2,1)S(1)}, bf16[1152]{0:T(1024)(128)(2,1)}, u32[]{:S(2)}) copy-start(bf16[1152]{0:T(1024)(128)(2,1)} %param.22) | copy-start | bytes 6916
Sparse Core Ops, SparseCore 0:
  10.2 148.9 all-gather.2
  161.5 129.1 all-gather.4
  354.4 178.3 reduce-scatter.6
  536.8 166.1 reduce-scatter.4

commit v4 on v3

--- a/solution.py
+++ b/solution.py
@@ -18,10 +18,6 @@
 
 def rms_norm(values, gain):
     return values * lax.rsqrt(jnp.mean(values * values, axis=-1, keepdims=True) + 1e-05) * gain
-
-
-def gelu_exact(values):
-    return jax.nn.gelu(values, approximate=False)
 
 
 def inner_rows(left, right, precision=None):
@@ -68,7 +64,7 @@
 
 
 MESH = pl.DeviceIdType.MESH
-VMEM_LIMIT = 56 * 1024 * 1024
+VMEM_LIMIT = 60 * 1024 * 1024
 
 
 def dot_nn(left, right, precision=None):
@@ -128,15 +124,247 @@
         self.rows = self.skip + 1
 
 
+class Relay:
+    def __init__(self, axis, half, high, low, seat, block, refs):
+        self.axis, self.half, self.high, self.low = axis, half, high, low
+        self.seat, self.block = seat, block
+        self.other = lax.axis_index("dp" if axis == "seq" else "seq")
+        self.part, self.across, self.along = refs[:3]
+        self.send_x, self.recv_x, self.send_hi, self.recv_hi = refs[3:]
+
+    def remote(self, source, target, send_sem, recv_sem, position):
+        if self.axis == "seq":
+            return remote(source, target, send_sem, recv_sem, self.other, position)
+        return remote(source, target, send_sem, recv_sem, position, self.other)
+
+    def over(self, i, low):
+        return self.remote(
+            self.part.at[self.block(i, low)], self.across.at[i], self.send_x.at[i],
+            self.recv_x.at[i], self.seat(self.high, 1 - self.low),
+        )
+
+    def on(self, i):
+        k = lax.rem(i - self.high + self.half, self.half)
+        return self.remote(
+            self.across.at[i], self.along.at[k], self.send_hi.at[k], self.recv_hi.at[k],
+            self.seat(i, self.low),
+        )
+
+    def made(self, i, low):
+        @pl.when(low != self.low)
+        def _():
+            self.over(i, low).start()
+
+    def summed(self, i):
+        self.over(i, self.low).wait_recv()
+        return self.part[self.block(i, self.low)].astype(jnp.float32) + self.across[i].astype(
+            jnp.float32
+        )
+
+    def pass_on(self, i, low):
+        @pl.when((low == self.low) & (i != self.high))
+        def _():
+            self.across[i] = self.summed(i).astype(jnp.bfloat16)
+            self.on(i).start()
+
+    def finish(self):
+        total = self.summed(self.high)
+        for k in range(1, self.half):
+            self.on(lax.rem(self.high + k, self.half)).wait_recv()
+            total = total + self.along[k].astype(jnp.float32)
+        for i in range(self.half):
+            self.over(i, 1 - self.low).wait_send()
+        for k in range(1, self.half):
+            self.on(lax.rem(self.high + k, self.half)).wait_send()
+        return total
+
+
+def whole_relay(axis, count, refs):
+    own = lax.axis_index(axis)
+
+    def seat(i, low):
+        return 2 * i + low
+
+    return Relay(axis, count // 2, own // 2, lax.rem(own, 2), seat, seat, refs)
+
+
+def relay_scratch(count, rows, width, part=True):
+    half = count // 2
+    dma = pltpu.SemaphoreType.DMA
+    own = [pltpu.VMEM((count, rows, width), jnp.bfloat16)] if part else []
+    return own + [
+        pltpu.VMEM((half, rows, width), jnp.bfloat16),
+        pltpu.VMEM((half, rows, width), jnp.bfloat16),
+        dma((half,)), dma((half,)), dma((half,)), dma((half,)),
+    ]
+
+
+def square():
+    own = lax.axis_index("seq")
+    return own // 4, lax.rem(own // 2, 2), lax.rem(own, 2)
+
+
+def seat_of(q, f, low):
+    return 4 * q + 2 * f + low
+
+
+class Gather:
+    def __init__(self, count, shard_ref, land_ref, swap_s, swap_r, line_s, line_r, pair_s, pair_r):
+        self.line = lax.axis_index("dp")
+        self.q, self.f, self.low = square()
+        self.quarter = count // 4
+        self.shard, self.land = shard_ref, land_ref
+        self.swap_s, self.swap_r = swap_s, swap_r
+        self.line_s, self.line_r, self.pair_s, self.pair_r = line_s, line_r, pair_s, pair_r
+        self.cut = land_ref.shape[2]
+
+    def columns(self, f):
+        return pl.ds(pl.multiple_of(f * self.cut, LANES), self.cut)
+
+    def piece(self, j, k, low):
+        q = lax.rem(self.q - k + self.quarter, self.quarter)
+        return seat_of(q, lax.rem(self.f + j, 2), low)
+
+    def swap(self):
+        own = self.piece(0, 0, self.low)
+        return remote(
+            self.shard.at[:, self.columns(1 - self.f)], self.land.at[own], self.swap_s, self.swap_r,
+            self.line, self.piece(1, 0, self.low),
+        )
+
+    def along(self, j, k):
+        piece = self.piece(j, 0, self.low)
+        there = seat_of(lax.rem(self.q + k, self.quarter), self.f, self.low)
+        return remote(
+            self.land.at[piece], self.land.at[piece], self.line_s.at[j, k], self.line_r.at[j, k],
+            self.line, there,
+        )
+
+    def pair(self, j, k, low):
+        piece = self.piece(j, k, low)
+        return remote(
+            self.land.at[piece], self.land.at[piece], self.pair_s.at[j, k], self.pair_r.at[j, k],
+            self.line, seat_of(self.q, self.f, 1 - self.low),
+        )
+
+    def start(self):
+        self.swap().start()
+        self.land[self.piece(0, 0, self.low)] = self.shard[:, self.columns(self.f)]
+
+    def spread(self, j):
+        if j == 1:
+            mate = self.piece(1, 0, self.low)
+            remote(
+                self.land.at[mate], self.land.at[mate], self.swap_s, self.swap_r, self.line, mate
+            ).wait_recv()
+        for k in range(1, self.quarter):
+            self.along(j, k).start()
+        self.pair(j, 0, self.low).start()
+
+    def forward(self):
+        for j in range(2):
+            for k in range(1, self.quarter):
+                piece = self.piece(j, k, self.low)
+                remote(
+                    self.land.at[piece], self.land.at[piece], self.line_s.at[j, k],
+                    self.line_r.at[j, k], self.line, piece,
+                ).wait_recv()
+                self.pair(j, k, self.low).start()
+
+    def finish(self):
+        for j in range(2):
+            for k in range(self.quarter):
+                self.pair(j, k, 1 - self.low).wait_recv()
+        self.swap().wait_send()
+        for j in range(2):
+            for k in range(1, self.quarter):
+                self.along(j, k).wait_send()
+            for k in range(self.quarter):
+                self.pair(j, k, self.low).wait_send()
+
+
+def gather_scratch(count):
+    dma = pltpu.SemaphoreType.DMA
+    quarter = count // 4
+    return [dma, dma] + [dma((2, quarter)) for _ in range(4)]
+
+
+class Scatter:
+    def __init__(self, count, part_ref, other_ref, held_ref, swap_s, swap_r, refs):
+        self.line = lax.axis_index("dp")
+        self.q, self.f, self.low = square()
+        self.quarter = count // 4
+        self.other, self.held = other_ref, held_ref
+        self.swap_s, self.swap_r = swap_s, swap_r
+        self.relays = []
+        for j in range(2):
+            cut = lax.rem(self.f + j, 2)
+
+            def seat(i, low):
+                return seat_of(i, self.f, low)
+
+            def block(i, low, cut=cut):
+                return seat_of(i, cut, low)
+
+            mine = tuple(ref.at[j] for ref in refs)
+            self.relays.append(
+                Relay("seq", self.quarter, self.q, self.low, seat, block, (part_ref, *mine))
+            )
+
+    def swap(self):
+        return remote(
+            self.held, self.other, self.swap_s, self.swap_r, self.line,
+            seat_of(self.q, 1 - self.f, self.low),
+        )
+
+    def start(self):
+        for j in (1, 0):
+            for i in range(self.quarter):
+                self.relays[j].over(i, 1 - self.low).start()
+
+    def pass_on(self):
+        for j in (1, 0):
+            for k in range(1, self.quarter):
+                self.relays[j].pass_on(lax.rem(self.q + k, self.quarter), self.low)
+
+    def hand_over(self):
+        self.held[...] = self.relays[1].finish().astype(jnp.bfloat16)
+        self.swap().start()
+
+    def finish(self, out_ref):
+        cut = self.held.shape[1]
+        out_ref[:, pl.ds(pl.multiple_of(self.f * cut, LANES), cut)] = self.relays[0].finish()
+        self.swap().wait_recv()
+        out_ref[:, pl.ds(pl.multiple_of((1 - self.f) * cut, LANES), cut)] = self.other[...].astype(
+            jnp.float32
+        )
+        self.swap().wait_send()
+
+
+def scatter_scratch(count, rows, cut):
+    dma = pltpu.SemaphoreType.DMA
+    quarter = count // 4
+    return [
+        pltpu.VMEM((rows, cut), jnp.bfloat16),
+        pltpu.VMEM((rows, cut), jnp.bfloat16),
+        dma, dma,
+        pltpu.VMEM((2, quarter, rows, cut), jnp.bfloat16),
+        pltpu.VMEM((2, quarter, rows, cut), jnp.bfloat16),
+        *[dma((2, quarter)) for _ in range(4)],
+    ]
+
+
 def front_kernel(
     count, lines, cuts,
-    normed_ref, packed_ref,
-    all_ref, weights_ref, small_ref, ext_ref, sum_ref, act_ref, gate_ref, selected_ref,
+    normed_ref, packed_ref, expert_ref,
+    all_ref, weights_ref, small_ref, ext_ref, sum_ref, act_ref, gate_ref, selected_ref, land_ref,
     part_ref, partial_ref,
     send_w, recv_w, send_hi, recv_hi, send_x, recv_x, send_rs, recv_rs, send_ag, recv_ag,
+    *gather_refs,
 ):
     line, own, high, low = place()
     half = count // 2
+    gather = Gather(count, expert_ref, land_ref, *gather_refs)
     rows, width = normed_ref.shape
     shard = packed_ref.shape[0]
     inner = weights_ref.shape[0]
@@ -163,6 +391,7 @@
         )
         copy.start()
         copies.append(copy)
+    gather.start()
     all_ref[own] = normed_ref[...]
     weights_ref[shard_rows, :] = packed_ref[...]
     if lines * shard < inner:
@@ -180,6 +409,8 @@
         )
         copy.start()
         copies.append(copy)
+    gather.spread(0)
+    gather.spread(1)
     for k in range(1, lines):
         from_line = lax.rem(line - k + lines, lines)
         there = pl.ds(pl.multiple_of(from_line * shard, 16), shard)
@@ -221,6 +452,7 @@
 
     lax.fori_loop(0, count, convolve, 0)
 
+    gather.forward()
     for k in range(1, count):
         there = lax.rem(own + k, count)
         copy = remote(
@@ -250,9 +482,10 @@
         ).wait_recv()
     for copy in copies:
         copy.wait_send()
-
-
-def front(count, lines, cuts, normed, packed):
+    gather.finish()
+
+
+def front(count, lines, cuts, normed, packed, expert):
     rows, width = normed.shape
     shard, columns = packed.shape
     inner = -(-lines * shard // LANES) * LANES
@@ -267,8 +500,8 @@
     dma = pltpu.SemaphoreType.DMA
     return pl.pallas_call(
         functools.partial(front_kernel, count, lines, cuts),
-        in_specs=[vmem] * 2,
-        out_specs=[vmem] * 8,
+        in_specs=[vmem] * 3,
+        out_specs=[vmem] * 9,
         out_shape=[
             jax.ShapeDtypeStruct((count, rows, width), jnp.bfloat16),
             jax.ShapeDtypeStruct((inner, columns), jnp.bfloat16),
@@ -278,12 +511,14 @@
             f32(length, inner),
             f32(length, inner),
             f32(count, cuts.picks, rows),
+            jax.ShapeDtypeStruct((count, expert.shape[0], expert.shape[1] // 2), jnp.bfloat16),
         ],
         scratch_shapes=[
             pltpu.VMEM((count, cuts.picks, rows), jnp.float32),
             pltpu.VMEM((count, cuts.picks, rows), jnp.float32),
             dma((lines,)), dma((lines,)), dma((half,)), dma((half,)), dma((half,)), dma((half,)),
             dma((count,)), dma((count,)), dma((count,)), dma((count,)),
+            *gather_scratch(count),
         ],
         compiler_params=pltpu.CompilerParams(
             collective_id=0, has_side_effects=True, vmem_limit_bytes=VMEM_LIMIT
@@ -294,99 +529,37 @@
             transcendentals=length * inner,
         ),
         name="front",
-    )(normed, packed)
-
-
-class Relay:
-    def __init__(self, axis, count, part, across, along, send_x, recv_x, send_hi, recv_hi):
-        self.axis = axis
-        self.own = lax.axis_index(axis)
-        self.other = lax.axis_index("dp" if axis == "seq" else "seq")
-        self.high, self.low = self.own // 2, lax.rem(self.own, 2)
-        self.half = count // 2
-        self.part, self.across, self.along = part, across, along
-        self.send_x, self.recv_x, self.send_hi, self.recv_hi = send_x, recv_x, send_hi, recv_hi
-        self.partner = 2 * self.high + 1 - self.low
-
-    def remote(self, source, target, send_sem, recv_sem, position):
-        if self.axis == "seq":
-            return remote(source, target, send_sem, recv_sem, self.other, position)
-        return remote(source, target, send_sem, recv_sem, position, self.other)
-
-    def over(self, block):
-        i = block // 2
-        return self.remote(
-            self.part.at[block], self.across.at[i], self.send_x.at[i], self.recv_x.at[i],
-            self.partner,
-        )
-
-    def on(self, block):
-        i = block // 2
-        k = lax.rem(i - self.high + self.half, self.half)
-        return self.remote(
-            self.part.at[block], self.along.at[k], self.send_hi.at[k], self.recv_hi.at[k],
-            2 * i + self.low,
-        )
-
-    def made(self, block):
-        @pl.when(lax.rem(block, 2) != self.low)
-        def _():
-            self.over(block).start()
-
-    def pass_on(self, block):
-        @pl.when((lax.rem(block, 2) == self.low) & (block // 2 != self.high))
-        def _():
-            self.over(block).wait_recv()
-            both = self.part[block].astype(jnp.float32) + self.across[block // 2].astype(
-                jnp.float32
-            )
-            self.part[block] = both.astype(jnp.bfloat16)
-            self.on(block).start()
-
-    def finish(self):
-        self.over(self.own).wait_recv()
-        total = self.part[self.own].astype(jnp.float32) + self.across[self.high].astype(
-            jnp.float32
-        )
-        for k in range(1, self.half):
-            block = 2 * lax.rem(self.high + k, self.half) + self.low
-            self.on(block).wait_recv()
-            total = total + self.along[k].astype(jnp.float32)
-        for i in range(self.half):
-            self.over(2 * i + 1 - self.low).wait_send()
-        for k in range(1, self.half):
-            self.on(2 * lax.rem(self.high + k, self.half) + self.low).wait_send()
-        return total
-
-    @staticmethod
-    def scratch(count, rows, width):
-        half = count // 2
-        dma = pltpu.SemaphoreType.DMA
-        return [
-            pltpu.VMEM((count, rows, width), jnp.bfloat16),
-            pltpu.VMEM((half, rows, width), jnp.bfloat16),
-            pltpu.VMEM((half, rows, width), jnp.bfloat16),
-            dma((half,)), dma((half,)), dma((half,)), dma((half,)),
-        ]
+    )(normed, packed, expert)
 
 
 def scan_forward_kernel(
     count, cuts,
-    act_ref, gate_ref, selected_ref, small_ref, output_ref,
-    pre_ref, mixed_ref, mixer_low_ref, prior_ref, end_ref, summed_ref,
-    state_ref, delta_ref, scanned_ref, *relay_refs,
+    act_ref, gate_ref, selected_ref, small_ref, output_ref, expert_ref,
+    pre_ref, mixed_ref, mixer_low_ref, prior_ref, end_ref, summed_ref, expert_out_ref,
+    state_ref, delta_ref, scanned_ref, land_ref, *refs,
 ):
     steps, inner = act_ref.shape
     tiles = inner // LANES
     state = cuts.state
     halves = state // 8
     step = pl.program_id(0)
-    relay = Relay("seq", count, *relay_refs)
+    relay = whole_relay("seq", count, refs[:7])
+    gather = Gather(count, expert_ref, land_ref, *refs[7:])
 
     @pl.when(step == 0)
     def _():
         greet(count)
+        gather.start()
         state_ref[...] = jnp.zeros_like(state_ref)
+
+    @pl.when(step == 1)
+    def _():
+        gather.spread(0)
+        gather.spread(1)
+
+    @pl.when(step == count // 2)
+    def _():
+        gather.forward()
 
     rates2 = -LOG2E * jnp.exp(small_ref[cuts.decay : cuts.decay + state, :])
     pre = inner_rows(
@@ -452,25 +625,31 @@
     mixed_ref[...] = mixed
     mixer_low_ref[...] = low
     relay.part[step] = dot_nn(low, output_ref[...]).astype(jnp.bfloat16)
-    relay.made(step)
+    relay.made(step // 2, lax.rem(step, 2))
+
+    def pass_on(block):
+        relay.pass_on(block // 2, lax.rem(block, 2))
 
     @pl.when(step >= 2)
     def _():
-        relay.pass_on(step - 2)
+        pass_on(step - 2)
 
     @pl.when(step == count - 1)
     def _():
-        relay.pass_on(step - 1)
-        relay.pass_on(step)
+        pass_on(step - 1)
+        pass_on(step)
         summed_ref[...] = relay.finish()
-
-
-def scan_forward(count, cuts, width, act, gate, selected, small, weights):
+        gather.finish()
+        expert_out_ref[...] = land_ref[...]
+
+
+def scan_forward(count, cuts, width, act, gate, selected, small, weights, expert):
     length, inner = act.shape
     state = cuts.state
     block = length // count
     rows = pl.BlockSpec((block, inner), lambda t: (t, 0))
     whole = pl.BlockSpec((state, inner), lambda t: (0, 0))
+    pieces = (count, expert.shape[0], expert.shape[1] // 2)
     return pl.pallas_call(
         functools.partial(scan_forward_kernel, count, cuts),
         grid=(count,),
@@ -480,6 +659,7 @@
             pl.BlockSpec((1, cuts.picks, block), lambda t: (t, 0, 0)),
             pl.BlockSpec(small.shape, lambda t: (0, 0)),
             pl.BlockSpec((inner, width), lambda t: (0, 2)),
+            pl.BlockSpec(expert.shape, lambda t: (0, 0)),
         ],
         out_specs=[
             rows,
@@ -488,6 +668,7 @@
             pl.BlockSpec((block, state, inner), lambda t: (t, 0, 0)),
             whole,
             pl.BlockSpec((block, width), lambda t: (0, 0)),
+            pl.BlockSpec(pieces, lambda t: (0, 0, 0)),
         ],
         out_shape=[
             jax.ShapeDtypeStruct((length, inner), jnp.float32),
@@ -496,12 +677,15 @@
             jax.ShapeDtypeStruct((length, state, inner), jnp.float32),
             jax.ShapeDtypeStruct((state, inner), jnp.float32),
             jax.ShapeDtypeStruct((block, width), jnp.float32),
+            jax.ShapeDtypeStruct(pieces, jnp.bfloat16),
         ],
         scratch_shapes=[
             pltpu.VMEM((state, inner), jnp.float32),
             pltpu.VMEM((block, inner), jnp.float32),
             pltpu.VMEM((block, inner), jnp.float32),
-            *Relay.scratch(count, block, width),
+            pltpu.VMEM(pieces, jnp.bfloat16),
+            *relay_scratch(count, block, width),
+            *gather_scratch(count),
         ],
         compiler_params=pltpu.CompilerParams(
             collective_id=1, has_side_effects=True, vmem_limit_bytes=VMEM_LIMIT
@@ -512,18 +696,19 @@
             transcendentals=length * state * inner,
         ),
         name="scan_forward",
-    )(act, gate, selected, small, weights)
+    )(act, gate, selected, small, weights, expert)
 
 
 def scan_backward_kernel(
     count, cuts,
     own_ref, act_ref, gate_ref, mixed_ref, pre_ref, selected_ref, small_ref, output_ref,
-    prior_ref, end_ref,
+    prior_ref, end_ref, expert_ref,
     grad_gate_ref, grad_act_ref, grad_step_ref, rate_total_ref, rows_ref, grad_selected_ref,
-    all_out_ref,
+    all_out_ref, expert_out_ref,
     incoming_ref, post_ref, delta_ref, grad_ref, grad_delta_ref, all_ref,
     part_ref, partial_ref, total_ref,
     send_hi, recv_hi, send_x, recv_x, send_rs, recv_rs, send_ag, recv_ag,
+    other_ref, held_ref, swap_s, swap_r, *scatter_refs,
 ):
     steps, inner = act_ref.shape
     tiles = inner // LANES
@@ -535,6 +720,7 @@
     partner = 2 * high + 1 - low
     index = pl.program_id(0)
     now = count - 1 - index
+    scatter = Scatter(count, expert_ref, other_ref, held_ref, swap_s, swap_r, scatter_refs)
 
     def along(k):
         return remote(
@@ -720,6 +906,18 @@
     def _():
         hand_over(now - 2)
 
+    @pl.when(index == 1)
+    def _():
+        scatter.start()
+
+    @pl.when(index == count // 2)
+    def _():
+        scatter.pass_on()
+
+    @pl.when(index == count - 2)
+    def _():
+        scatter.hand_over()
+
     @pl.when(index == jnp.minimum(count - 1 - own + 2, count - 1))
     def _():
         total = part_ref[own]
@@ -751,9 +949,12 @@
         for k in range(1, count):
             partial_to(lax.rem(own + k, count)).wait_send()
             total_to(k).wait_send()
-
-
-def scan_backward(count, cuts, grad_low, act, gate, mixed, pre, selected, small, weights, priors, end):
+        scatter.finish(expert_out_ref)
+
+
+def scan_backward(
+    count, cuts, grad_low, act, gate, mixed, pre, selected, small, weights, priors, end, expert
+):
     length, inner = act.shape
     state = cuts.state
     block = length // count
@@ -781,6 +982,7 @@
             pl.BlockSpec((inner, width), lambda t: (0, 2)),
             pl.BlockSpec((block, state, inner), lambda t: (back(t), 0, 0)),
             whole,
+            pl.BlockSpec(expert.shape, lambda t: (0, 0, 0)),
         ],
         out_specs=[
             rows,
@@ -790,6 +992,7 @@
             pl.BlockSpec((8, inner), lambda t: (0, 0)),
             pl.BlockSpec(picked, lambda t: (0, 0, 0)),
             pl.BlockSpec((count, block, width), lambda t: (0, 0, 0)),
+            pl.BlockSpec((expert.shape[1], 2 * expert.shape[2]), lambda t: (0, 0)),
         ],
         out_shape=[
             jax.ShapeDtypeStruct((length, inner), jnp.bfloat16),
@@ -799,6 +1002,7 @@
             jax.ShapeDtypeStruct((8, inner), jnp.float32),
             jax.ShapeDtypeStruct(picked, jnp.float32),
             jax.ShapeDtypeStruct((count, block, width), jnp.bfloat16),
+            jax.ShapeDtypeStruct((expert.shape[1], 2 * expert.shape[2]), jnp.float32),
         ],
         scratch_shapes=[
             pltpu.VMEM((state, inner), jnp.float32),
@@ -812,6 +1016,7 @@
             pltpu.VMEM(picked, jnp.float32),
             dma((half,)), dma((half,)), dma((half,)), dma((half,)),
             dma((count,)), dma((count,)), dma((count,)), dma((count,)),
+            *scatter_scratch(count, expert.shape[1], expert.shape[2]),
         ],
         compiler_params=pltpu.CompilerParams(
             collective_id=2, has_side_effects=True, vmem_limit_bytes=VMEM_LIMIT
@@ -822,20 +1027,21 @@
             transcendentals=length * state * inner,
         ),
         name="scan_backward",
-    )(grad_low, act, gate, mixed, pre, selected, small, weights, priors, end)
+    )(grad_low, act, gate, mixed, pre, selected, small, weights, priors, end, expert)
 
 
 def back_kernel(
     count, lines, cuts,
     grad_selected_ref, small_ref, weights_ref, ext_ref, sum_ref, grad_act_ref, grad_gate_ref,
     mixer_low_ref, normed_ref, grad_middle_ref, grad_step_ref, rate_total_ref, scan_rows_ref,
-    vectors_ref,
-    summed_ref, shard_ref, totals_ref,
+    vectors_ref, expert_ref,
+    summed_ref, shard_ref, totals_ref, expert_out_ref,
     grad_sum_ref, grad_conv_ref, grad_small_ref, ours_ref, theirs_ref,
-    send_v, recv_v, send_u, recv_u, *relay_refs,
+    send_v, recv_v, send_u, recv_u, other_ref, held_ref, swap_s, swap_r, *refs,
 ):
-    relay = Relay("seq", count, *relay_refs[:7])
-    spread = Relay("dp", lines, *relay_refs[7:])
+    scatter = Scatter(count, expert_ref, other_ref, held_ref, swap_s, swap_r, refs[:6])
+    relay = whole_relay("seq", count, refs[6:13])
+    spread = whole_relay("dp", lines, refs[13:])
     line, own, _, _ = place()
     length, inner = sum_ref.shape
     width = normed_ref.shape[1]
@@ -843,6 +1049,7 @@
     kernel = cuts.kernel
     shard = shard_ref.shape[0]
     greet(count, lines)
+    scatter.start()
     grad_small_ref[...] = jnp.zeros_like(grad_small_ref)
     grad_sum_ref[length:, :] = jnp.zeros((8, inner), jnp.float32)
     select = small_ref[: cuts.picks, :].astype(jnp.bfloat16)
@@ -888,10 +1095,11 @@
             dot_nn(grad_conv, weights_ref[:, :width])
             + dot_nn(grad_gate_ref[pl.ds(start, rows), :], weights_ref[:, width : 2 * width])
         ).astype(jnp.bfloat16)
-        relay.made(b)
+        relay.made(b // 2, lax.rem(b, 2))
         return carry
 
     lax.fori_loop(0, count, second, 0)
+    scatter.pass_on()
 
     decay = slice(cuts.decay, cuts.decay + cuts.state)
     grad_small_ref[cuts.step : cuts.step + cuts.rank, :] = grad_step_ref[...]
@@ -901,6 +1109,12 @@
     for d in range(lines):
         spread.part[d, :, 3 * width :] = small_t[d * shard : (d + 1) * shard].astype(jnp.bfloat16)
     chunk = width // 3
+
+    def pass_on(j, carry):
+        b = order(j)
+        relay.pass_on(b // 2, lax.rem(b, 2))
+        return carry
+
     ours_ref[...] = vectors_ref[...]
     for left_ref, right_ref, place_at in (
         (mixer_low_ref, grad_middle_ref, 2 * width),
@@ -923,9 +1137,10 @@
 
         lax.fori_loop(0, 3, columns, 0)
         if place_at == 2 * width:
-            lax.fori_loop(0, count, lambda j, carry: (relay.pass_on(order(j)), carry)[1], 0)
+            lax.fori_loop(0, count, pass_on, 0)
     for d in range(lines):
-        spread.made(d)
+        spread.made(d // 2, d % 2)
+    scatter.hand_over()
 
     def sum_over(size, axis, send, recv):
         here = own if axis == "seq" else line
@@ -948,15 +1163,16 @@
 
     ours_ref[...] = sum_over(count, "seq", send_v, recv_v)
     for d in range(lines):
-        spread.pass_on(d)
+        spread.pass_on(d // 2, d % 2)
     totals_ref[...] = sum_over(lines, "dp", send_u, recv_u)
     summed_ref[...] = relay.finish()
     shard_ref[...] = spread.finish()
+    scatter.finish(expert_out_ref)
 
 
 def back(
     count, lines, shard, cuts, grad_selected, small, weights, ext, conv_sum, grad_act, grad_gate,
-    mixer_low, normed, grad_middle, grad_step, rate_total, scan_rows, vectors,
+    mixer_low, normed, grad_middle, grad_step, rate_total, scan_rows, vectors, expert,
 ):
     length, inner = conv_sum.shape
     width = normed.shape[1]
@@ -966,16 +1182,17 @@
     dma = pltpu.SemaphoreType.DMA
     args = (
         grad_selected, small, weights, ext, conv_sum, grad_act, grad_gate, mixer_low, normed,
-        grad_middle, grad_step, rate_total, scan_rows, vectors,
+        grad_middle, grad_step, rate_total, scan_rows, vectors, expert,
     )
     return pl.pallas_call(
         functools.partial(back_kernel, count, lines, cuts),
         in_specs=[vmem] * len(args),
-        out_specs=[vmem] * 3,
+        out_specs=[vmem] * 4,
         out_shape=[
             jax.ShapeDtypeStruct((rows, width), jnp.float32),
             jax.ShapeDtypeStruct((shard, columns), jnp.float32),
             jax.ShapeDtypeStruct(vectors.shape, jnp.float32),
+            jax.ShapeDtypeStruct((expert.shape[1], 2 * expert.shape[2]), jnp.float32),
         ],
         scratch_shapes=[
             pltpu.VMEM((length + 8, inner), jnp.float32),
@@ -984,8 +1201,9 @@
             pltpu.VMEM(vectors.shape, jnp.float32),
             pltpu.VMEM((count + lines, *vectors.shape), jnp.float32),
             dma((count,)), dma((count,)), dma((lines,)), dma((lines,)),
-            *Relay.scratch(count, rows, width),
-            *Relay.scratch(lines, shard, columns),
+            *scatter_scratch(count, expert.shape[1], expert.shape[2]),
+            *relay_scratch(count, rows, width),
+            *relay_scratch(lines, shard, columns),
         ],
         compiler_params=pltpu.CompilerParams(
             collective_id=3, has_side_effects=True, vmem_limit_bytes=VMEM_LIMIT
@@ -996,6 +1214,254 @@
             transcendentals=length * inner,
         ),
         name="back",
+    )(*args)
+
+
+SLOTS = 64
+
+
+def gauss(values):
+    return 0.5 * (1.0 + lax.erf(values * math.sqrt(0.5)))
+
+
+def split_low(values):
+    high = values.astype(jnp.bfloat16)
+    return high, (values - high.astype(jnp.float32)).astype(jnp.bfloat16)
+
+
+def experts_kernel(
+    count, lines, experts,
+    x_ref, mixer_ref, grad_ref, chosen_ref, table_ref, back_table_ref, gain_ref, router_ref,
+    up_ref, down_ref,
+    output_ref, grad_middle_ref, grad_low_ref, vectors_ref, grad_up_ref, grad_down_ref,
+    middle_ref, normed_ref, send_ref, rows_ref, made_ref, got_ref, act_ref, slope_ref, pre_ref,
+    send_sem, recv_sem, home_s, home_r,
+):
+    line, own, _, _ = place()
+    q, f, low = square()
+    mate = seat_of(q, 1 - f, low)
+    copies = lines // experts
+    barrier = pltpu.get_barrier_semaphore()
+    for d in range(1, lines):
+        for where in (own, mate):
+            pl.semaphore_signal(
+                barrier, inc=1, device_id=(lax.rem(line + d, lines), where), device_id_type=MESH
+            )
+    pl.semaphore_signal(barrier, inc=1, device_id=(line, mate), device_id_type=MESH)
+    pl.semaphore_wait(barrier, 2 * lines - 1)
+
+    peers = [(j, d) for d in range(lines) for j in (1, 0) if (j, d) != (0, 0)]
+
+    def out_copy(what, j, d):
+        there = lax.rem(line + d, lines)
+        return remote(
+            send_ref.at[what, there // copies], rows_ref.at[what, j, line],
+            send_sem.at[what, j, d], recv_sem.at[what, j, line],
+            there, mate if j else own,
+        )
+
+    def arrived(what, j, d):
+        from_line = lax.rem(line + d, lines)
+        return remote(
+            send_ref.at[what, 0], rows_ref.at[what, j, from_line],
+            send_sem.at[what, j, d], recv_sem.at[what, j, from_line],
+            from_line, mate if j else own,
+        )
+
+    def home_copy(what, j, d):
+        there = lax.rem(line + d, lines)
+        return remote(
+            made_ref.at[what, j, there], got_ref.at[what, j, line],
+            home_s.at[what, j, d], home_r.at[what, j, line],
+            there, mate if j else own,
+        )
+
+    def came_home(what, j, d):
+        from_line = lax.rem(line + d, lines)
+        return remote(
+            made_ref.at[what, j, 0], got_ref.at[what, j, from_line],
+            home_s.at[what, j, d], home_r.at[what, j, from_line],
+            from_line, mate if j else own,
+        )
+
+    middle = x_ref[...] + mixer_ref[...]
+    middle_ref[...] = middle
+    gain = gain_ref[...]
+    scale = lax.rsqrt(jnp.mean(middle * middle, axis=1, keepdims=True) + 1e-05)
+    normed = (middle * scale * gain).astype(jnp.bfloat16)
+    normed_ref[...] = normed
+    rows, width = middle.shape
+    slots = table_ref.shape[0] // experts
+
+    def dispatch(what, values):
+        sent = dot_nn(table_ref[...], values).astype(jnp.bfloat16)
+        for e in range(experts):
+            send_ref[what, e] = sent[e * slots : (e + 1) * slots]
+        for j, d in peers:
+            out_copy(what, j, d).start()
+        rows_ref[what, 0, line] = send_ref[what, line // copies]
+
+    dispatch(0, normed)
+    lane = lax.broadcasted_iota(jnp.int32, (rows, LANES), 1)
+    logits = jnp.where(lane < experts, outer_cols(normed, router_ref[...]), -jnp.inf)
+    grown = jnp.exp(logits - jnp.max(logits, axis=1, keepdims=True))
+    probs = grown / jnp.sum(grown, axis=1, keepdims=True)
+    chosen = chosen_ref[...]
+    gate = jnp.sum(chosen * probs, axis=1, keepdims=True)
+    dispatch(1, (gate * grad_ref[...]).astype(jnp.bfloat16))
+
+    total = 2 * lines * slots
+    hidden = up_ref.shape[1]
+    chunk = hidden // 3 if hidden % (3 * LANES) == 0 else hidden
+    parts = hidden // chunk
+
+    def rows_of(ref, what):
+        return ref[what].reshape(total, width)
+
+    def columns(c):
+        return pl.ds(pl.multiple_of(c * chunk, LANES), chunk)
+
+    for j, d in peers:
+        arrived(0, j, d).wait_recv()
+
+    def rise(c, carry):
+        pre_ref[:, columns(c)] = dot_nn(rows_of(rows_ref, 0), up_ref[:, columns(c)])
+        pre = pre_ref[:, columns(c)]
+        half = gauss(pre)
+        act_ref[:, columns(c)] = (pre * half).astype(jnp.bfloat16)
+        pre_ref[:, columns(c)] = half + pre * (
+            jnp.exp(-0.5 * pre * pre) * (1.0 / math.sqrt(2.0 * math.pi))
+        )
+        return carry
+
+    lax.fori_loop(0, parts, rise, 0)
+
+    wide = width // 3
+
+    def send_home(what, left_ref, right_ref):
+        def make(c, carry):
+            here = pl.ds(pl.multiple_of(c * wide, LANES), wide)
+            there = pl.ds(pl.multiple_of(c * wide, LANES), wide)
+            made = outer_cols(left_ref[...], right_ref[there, :]).astype(jnp.bfloat16)
+            made_ref[what, :, :, :, here] = made.reshape(2, lines, slots, wide)
+            return carry
+
+        lax.fori_loop(0, 3, make, 0)
+        for j, d in peers:
+            home_copy(what, j, d).start()
+        got_ref[what, 0, line] = made_ref[what, 0, line]
+
+    for j, d in peers:
+        arrived(1, j, d).wait_recv()
+
+    def fall(c, carry):
+        slope_ref[:, columns(c)] = (
+            dot_nn(rows_of(rows_ref, 1), down_ref[:, columns(c)]) * pre_ref[:, columns(c)]
+        ).astype(jnp.bfloat16)
+        return carry
+
+    lax.fori_loop(0, parts, fall, 0)
+    send_home(1, slope_ref, up_ref)
+    send_home(0, act_ref, down_ref)
+
+    pieces = grad_up_ref.shape[1]
+
+    def weigh(c, carry):
+        up = inner_rows(rows_of(rows_ref, 0), slope_ref[:, columns(c)]).astype(jnp.bfloat16)
+        down = inner_rows(rows_of(rows_ref, 1), act_ref[:, columns(c)]).astype(jnp.bfloat16)
+        grad_up_ref[:, :, columns(c)] = up.reshape(count, pieces, chunk)
+        grad_down_ref[:, :, columns(c)] = down.reshape(count, pieces, chunk)
+        return carry
+
+    lax.fori_loop(0, parts, weigh, 0)
+
+    def home(what):
+        for j, d in peers:
+            came_home(what, j, d).wait_recv()
+        both = None
+        for e in range(experts):
+            own_rows = None
+            for c in range(copies):
+                for j in range(2):
+                    term = got_ref[what, j, e * copies + c].astype(jnp.float32)
+                    own_rows = term if own_rows is None else own_rows + term
+            high, rest = split_low(own_rows)
+            here = back_table_ref[e]
+            term = dot_nn(here, high) + dot_nn(here, rest)
+            both = term if both is None else both + term
+        return both
+
+    grad = grad_ref[...]
+    middle = middle_ref[...]
+    picked = home(0)
+    output_ref[...] = middle + gate * picked
+    grad_gate = jnp.sum(grad * picked, axis=1, keepdims=True)
+    grad_logits = gate * (chosen - probs) * grad_gate
+    grad_normed = home(1) + dot_nn(grad_logits, router_ref[...].astype(jnp.float32), HIGHEST)
+    scaled = gain * grad_normed
+    grad_middle = (
+        grad
+        + scale * scaled
+        - middle * (scale * scale * scale) * jnp.mean(scaled * middle, axis=1, keepdims=True)
+    )
+    grad_middle_ref[...] = grad_middle
+    grad_low_ref[...] = grad_middle.astype(jnp.bfloat16)
+    vectors_ref[...] = jnp.zeros_like(vectors_ref)
+    vectors_ref[1:2, :] = jnp.sum(grad_normed * middle * scale, axis=0, keepdims=True)
+    vectors_ref[2 : 2 + experts, :] = inner_rows(
+        grad_logits, normed_ref[...].astype(jnp.float32), HIGHEST
+    )[:experts]
+    for what in range(2):
+        for j, d in peers:
+            out_copy(what, j, d).wait_send()
+            home_copy(what, j, d).wait_send()
+
+
+def run_experts(
+    count, lines, experts, x, mixer, grad, chosen, table, back_table, gain, router, up, down
+):
+    rows, width = x.shape
+    slots = table.shape[0] // experts
+    total = 2 * lines * slots
+    hidden = up.shape[1]
+    pieces = (count, up.shape[0] // count, hidden)
+    vmem = pl.BlockSpec(memory_space=pltpu.VMEM)
+    dma = pltpu.SemaphoreType.DMA
+    args = (x, mixer, grad, chosen, table, back_table, gain, router, up, down)
+    low = jnp.bfloat16
+    return pl.pallas_call(
+        functools.partial(experts_kernel, count, lines, experts),
+        in_specs=[vmem] * len(args),
+        out_specs=[vmem] * 6,
+        out_shape=[
+            jax.ShapeDtypeStruct((rows, width), jnp.float32),
+            jax.ShapeDtypeStruct((rows, width), jnp.float32),
+            jax.ShapeDtypeStruct((rows, width), low),
+            jax.ShapeDtypeStruct((8, width), jnp.float32),
+            jax.ShapeDtypeStruct(pieces, low),
+            jax.ShapeDtypeStruct(pieces, low),
+        ],
+        scratch_shapes=[
+            pltpu.VMEM((rows, width), jnp.float32),
+            pltpu.VMEM((rows, width), low),
+            pltpu.VMEM((2, experts, slots, width), low),
+            pltpu.VMEM((2, 2, lines, slots, width), low),
+            pltpu.VMEM((2, 2, lines, slots, width), low),
+            pltpu.VMEM((2, 2, lines, slots, width), low),
+            pltpu.VMEM((total, hidden), low),
+            pltpu.VMEM((total, hidden), low),
+            pltpu.VMEM((total, hidden), jnp.float32),
+            dma((2, 2, lines)), dma((2, 2, lines)), dma((2, 2, lines)), dma((2, 2, lines)),
+        ],
+        compiler_params=pltpu.CompilerParams(
+            collective_id=4, has_side_effects=True, vmem_limit_bytes=VMEM_LIMIT
+        ),
+        cost_estimate=pl.CostEstimate(
+            flops=12 * total * width * hidden,
+            bytes_accessed=8 * width * hidden,
+            transcendentals=2 * total * hidden,
+        ),
+        name="experts",
     )(*args)
 
 
@@ -1052,120 +1518,61 @@
         [input_proj.reshape(2 * width, shard).T, output_proj, small.T], axis=1
     )
     packed = jnp.pad(packed, ((0, shard_rows - shard), (0, 0)))
-    w_up, w_down = (
-        lax.all_gather(expert_up, "seq", axis=0, tiled=True),
-        lax.all_gather(expert_down, "seq", axis=1, tiled=True),
-    )
-    (normed_all, weights, small_all, conv_ext, conv_sum, conv_act, gate_branch, selected) = front(
-        count, lines, cuts, normed, packed
-    )
-    pre, mixed, mixer_low, priors, end, mixer_out = scan_forward(
-        count, cuts, width, conv_act, gate_branch, selected, small_all, weights
-    )
-    middle = x_in + mixer_out
+    (normed_all, weights, small_all, conv_ext, conv_sum, conv_act, gate_branch, selected, up_cut) = (
+        front(count, lines, cuts, normed, packed, expert_up)
+    )
+    pre, mixed, mixer_low, priors, end, mixer_out, down_cut = scan_forward(
+        count, cuts, width, conv_act, gate_branch, selected, small_all, weights, expert_down.T
+    )
 
     experts = router.shape[0]
-    copies = lax.axis_size("dp") // experts
-    capacity = CAP
-    gain_two = expert_gain.astype(jnp.float32)
-    normed_two = rms_norm(middle, gain_two).astype(jnp.bfloat16)
-    probs = jax.nn.softmax(outer_cols(normed_two, router), axis=-1)
     route = routes.reshape(rows)
-    chosen = (route[:, None] == lax.broadcasted_iota(jnp.int32, (rows, experts), 1)).astype(
+    chosen = (route[:, None] == lax.broadcasted_iota(jnp.int32, (rows, LANES), 1)).astype(
         jnp.float32
     )
-    gate = jnp.sum(chosen * probs, axis=1)
     earlier = (
         lax.broadcasted_iota(jnp.int32, (rows, rows), 0)
         > lax.broadcasted_iota(jnp.int32, (rows, rows), 1)
     ).astype(jnp.float32)
     before = jnp.dot(earlier, chosen, precision=HIGHEST)
     position = jnp.sum(before * chosen, axis=1).astype(jnp.int32)
-    slot = route * capacity + position
-    dispatch_table = (
-        slot[None, :] == lax.broadcasted_iota(jnp.int32, (experts * capacity, rows), 0)
+    slot = route * SLOTS + position
+    table = (
+        slot[None, :] == lax.broadcasted_iota(jnp.int32, (experts * SLOTS, rows), 0)
     ).astype(jnp.bfloat16)
-    buffer = jnp.dot(dispatch_table, normed_two, preferred_element_type=jnp.float32).astype(
-        jnp.bfloat16
-    )
-    send = jnp.repeat(buffer.reshape(experts, capacity, width), copies, axis=0)
-    received = lax.all_to_all(send, "dp", split_axis=0, concat_axis=0, tiled=True)
-    sources = received.shape[0]
-    expert_rows = received.reshape(-1, width)
-    expert_pre = jnp.dot(expert_rows, w_up, preferred_element_type=jnp.float32)
-    expert_act, gelu_pull = jax.vjp(gelu_exact, expert_pre)
-    act_low = expert_act.astype(jnp.bfloat16)
-    partial_out = jnp.dot(act_low, w_down, preferred_element_type=jnp.float32).reshape(
-        sources, capacity, width
-    )
-    returned = lax.all_to_all(
-        partial_out.astype(jnp.bfloat16), "dp", split_axis=0, concat_axis=0, tiled=True
-    ).astype(partial_out.dtype)
-    expert_out = jnp.sum(returned.reshape(experts, copies, capacity, width), axis=1).reshape(
-        experts * capacity, width
-    )
-    picked = jnp.take(expert_out, slot, axis=0)
-    output = middle + gate[:, None] * picked
-    grad_out = cotangent.reshape(rows, width)
-    grad_pick = (gate[:, None] * grad_out).astype(jnp.bfloat16)
-    grad_gate = jnp.sum(grad_out * picked, axis=1)
-    grad_buffer = jnp.dot(dispatch_table, grad_pick, preferred_element_type=jnp.float32).astype(
-        jnp.bfloat16
-    )
-    grad_send = jnp.repeat(grad_buffer.reshape(experts, capacity, width), copies, axis=0)
-    grad_rows = lax.all_to_all(grad_send, "dp", split_axis=0, concat_axis=0, tiled=True)
-    grad_flat = grad_rows.reshape(-1, width)
-    grad_down_w = inner_rows(act_low, grad_flat)
-    grad_act = outer_cols(grad_flat, w_down)
-    grad_pre = gelu_pull(grad_act)[0].astype(jnp.bfloat16)
-    grad_up_w = inner_rows(expert_rows, grad_pre)
-    grad_in_rows = outer_cols(grad_pre, w_up).reshape(sources, capacity, width)
-    grad_back = lax.all_to_all(
-        grad_in_rows.astype(jnp.bfloat16), "dp", split_axis=0, concat_axis=0, tiled=True
-    ).astype(grad_in_rows.dtype)
-    grad_slots = jnp.sum(grad_back.reshape(experts, copies, capacity, width), axis=1).reshape(
-        experts * capacity, width
-    )
-    grad_logits = gate[:, None] * (chosen - probs) * grad_gate[:, None]
-    router_full = router.astype(jnp.float32)
-    grad_normed_two = jnp.take(grad_slots, slot, axis=0) + jnp.dot(
-        grad_logits, router_full, precision=HIGHEST
-    )
-    grad_router = inner_rows(grad_logits, normed_two.astype(jnp.float32), HIGHEST)
-    unused_two, pull_two = jax.vjp(rms_norm, middle, gain_two)
-    grad_middle_norm, grad_gain_two = pull_two(grad_normed_two)
-    grad_middle = grad_out + grad_middle_norm
-    grad_middle_low = grad_middle.astype(jnp.bfloat16)
-
-    grad_middle_low, grad_up_low, grad_down_low = lax.optimization_barrier(
-        (grad_middle_low, grad_up_w.astype(jnp.bfloat16), grad_down_w.astype(jnp.bfloat16))
-    )
-    expert_grads = (
-        lax.psum_scatter(grad_up_low, "seq", scatter_dimension=0, tiled=True).astype(jnp.float32),
-        lax.psum_scatter(grad_down_low, "seq", scatter_dimension=1, tiled=True).astype(
-            jnp.float32
-        ),
-    )
-
-    (grad_gate_branch, grad_act, grad_step_w, rate_total, scan_rows, grad_selected, grad_middle_all) = (
+    back_table = (
+        slot[None, :, None]
+        == lax.broadcasted_iota(jnp.int32, (experts, rows, SLOTS), 2)
+        + SLOTS * lax.broadcasted_iota(jnp.int32, (experts, rows, SLOTS), 0)
+    ).astype(jnp.bfloat16)
+    output, grad_middle, grad_middle_low, vectors, grad_up_low, grad_down_low = run_experts(
+        count,
+        lines,
+        experts,
+        x_in,
+        mixer_out,
+        cotangent.reshape(rows, width),
+        chosen,
+        table,
+        back_table,
+        expert_gain.astype(jnp.float32)[None],
+        jnp.pad(router, ((0, LANES - experts), (0, 0))),
+        up_cut.reshape(-1, up_cut.shape[2]),
+        down_cut.reshape(-1, down_cut.shape[2]),
+    )
+
+    (grad_gate_branch, grad_act, grad_step_w, rate_total, scan_rows, grad_selected, grad_middle_all,
+     grad_down_t) = (
         scan_backward(
             count, cuts, grad_middle_low, conv_act, gate_branch, mixed, pre, selected, small_all,
-            weights, priors, end,
-        )
-    )
-    vectors = jnp.concatenate(
-        [
-            jnp.zeros((1, width), jnp.float32),
-            grad_gain_two[None],
-            grad_router,
-            jnp.zeros((6 - experts, width), jnp.float32),
-        ],
-        axis=0,
-    )
-    grad_normed, grad_shard, totals = back(
+            weights, priors, end, grad_down_low,
+        )
+    )
+    grad_normed, grad_shard, totals, grad_up = back(
         count, lines, shard_rows, cuts, grad_selected, small_all, weights, conv_ext, conv_sum,
         grad_act, grad_gate_branch, mixer_low, normed_all.reshape(-1, width),
         grad_middle_all.reshape(-1, width), grad_step_w, rate_total, scan_rows, vectors,
+        grad_up_low,
     )
     grad_shard = grad_shard[:shard]
     grad_input_w = grad_shard[:, : 2 * width].T.reshape(2, width, shard)
@@ -1192,8 +1599,8 @@
         grad_shard[:, 2 * width : 3 * width],
         totals[1],
         totals[2 : 2 + experts],
-        expert_grads[0],
-        expert_grads[1],
+        grad_up,
+        grad_down_t.T,
     )
 
 

time: 717 us -> 594 us (0.83)
  waiting for transfers between devices: 86.1 us -> 0 us
  Pallas kernels: 500 us -> 562 us
  matrix products: 41 us -> 1.05 us
  starting transfers between devices: 20.2 us -> 0 us
  local copies, waits for them, and re-layouts: 34.7 us -> 18.3 us
  between operations: 14 us -> 0.86 us
    pallas_call x0 -> x1, Pallas kernels: none -> 77.4 us  [run_experts(): pl.pallas_call(functools.partial(experts_kernel, count, lines, experts),...]
    reduce_scatter x1 -> x0, waiting for transfers between devices: 42 us -> none  [body(): lax.psum_scatter(grad_up_low, 'seq', scatter_dimension=0, tiled=True)]
    dot_general x11 -> x0, matrix products: 40.8 us -> none  [the longest x3 17.9 us: outer_cols(): lax.dot_general(left, right, (((1,), (1,)), ((), ())), precision=precisio...]
    all_gather x2 -> x0, waiting for transfers between devices: 32.2 us -> none  [the longest x1 32.2 us: body(): lax.all_gather(expert_down, 'seq', axis=1, tiled=True)]
    pallas_call x1, Pallas kernels: 125 us -> 102 us  [front(): pl.pallas_call(functools.partial(front_kernel, count, lines, cuts), in_sp...]
    all_to_all x4 -> x0, starting transfers between devices: 20.1 us -> none  [the longest x1 6.48 us: body(): lax.all_to_all(send, 'dp', split_axis=0, concat_axis=0, tiled=True)]
    pallas_call x1, Pallas kernels: 116 us -> 133 us  [back(): pl.pallas_call(functools.partial(back_kernel, count, lines, cuts), in_spe...]
    pallas_call x1, Pallas kernels: 173 us -> 159 us  [scan_backward(): pl.pallas_call(functools.partial(scan_backward_kernel, count, cuts), grid...]
  transfers between devices with their start and end apart: 8 -> 0, of which waited for: 5 -> 0; matrix products, arithmetic and copies ran while one was open for 7% -> 0% of each run, Pallas kernels for 70% -> 0%
where the time goes in v4:
time: 594 us; the launch traced here: 593 us
  Pallas kernels  562 us (95%)
  local copies, waits for them, and re-layouts  18.3 us (3%)
  other arithmetic  10.7 us (2%)
    pallas_call x1, Pallas kernels, scan_backward(): pl.pallas_call(functools.partial(scan_backward_kernel, count, cuts), grid...  159 us
    pallas_call x1, Pallas kernels, back(): pl.pallas_call(functools.partial(back_kernel, count, lines, cuts), in_spe...  133 us
    pallas_call x1, Pallas kernels, front(): pl.pallas_call(functools.partial(front_kernel, count, lines, cuts), in_sp...  102 us
    pallas_call x1, Pallas kernels, scan_forward(): pl.pallas_call(functools.partial(scan_forward_kernel, count, cuts), grid=...  91.2 us
    pallas_call x1, Pallas kernels, run_experts(): pl.pallas_call(functools.partial(experts_kernel, count, lines, experts),...  77.4 us

profile of v4, /device:TPU:31, one launch (start us, length us, event | category | flops | bytes accessed | tf_op | source)
XLA Modules:
  0.0 593.3 jit_solution(17420853903790582081)
XLA Ops:
  0.6 0.0 copy-start
  0.7 1.1 fusion.3
  1.7 0.0 copy-start.9
  1.7 1.2 multiply_reduce_fusion.1
  3.0 0.7 fusion.12
  3.6 0.7 convert_add_fusion
  4.3 1.3 reshape.120.gain_ref
  5.6 0.7 convert_element_type.40
  6.3 0.8 copy.48
  7.1 0.8 copy.49
  7.8 0.8 copy.46
  8.6 0.8 copy.50
  9.4 0.8 copy.47
  10.2 0.8 copy.51
  11.0 0.8 concatenate.6
  11.8 0.7 fusion.9.table_ref
  12.5 1.4 fusion.10.chosen_ref
  13.8 0.8 fusion.8.back_table_ref
  14.6 0.8 multiply_convert_fusion.normed_ref
  15.4 0.7 pad.14.router_ref
  16.2 0.9 fusion.5.packed_ref
  17.1 101.5 %front.1 = (bf16[8,128,1152]{2,1,0:T(8,128)(2,1)}, bf16[384,3712]{1,0:T(8,128)(2,1)}, f32[256,384]{1,0:T(8,128)}, f32[1032,384]{1,0:T(8,128)}, f32[1024,384]{1,0...) custom-call(bf16[128,1152]{1,0:T(8,128)(2,1)} %multiply_convert_fusi, ...), custom_call_target="tpu_custom_call" | custom-call | flops 1811939328 | bytes 7864320 | tf_op jit(solution)/shard_map/front/pallas_call | solution.py:501
  118.6 91.2 %scan_forward.1 = (f32[1024,384]{1,0:T(8,128)}, f32[1024,384]{1,0:T(8,128)}, bf16[1024,384]{1,0:T(8,128)(2,1)}, f32[1024,16,384]{2,1,0:T(8,128)}, f32[16,384]{1,...) custom-call(f32[1024,384]{1,0:T(8,128)} %get-tuple-element.50.act_ref, ...), custom_call_target="tpu_custom_call" | custom-call | flops 50331648 | bytes 34603008 | tf_op jit(solution)/shard_map/scan_forward/pallas_call | solution.py:653
  209.8 77.4 %experts.1 = (f32[128,1152]{1,0:T(8,128)}, f32[128,1152]{1,0:T(8,128)}, bf16[128,1152]{1,0:T(8,128)(2,1)}, f32[8,1152]{1,0:T(8,128)}, bf16[8,144,1536]{2,1,0:T(8,128)(2,1)}, /*index=5*/bf16[8,144,1536]{2,1,0:T(8,128)(2,1)}) custom-call(f32[128,1152]{1,0:T(8,128)} %bitcast.39, f32[128,1152]{1,0:T(8,128)} %get-tuple-element.55.mixer_ref, ...), custom_call_target="tpu_custom_call" | custom-call | flops 10871635968 | bytes 14155776 | tf_op jit(solution)/shard_map/experts/pallas_call | solution.py:1432
  287.2 159.4 %scan_backward.1 = (bf16[1024,384]{1,0:T(8,128)(2,1)}, f32[1024,384]{1,0:T(8,128)}, f32[72,384]{1,0:T(8,128)}, f32[16,384]{1,0:T(8,128)}, f32[8,384]{1,0:T(8,128...) custom-call(bf16[128,1152]{1,0:T(8,128)(2,1)} %get-tuple-element.60.own_ref, ...), custom_call_target="tpu_custom_call" | custom-call | flops 125829120 | bytes 34603008 | tf_op jit(solution)/shard_map/scan_backward/pallas_call | solution.py:971
  446.6 0.0 copy-start.1
  446.6 132.9 %back.1 = (f32[128,1152]{1,0:T(8,128)}, f32[80,3712]{1,0:T(8,128)}, f32[8,1152]{1,0:T(8,128)}, f32[144,3072]{1,0:T(8,128)}) custom-call(f32[8,104,128]{2,1,0:T(8,128)} %get-tuple-element.66.grad_selected_ref, f32[256,384]{1,0:T(8,128)} %get-tuple-element.53.small_ref, bf16[384,3712]{1,0:T(8,128)(2,1)} %get-tuple-element.54.output_ref.weights_ref, ...), custom_call_target="tpu_custom_call" | custom-call | flops 4529848320 | bytes 11796480 | tf_op jit(solution)/shard_map/back/pallas_call | solution.py:1187
  579.5 0.0 copy-start.11
  579.6 1.4 multiply_reduce_fusion
  581.0 1.0 fusion.7
  581.9 0.6 slice_reduce_fusion.3
  582.6 0.6 slice.55
  583.2 0.6 convert_divide_fusion
  583.8 0.7 slice_reduce_fusion
  584.5 0.1 slice.59
  584.6 0.7 copy.55
  585.3 0.6 slice.58
  585.9 0.1 slice.61
  586.0 0.1 slice.56
  586.1 0.7 copy.54
  586.8 0.7 copy.56
  587.4 0.7 slice.53
  588.2 0.9 copy.61
  589.1 0.8 copy.65
  589.9 0.1 copy-done.4
  590.0 1.2 copy.66
  591.2 0.9 copy-done.3
  592.1 1.2 copy.67
  (27 shorter events, 0.2 us)
Async XLA Ops:
  0.6 14.0 %copy-start = (f32[1,128,1152]{2,1,0:T(8,128)S(1)}, f32[1,128,1152]{2,1,0:T(8,128)}, u32[]{:S(2)}) copy-start(f32[1,128,1152]{2,1,0:T(8,128)} %param.17) | copy-start | bytes 1769476
  0.7 14.8 %copy-start.12 = (bf16[4,1152]{1,0:T(4,128)(2,1)S(1)}, bf16[4,1152]{1,0:T(4,128)(2,1)}, u32[]{:S(2)}) copy-start(bf16[4,1152]{1,0:T(4,128)(2,1)} %param.31) | copy-start | bytes 27652
  0.7 15.5 %copy-start.8 = (bf16[2,1152,72]{1,2,0:T(8,128)(2,1)S(1)}, bf16[2,1152,72]{1,2,0:T(8,128)(2,1)}, u32[]{:S(2)}) copy-start(bf16[2,1152,72]{1,2,0:T(8,128)(2,1)} %param.21) | copy-start | bytes 995332
  1.7 14.5 %copy-start.9 = (bf16[72,1152]{1,0:T(8,128)(2,1)S(1)}, bf16[72,1152]{1,0:T(8,128)(2,1)}, u32[]{:S(2)}) copy-start(bf16[72,1152]{1,0:T(8,128)(2,1)} %param.29) | copy-start | bytes 497668
  446.6 132.9 %copy-start.1 = (f32[1,128,1152]{2,1,0:T(8,128)S(1)}, f32[1,128,1152]{2,1,0:T(8,128)}, u32[]{:S(2)}) copy-start(f32[1,128,1152]{2,1,0:T(8,128)} %param.17) | copy-start | bytes 1769476
  579.5 1.4 copy-start.2
  579.5 1.4 copy-start.7
  579.5 2.4 copy-start.10
  579.5 3.6 copy-start.11
  579.6 4.2 copy-start.5
  587.4 1.7 copy-start.6
  588.2 1.8 copy-start.4
  590.0 2.1 copy-start.3

commit v5 on v4

--- a/solution.py
+++ b/solution.py
@@ -59,10 +59,6 @@
     return jnp.where(low1, a, b) + jnp.where(low1, pltpu.roll(a, 7, 0), pltpu.roll(b, 1, 0))
 
 
-def lane_column(block, k):
-    return jnp.broadcast_to(block[:, k : k + 1], block.shape)
-
-
 MESH = pl.DeviceIdType.MESH
 VMEM_LIMIT = 60 * 1024 * 1024
 
@@ -122,6 +118,7 @@
         self.step_bias = self.conv_bias + 1
         self.skip = self.step_bias + 1
         self.rows = self.skip + 1
+        self.sent = -(-picks // 16) * 16
 
 
 class Relay:
@@ -261,15 +258,14 @@
             self.along(j, k).start()
         self.pair(j, 0, self.low).start()
 
-    def forward(self):
-        for j in range(2):
-            for k in range(1, self.quarter):
-                piece = self.piece(j, k, self.low)
-                remote(
-                    self.land.at[piece], self.land.at[piece], self.line_s.at[j, k],
-                    self.line_r.at[j, k], self.line, piece,
-                ).wait_recv()
-                self.pair(j, k, self.low).start()
+    def forward(self, j):
+        for k in range(1, self.quarter):
+            piece = self.piece(j, k, self.low)
+            remote(
+                self.land.at[piece], self.land.at[piece], self.line_s.at[j, k],
+                self.line_r.at[j, k], self.line, piece,
+            ).wait_recv()
+            self.pair(j, k, self.low).start()
 
     def finish(self):
         for j in range(2):
@@ -317,15 +313,29 @@
             seat_of(self.q, 1 - self.f, self.low),
         )
 
-    def start(self):
-        for j in (1, 0):
-            for i in range(self.quarter):
-                self.relays[j].over(i, 1 - self.low).start()
-
-    def pass_on(self):
-        for j in (1, 0):
-            for k in range(1, self.quarter):
-                self.relays[j].pass_on(lax.rem(self.q + k, self.quarter), self.low)
+    def turns(self):
+        far = [(j, lax.rem(self.q + k, self.quarter)) for k in range(1, self.quarter) for j in (1, 0)]
+        return far + [(1, self.q), (0, self.q)]
+
+    def send(self, turn):
+        j, i = self.turns()[turn]
+        self.relays[j].over(i, 1 - self.low).start()
+
+    def pass_on(self, turn):
+        j, i = self.turns()[turn]
+        self.relays[j].pass_on(i, self.low)
+
+    def send_far(self):
+        for turn in range(2 * self.quarter - 2):
+            self.send(turn)
+
+    def pass_far(self):
+        for turn in range(2 * self.quarter - 2):
+            self.pass_on(turn)
+
+    def send_near(self):
+        self.send(2 * self.quarter - 2)
+        self.send(2 * self.quarter - 1)
 
     def hand_over(self):
         self.held[...] = self.relays[1].finish().astype(jnp.bfloat16)
@@ -358,8 +368,8 @@
     count, lines, cuts,
     normed_ref, packed_ref, expert_ref,
     all_ref, weights_ref, small_ref, ext_ref, sum_ref, act_ref, gate_ref, selected_ref, land_ref,
-    part_ref, partial_ref,
-    send_w, recv_w, send_hi, recv_hi, send_x, recv_x, send_rs, recv_rs, send_ag, recv_ag,
+    part_ref, partial_ref, total_ref,
+    send_w, recv_w, send_up, send_down, recv_hi, send_x, recv_x, send_rs, recv_rs, send_ag, recv_ag,
     *gather_refs,
 ):
     line, own, high, low = place()
@@ -374,16 +384,24 @@
 
     copies = []
     shard_rows = pl.ds(pl.multiple_of(line * shard, 16), shard)
-    for k in range(1, half):
-        copy = remote(
-            normed_ref, all_ref.at[own], send_hi.at[k], recv_hi.at[k],
-            line, 2 * lax.rem(high + k, half) + low,
-        )
-        copy.start()
-        copies.append(copy)
-    copy = remote(normed_ref, all_ref.at[own], send_x.at[0], recv_x.at[0], line, partner)
-    copy.start()
-    copies.append(copy)
+    def step_on(i, up):
+        block = 2 * i + low
+        return remote(
+            all_ref.at[block], all_ref.at[block], (send_up if up else send_down).at[i],
+            recv_hi.at[i], line, 2 * (high + (1 if up else -1)) + low,
+        )
+
+    def can_go(up):
+        return high < half - 1 if up else high > 0
+
+    all_ref[own] = normed_ref[...]
+    for up in (True, False):
+
+        @pl.when(can_go(up))
+        def _(up=up):
+            step_on(high, up).start()
+
+    remote(all_ref.at[own], all_ref.at[own], send_x.at[high], recv_x.at[high], line, partner).start()
     for k in range(1, lines):
         copy = remote(
             packed_ref, weights_ref.at[shard_rows], send_w.at[k], recv_w.at[k],
@@ -392,23 +410,32 @@
         copy.start()
         copies.append(copy)
     gather.start()
-    all_ref[own] = normed_ref[...]
     weights_ref[shard_rows, :] = packed_ref[...]
     if lines * shard < inner:
         weights_ref[lines * shard :, :] = jnp.zeros(
             (inner - lines * shard, weights_ref.shape[1]), weights_ref.dtype
         )
     ext_ref[0:8, :] = jnp.zeros((8, inner), jnp.float32)
+    def cross(i):
+        block = 2 * i + low
+        return remote(
+            all_ref.at[block], all_ref.at[block], send_x.at[i], recv_x.at[i], line, partner
+        )
+
     for k in range(1, half):
-        block = 2 * lax.rem(high - k + half, half) + low
-        remote(
-            normed_ref, all_ref.at[block], send_hi.at[k], recv_hi.at[k], line, partner
-        ).wait_recv()
-        copy = remote(
-            all_ref.at[block], all_ref.at[block], send_x.at[k], recv_x.at[k], line, partner
-        )
-        copy.start()
-        copies.append(copy)
+        for up in (True, False):
+            i = high - k if up else high + k
+
+            @pl.when(i >= 0 if up else i < half)
+            def _(i=i, up=up):
+                step_on(i, up).wait_recv()
+
+                @pl.when(can_go(up))
+                def _():
+                    step_on(i, up).start()
+
+                cross(i).start()
+
     gather.spread(0)
     gather.spread(1)
     for k in range(1, lines):
@@ -418,10 +445,10 @@
             packed_ref, weights_ref.at[there], send_w.at[k], recv_w.at[k], from_line, own
         ).wait_recv()
     small_ref[...] = weights_ref[:, 3 * width :].astype(jnp.float32).T
-    for k in range(half):
-        block = 2 * lax.rem(high - k + half, half) + 1 - low
+    for i in range(half):
+        block = 2 * i + 1 - low
         remote(
-            normed_ref, all_ref.at[block], send_x.at[k], recv_x.at[k], line, partner
+            all_ref.at[block], all_ref.at[block], send_x.at[i], recv_x.at[i], line, partner
         ).wait_recv()
 
     def project(b, carry):
@@ -446,13 +473,12 @@
         sum_ref[pl.ds(start, rows), :] = total
         act_ref[pl.ds(start, rows), :] = act
         part_ref[b] = outer_cols(
-            small_ref[: cuts.picks, :].astype(jnp.bfloat16), act.astype(jnp.bfloat16)
-        )
+            small_ref[: cuts.sent, :].astype(jnp.bfloat16), act.astype(jnp.bfloat16)
+        ).astype(jnp.bfloat16)
         return carry
 
     lax.fori_loop(0, count, convolve, 0)
 
-    gather.forward()
     for k in range(1, count):
         there = lax.rem(own + k, count)
         copy = remote(
@@ -460,28 +486,39 @@
         )
         copy.start()
         copies.append(copy)
-    total = part_ref[own]
+    total = part_ref[own].astype(jnp.float32)
     for k in range(1, count):
         remote(
             part_ref.at[own], partial_ref.at[k], send_rs.at[k], recv_rs.at[k], line, partner
         ).wait_recv()
-        total = total + partial_ref[k]
-    selected_ref[own] = total
+        total = total + partial_ref[k].astype(jnp.float32)
+    total_ref[own] = total.astype(jnp.bfloat16)
     for k in range(1, count):
         copy = remote(
-            selected_ref.at[own], selected_ref.at[own], send_ag.at[k], recv_ag.at[k],
+            total_ref.at[own], total_ref.at[own], send_ag.at[k], recv_ag.at[k],
             line, lax.rem(own + k, count),
         )
         copy.start()
         copies.append(copy)
+    gather.forward(0)
+    gather.forward(1)
     for k in range(1, count):
         block = lax.rem(own - k + count, count)
         remote(
-            selected_ref.at[block], selected_ref.at[block], send_ag.at[k], recv_ag.at[k],
+            total_ref.at[block], total_ref.at[block], send_ag.at[k], recv_ag.at[k],
             line, partner,
         ).wait_recv()
+    selected_ref[...] = total_ref[...].astype(jnp.float32)[:, : cuts.picks]
     for copy in copies:
         copy.wait_send()
+    for i in range(half):
+        cross(i).wait_send()
+        for up in (True, False):
+
+            @pl.when(can_go(up) & (i <= high if up else i >= high))
+            def _(i=i, up=up):
+                step_on(i, up).wait_send()
+
     gather.finish()
 
 
@@ -514,10 +551,9 @@
             jax.ShapeDtypeStruct((count, expert.shape[0], expert.shape[1] // 2), jnp.bfloat16),
         ],
         scratch_shapes=[
-            pltpu.VMEM((count, cuts.picks, rows), jnp.float32),
-            pltpu.VMEM((count, cuts.picks, rows), jnp.float32),
+            *[pltpu.VMEM((count, cuts.sent, rows), jnp.bfloat16)] * 3,
             dma((lines,)), dma((lines,)), dma((half,)), dma((half,)), dma((half,)), dma((half,)),
-            dma((count,)), dma((count,)), dma((count,)), dma((count,)),
+            dma((half,)), dma((count,)), dma((count,)), dma((count,)), dma((count,)),
             *gather_scratch(count),
         ],
         compiler_params=pltpu.CompilerParams(
@@ -532,11 +568,31 @@
     )(normed, packed, expert)
 
 
+def spread_lanes(values, wide_ref, out_ref):
+    state, steps = values.shape
+    high = values.astype(jnp.bfloat16).astype(jnp.float32)
+    rest = values - high
+    lane = lax.broadcasted_iota(jnp.int32, (state, steps), 1)
+
+    def fill(g, carry):
+        for k in range(8):
+            t = g * 8 + k
+            here = pl.ds(pl.multiple_of(t * state, state), state)
+            mask = lane == t
+            wide_ref[here, :steps] = jnp.where(mask, high, 0.0).astype(jnp.bfloat16)
+            wide_ref[here, steps:] = jnp.where(mask, rest, 0.0).astype(jnp.bfloat16)
+        return carry
+
+    lax.fori_loop(0, steps // 8, fill, 0)
+    ones = jnp.ones((2 * steps, LANES), jnp.bfloat16)
+    out_ref[...] = dot_nn(wide_ref[...], ones)
+
+
 def scan_forward_kernel(
     count, cuts,
     act_ref, gate_ref, selected_ref, small_ref, output_ref, expert_ref,
     pre_ref, mixed_ref, mixer_low_ref, prior_ref, end_ref, summed_ref, expert_out_ref,
-    state_ref, delta_ref, scanned_ref, land_ref, *refs,
+    state_ref, delta_ref, scanned_ref, wide_ref, wide_in_ref, wide_out_ref, land_ref, *refs,
 ):
     steps, inner = act_ref.shape
     tiles = inner // LANES
@@ -552,14 +608,13 @@
         gather.start()
         state_ref[...] = jnp.zeros_like(state_ref)
 
-    @pl.when(step == 1)
+    @pl.when(step == 0)
     def _():
         gather.spread(0)
+
+    @pl.when(step == 3)
+    def _():
         gather.spread(1)
-
-    @pl.when(step == count // 2)
-    def _():
-        gather.forward()
 
     rates2 = -LOG2E * jnp.exp(small_ref[cuts.decay : cuts.decay + state, :])
     pre = inner_rows(
@@ -571,25 +626,19 @@
     delta_ref[...] = softplus(pre)
     in_rows = cuts.rank
     out_rows = cuts.rank + state
+    spread_lanes(selected_ref[0, in_rows : in_rows + state, :], wide_ref, wide_in_ref)
+    spread_lanes(selected_ref[0, out_rows : out_rows + state, :], wide_ref, wide_out_ref)
 
     def group(g, states):
         states = [list(s) for s in states]
         base = pl.multiple_of(g * 8, 8)
-        shift = lax.rem(steps - base, steps)
-        b_cols = [
-            pltpu.roll(selected_ref[0, in_rows + 8 * i : in_rows + 8 * i + 8, :], shift, 1)
-            for i in range(halves)
-        ]
-        c_cols = [
-            pltpu.roll(selected_ref[0, out_rows + 8 * i : out_rows + 8 * i + 8, :], shift, 1)
-            for i in range(halves)
-        ]
         d8 = delta_ref[pl.ds(base, 8), :]
         du8 = d8 * act_ref[pl.ds(base, 8), :]
         parts = [[None] * 8 for _ in range(tiles)]
         for k in range(8):
-            b_now = [lane_column(b, k) for b in b_cols]
-            c_now = [lane_column(c, k) for c in c_cols]
+            rows_now = [pl.ds((base + k) * state + 8 * i, 8) for i in range(halves)]
+            b_now = [wide_in_ref[here, :] for here in rows_now]
+            c_now = [wide_out_ref[here, :] for here in rows_now]
             for j in range(tiles):
                 cols = slice(j * LANES, (j + 1) * LANES)
                 d = jnp.broadcast_to(d8[k : k + 1, cols], (8, LANES))
@@ -630,14 +679,16 @@
     def pass_on(block):
         relay.pass_on(block // 2, lax.rem(block, 2))
 
-    @pl.when(step >= 2)
+    @pl.when(step >= LAG)
     def _():
-        pass_on(step - 2)
+        pass_on(step - LAG)
 
     @pl.when(step == count - 1)
     def _():
-        pass_on(step - 1)
-        pass_on(step)
+        for late in range(LAG - 1, -1, -1):
+            pass_on(step - late)
+        gather.forward(0)
+        gather.forward(1)
         summed_ref[...] = relay.finish()
         gather.finish()
         expert_out_ref[...] = land_ref[...]
@@ -683,6 +734,9 @@
             pltpu.VMEM((state, inner), jnp.float32),
             pltpu.VMEM((block, inner), jnp.float32),
             pltpu.VMEM((block, inner), jnp.float32),
+            pltpu.VMEM((block * state, 2 * block), jnp.bfloat16),
+            pltpu.VMEM((block * state, LANES), jnp.float32),
+            pltpu.VMEM((block * state, LANES), jnp.float32),
             pltpu.VMEM(pieces, jnp.bfloat16),
             *relay_scratch(count, block, width),
             *gather_scratch(count),
@@ -705,8 +759,9 @@
     prior_ref, end_ref, expert_ref,
     grad_gate_ref, grad_act_ref, grad_step_ref, rate_total_ref, rows_ref, grad_selected_ref,
     all_out_ref, expert_out_ref,
-    incoming_ref, post_ref, delta_ref, grad_ref, grad_delta_ref, all_ref,
-    part_ref, partial_ref, total_ref,
+    incoming_ref, post_ref, delta_ref, grad_ref, grad_delta_ref, wide_ref, wide_in_ref,
+    wide_out_ref, all_ref,
+    stage_ref, part_ref, partial_ref, total_ref,
     send_hi, recv_hi, send_x, recv_x, send_rs, recv_rs, send_ag, recv_ag,
     other_ref, held_ref, swap_s, swap_r, *scatter_refs,
 ):
@@ -755,6 +810,7 @@
         rate_total_ref[...] = jnp.zeros_like(rate_total_ref)
         grad_step_ref[...] = jnp.zeros_like(grad_step_ref)
         rows_ref[...] = jnp.zeros_like(rows_ref)
+        stage_ref[...] = jnp.zeros_like(stage_ref)
 
     @pl.when(index == jnp.maximum(count - 3 - own, 0))
     def _():
@@ -784,6 +840,8 @@
     rates2 = -LOG2E * jnp.exp(small_ref[cuts.decay : cuts.decay + state, :])
     in_rows = cuts.rank
     out_rows = cuts.rank + state
+    spread_lanes(selected_ref[0, in_rows : in_rows + state, :], wide_ref, wide_in_ref)
+    spread_lanes(selected_ref[0, out_rows : out_rows + state, :], wide_ref, wide_out_ref)
 
     def tile_of(ref):
         return tuple(
@@ -798,15 +856,6 @@
         rate_total = [list(s) for s in rate_total]
         in_acc, out_acc = list(in_acc), list(out_acc)
         base = pl.multiple_of((steps // 8 - 1 - turn) * 8, 8)
-        shift = lax.rem(steps - base, steps)
-        b_cols = [
-            pltpu.roll(selected_ref[0, in_rows + 8 * i : in_rows + 8 * i + 8, :], shift, 1)
-            for i in range(halves)
-        ]
-        c_cols = [
-            pltpu.roll(selected_ref[0, out_rows + 8 * i : out_rows + 8 * i + 8, :], shift, 1)
-            for i in range(halves)
-        ]
         d8 = delta_ref[pl.ds(base, 8), :]
         u8 = act_ref[pl.ds(base, 8), :]
         du8 = d8 * u8
@@ -814,8 +863,9 @@
         rate_parts = [[None] * 8 for _ in range(tiles)]
         side_parts = [[None] * 8 for _ in range(tiles)]
         for k in range(7, -1, -1):
-            b_now = [lane_column(b, k) for b in b_cols]
-            c_now = [lane_column(c, k) for c in c_cols]
+            rows_now = [pl.ds((base + k) * state + 8 * i, 8) for i in range(halves)]
+            b_now = [wide_in_ref[here, :] for here in rows_now]
+            c_now = [wide_out_ref[here, :] for here in rows_now]
             in_sum = [None] * halves
             out_sum = [None] * halves
             for j in range(tiles):
@@ -871,8 +921,8 @@
         (tile_of(incoming_ref), tile_of(post_ref), tile_of(rate_total_ref), empty, empty),
     )
     for i in range(halves):
-        part_ref[now, in_rows + 8 * i : in_rows + 8 * i + 8, :] = in_acc[i]
-        part_ref[now, out_rows + 8 * i : out_rows + 8 * i + 8, :] = out_acc[i]
+        stage_ref[in_rows + 8 * i : in_rows + 8 * i + 8, :] = in_acc[i]
+        stage_ref[out_rows + 8 * i : out_rows + 8 * i + 8, :] = out_acc[i]
         for j in range(tiles):
             cols = slice(j * LANES, (j + 1) * LANES)
             incoming_ref[8 * i : 8 * i + 8, cols] = incoming[j][i]
@@ -883,9 +933,10 @@
     grad_pre = grad_delta_ref[...] * sigmoid(pre_ref[...])
     rows_ref[0:1, :] += jnp.sum(grad_pre, axis=0, keepdims=True)
     grad_step_ref[...] += dot_nn(selected_ref[0, : cuts.rank, :], grad_pre, HIGHEST)
-    part_ref[now, : cuts.rank, :] = outer_cols(
+    stage_ref[: cuts.rank, :] = outer_cols(
         small_ref[cuts.step : cuts.step + cuts.rank, :], grad_pre, HIGHEST
     )
+    part_ref[now] = stage_ref[...].astype(jnp.bfloat16)
 
     def partial_to(block):
         return remote(
@@ -906,29 +957,33 @@
     def _():
         hand_over(now - 2)
 
-    @pl.when(index == 1)
+    @pl.when(index == FAR_AT)
     def _():
-        scatter.start()
-
-    @pl.when(index == count // 2)
+        scatter.send_far()
+
+    @pl.when(index == NEAR_AT)
     def _():
-        scatter.pass_on()
-
-    @pl.when(index == count - 2)
+        scatter.send_near()
+
+    @pl.when(index == count // 2 + PASS_AFTER)
+    def _():
+        scatter.pass_far()
+
+    @pl.when(index == count - 1)
     def _():
         scatter.hand_over()
 
     @pl.when(index == jnp.minimum(count - 1 - own + 2, count - 1))
     def _():
-        total = part_ref[own]
+        total = part_ref[own].astype(jnp.float32)
         for k in range(1, count):
             there = lax.rem(own + k, count)
             remote(
                 part_ref.at[own], partial_ref.at[there], send_rs.at[own], recv_rs.at[there],
                 line, there,
             ).wait_recv()
-            total = total + partial_ref[there]
-        total_ref[own] = total
+            total = total + partial_ref[there].astype(jnp.float32)
+        total_ref[own] = total.astype(jnp.bfloat16)
         for k in range(1, count):
             total_to(k).start()
 
@@ -967,7 +1022,7 @@
     rows = pl.BlockSpec((block, inner), lambda t: (back(t), 0))
     whole = pl.BlockSpec((state, inner), lambda t: (0, 0))
     dma = pltpu.SemaphoreType.DMA
-    picked = (count, cuts.picks, block)
+    picked = (count, cuts.sent, block)
     return pl.pallas_call(
         functools.partial(scan_backward_kernel, count, cuts),
         grid=(count,),
@@ -1000,7 +1055,7 @@
             jax.ShapeDtypeStruct((cuts.rank, inner), jnp.float32),
             jax.ShapeDtypeStruct((state, inner), jnp.float32),
             jax.ShapeDtypeStruct((8, inner), jnp.float32),
-            jax.ShapeDtypeStruct(picked, jnp.float32),
+            jax.ShapeDtypeStruct(picked, jnp.bfloat16),
             jax.ShapeDtypeStruct((count, block, width), jnp.bfloat16),
             jax.ShapeDtypeStruct((expert.shape[1], 2 * expert.shape[2]), jnp.float32),
         ],
@@ -1010,10 +1065,12 @@
             pltpu.VMEM((block, inner), jnp.float32),
             pltpu.VMEM((block, inner), jnp.float32),
             pltpu.VMEM((block, inner), jnp.float32),
+            pltpu.VMEM((block * state, 2 * block), jnp.bfloat16),
+            pltpu.VMEM((block * state, LANES), jnp.float32),
+            pltpu.VMEM((block * state, LANES), jnp.float32),
             pltpu.VMEM((count, block, width), jnp.bfloat16),
-            pltpu.VMEM(picked, jnp.float32),
-            pltpu.VMEM(picked, jnp.float32),
-            pltpu.VMEM(picked, jnp.float32),
+            pltpu.VMEM(picked[1:], jnp.float32),
+            *[pltpu.VMEM(picked, jnp.bfloat16)] * 3,
             dma((half,)), dma((half,)), dma((half,)), dma((half,)),
             dma((count,)), dma((count,)), dma((count,)), dma((count,)),
             *scatter_scratch(count, expert.shape[1], expert.shape[2]),
@@ -1049,20 +1106,20 @@
     kernel = cuts.kernel
     shard = shard_ref.shape[0]
     greet(count, lines)
-    scatter.start()
+    scatter.send_far()
     grad_small_ref[...] = jnp.zeros_like(grad_small_ref)
     grad_sum_ref[length:, :] = jnp.zeros((8, inner), jnp.float32)
-    select = small_ref[: cuts.picks, :].astype(jnp.bfloat16)
+    select = small_ref[: cuts.sent, :].astype(jnp.bfloat16)
 
     def first(b, carry):
         start = pl.multiple_of(b * rows, rows)
-        grad_selected = grad_selected_ref[b].astype(jnp.bfloat16)
+        grad_selected = grad_selected_ref[b]
         total = sum_ref[pl.ds(start, rows), :]
         sig = sigmoid(total)
         grad_act = grad_act_ref[pl.ds(start, rows), :] + inner_rows(grad_selected, select)
         grad_sum = grad_act * (sig * (1.0 + total * (1.0 - sig)))
         grad_sum_ref[pl.ds(start, rows), :] = grad_sum
-        grad_small_ref[: cuts.picks, :] += dot_nn(
+        grad_small_ref[: cuts.sent, :] += dot_nn(
             grad_selected, (total * sig).astype(jnp.bfloat16)
         )
         window = ext_ref[pl.ds(start, rows + 8), :]
@@ -1099,7 +1156,8 @@
         return carry
 
     lax.fori_loop(0, count, second, 0)
-    scatter.pass_on()
+    scatter.send_near()
+    scatter.pass_far()
 
     decay = slice(cuts.decay, cuts.decay + cuts.state)
     grad_small_ref[cuts.step : cuts.step + cuts.rank, :] = grad_step_ref[...]
@@ -1217,6 +1275,10 @@
     )(*args)
 
 
+LAG = 3
+FAR_AT = 0
+NEAR_AT = 2
+PASS_AFTER = 0
 SLOTS = 64
 
 

time: 594 us -> 548 us (0.923)
  Pallas kernels: 562 us -> 516 us
    pallas_call x1, Pallas kernels: 159 us -> 134 us  [scan_backward(): pl.pallas_call(functools.partial(scan_backward_kernel, count, cuts), grid...]
    pallas_call x1, Pallas kernels: 91.2 us -> 78.1 us  [scan_forward(): pl.pallas_call(functools.partial(scan_forward_kernel, count, cuts), grid=...]
    pallas_call x1, Pallas kernels: 133 us -> 125 us  [back(): pl.pallas_call(functools.partial(back_kernel, count, lines, cuts), in_spe...]
where the time goes in v5:
time: 548 us; the launch traced here: 547 us
  Pallas kernels  516 us (94%)
  local copies, waits for them, and re-layouts  18.3 us (3%)
  other arithmetic  10.7 us (2%)
    pallas_call x1, Pallas kernels, scan_backward(): pl.pallas_call(functools.partial(scan_backward_kernel, count, cuts), grid...  134 us
    pallas_call x1, Pallas kernels, back(): pl.pallas_call(functools.partial(back_kernel, count, lines, cuts), in_spe...  125 us
    pallas_call x1, Pallas kernels, front(): pl.pallas_call(functools.partial(front_kernel, count, lines, cuts), in_sp...  106 us
    pallas_call x1, Pallas kernels, scan_forward(): pl.pallas_call(functools.partial(scan_forward_kernel, count, cuts), grid=...  78.1 us
    pallas_call x1, Pallas kernels, run_experts(): pl.pallas_call(functools.partial(experts_kernel, count, lines, experts),...  72.9 us

profile of v5, /device:TPU:31, one launch (start us, length us, event | category | flops | bytes accessed | tf_op | source)
XLA Modules:
  0.0 546.8 jit_solution(656451940315670159)
XLA Ops:
  0.6 0.0 copy-start
  0.7 1.1 fusion.3
  1.7 0.0 copy-start.9
  1.7 1.2 multiply_reduce_fusion.1
  3.0 0.7 fusion.12
  3.6 0.7 convert_add_fusion
  4.3 1.3 reshape.120.gain_ref
  5.6 0.7 convert_element_type.40
  6.3 0.8 copy.48
  7.1 0.8 copy.49
  7.8 0.8 copy.46
  8.6 0.8 copy.50
  9.4 0.8 copy.47
  10.2 0.8 copy.51
  11.0 0.8 concatenate.6
  11.8 0.7 fusion.9.table_ref
  12.5 1.4 fusion.10.chosen_ref
  13.8 0.8 fusion.8.back_table_ref
  14.6 0.8 multiply_convert_fusion.normed_ref
  15.4 0.7 pad.14.router_ref
  16.2 0.9 fusion.5.packed_ref
  17.1 106.3 %front.1 = (bf16[8,128,1152]{2,1,0:T(8,128)(2,1)}, bf16[384,3712]{1,0:T(8,128)(2,1)}, f32[256,384]{1,0:T(8,128)}, f32[1032,384]{1,0:T(8,128)}, f32[1024,384]{1,0...) custom-call(bf16[128,1152]{1,0:T(8,128)(2,1)} %multiply_convert_fusi, ...), custom_call_target="tpu_custom_call" | custom-call | flops 1811939328 | bytes 7864320 | tf_op jit(solution)/shard_map/front/pallas_call | solution.py:538
  123.3 78.1 %scan_forward.1 = (f32[1024,384]{1,0:T(8,128)}, f32[1024,384]{1,0:T(8,128)}, bf16[1024,384]{1,0:T(8,128)(2,1)}, f32[1024,16,384]{2,1,0:T(8,128)}, f32[16,384]{1,...) custom-call(f32[1024,384]{1,0:T(8,128)} %get-tuple-element.50.act_ref, ...), custom_call_target="tpu_custom_call" | custom-call | flops 50331648 | bytes 34603008 | tf_op jit(solution)/shard_map/scan_forward/pallas_call | solution.py:704
  201.4 72.9 %experts.1 = (f32[128,1152]{1,0:T(8,128)}, f32[128,1152]{1,0:T(8,128)}, bf16[128,1152]{1,0:T(8,128)(2,1)}, f32[8,1152]{1,0:T(8,128)}, bf16[8,144,1536]{2,1,0:T(8,128)(2,1)}, /*index=5*/bf16[8,144,1536]{2,1,0:T(8,128)(2,1)}) custom-call(f32[128,1152]{1,0:T(8,128)} %bitcast.39, f32[128,1152]{1,0:T(8,128)} %get-tuple-element.55.mixer_ref, ...), custom_call_target="tpu_custom_call" | custom-call | flops 10871635968 | bytes 14155776 | tf_op jit(solution)/shard_map/experts/pallas_call | solution.py:1494
  274.3 133.9 %scan_backward.1 = (bf16[1024,384]{1,0:T(8,128)(2,1)}, f32[1024,384]{1,0:T(8,128)}, f32[72,384]{1,0:T(8,128)}, f32[16,384]{1,0:T(8,128)}, f32[8,384]{1,0:T(8,128...) custom-call(bf16[128,1152]{1,0:T(8,128)(2,1)} %get-tuple-element.60.own_ref, ...), custom_call_target="tpu_custom_call" | custom-call | flops 125829120 | bytes 34603008 | tf_op jit(solution)/shard_map/scan_backward/pallas_call | solution.py:1026
  408.2 0.0 copy-start.1
  408.2 124.8 %back.1 = (f32[128,1152]{1,0:T(8,128)}, f32[80,3712]{1,0:T(8,128)}, f32[8,1152]{1,0:T(8,128)}, f32[144,3072]{1,0:T(8,128)}) custom-call(bf16[8,112,128]{2,1,0:T(8,128)(2,1)} %get-tuple-element.66.grad_selected_ref, f32[256,384]{1,0:T(8,128)} %get-tuple-element.53.small_ref, bf16[384,3712]{1,0:T(8,128)(2,1)} %get-tuple-element.54.output_ref.weights_ref, ...), custom_call_target="tpu_custom_call" | custom-call | flops 4529848320 | bytes 11796480 | tf_op jit(solution)/shard_map/back/pallas_call | solution.py:1245
  533.0 0.0 copy-start.11
  533.1 1.4 multiply_reduce_fusion
  534.4 1.0 fusion.7
  535.4 0.6 slice_reduce_fusion.3
  536.1 0.6 slice.55
  536.7 0.6 convert_divide_fusion
  537.3 0.7 slice_reduce_fusion
  538.0 0.1 slice.59
  538.1 0.7 copy.55
  538.8 0.6 slice.58
  539.4 0.1 slice.61
  539.5 0.1 slice.56
  539.6 0.7 copy.54
  540.3 0.7 copy.56
  540.9 0.7 slice.53
  541.7 0.9 copy.61
  542.6 0.8 copy.65
  543.4 0.1 copy-done.4
  543.5 1.2 copy.66
  544.7 0.9 copy-done.3
  545.6 1.2 copy.67
  (27 shorter events, 0.2 us)
Async XLA Ops:
  0.6 14.0 %copy-start = (f32[1,128,1152]{2,1,0:T(8,128)S(1)}, f32[1,128,1152]{2,1,0:T(8,128)}, u32[]{:S(2)}) copy-start(f32[1,128,1152]{2,1,0:T(8,128)} %param.17) | copy-start | bytes 1769476
  0.7 14.8 %copy-start.12 = (bf16[4,1152]{1,0:T(4,128)(2,1)S(1)}, bf16[4,1152]{1,0:T(4,128)(2,1)}, u32[]{:S(2)}) copy-start(bf16[4,1152]{1,0:T(4,128)(2,1)} %param.31) | copy-start | bytes 27652
  0.7 15.5 %copy-start.8 = (bf16[2,1152,72]{1,2,0:T(8,128)(2,1)S(1)}, bf16[2,1152,72]{1,2,0:T(8,128)(2,1)}, u32[]{:S(2)}) copy-start(bf16[2,1152,72]{1,2,0:T(8,128)(2,1)} %param.21) | copy-start | bytes 995332
  1.7 14.5 %copy-start.9 = (bf16[72,1152]{1,0:T(8,128)(2,1)S(1)}, bf16[72,1152]{1,0:T(8,128)(2,1)}, u32[]{:S(2)}) copy-start(bf16[72,1152]{1,0:T(8,128)(2,1)} %param.29) | copy-start | bytes 497668
  408.2 124.8 %copy-start.1 = (f32[1,128,1152]{2,1,0:T(8,128)S(1)}, f32[1,128,1152]{2,1,0:T(8,128)}, u32[]{:S(2)}) copy-start(f32[1,128,1152]{2,1,0:T(8,128)} %param.17) | copy-start | bytes 1769476
  533.0 1.4 copy-start.2
  533.0 1.4 copy-start.7
  533.0 2.4 copy-start.10
  533.0 3.6 copy-start.11
  533.1 4.2 copy-start.5
  540.9 1.7 copy-start.6
  541.7 1.8 copy-start.4
  543.5 2.1 copy-start.3

commit v6 on v5

--- a/solution.py
+++ b/solution.py
@@ -14,10 +14,6 @@
 LOG2E = math.log2(math.e)
 
 HIGHEST = lax.Precision.HIGHEST
-
-
-def rms_norm(values, gain):
-    return values * lax.rsqrt(jnp.mean(values * values, axis=-1, keepdims=True) + 1e-05) * gain
 
 
 def inner_rows(left, right, precision=None):
@@ -164,12 +160,12 @@
             self.across[i] = self.summed(i).astype(jnp.bfloat16)
             self.on(i).start()
 
-    def finish(self):
+    def finish(self, sent=None):
         total = self.summed(self.high)
         for k in range(1, self.half):
             self.on(lax.rem(self.high + k, self.half)).wait_recv()
             total = total + self.along[k].astype(jnp.float32)
-        for i in range(self.half):
+        for i in range(self.half) if sent is None else sent:
             self.over(i, 1 - self.low).wait_send()
         for k in range(1, self.half):
             self.on(lax.rem(self.high + k, self.half)).wait_send()
@@ -286,11 +282,11 @@
 
 
 class Scatter:
-    def __init__(self, count, part_ref, other_ref, held_ref, swap_s, swap_r, refs):
+    def __init__(self, count, part_ref, far_ref, other_ref, held_ref, swap_s, swap_r, refs):
         self.line = lax.axis_index("dp")
         self.q, self.f, self.low = square()
         self.quarter = count // 4
-        self.other, self.held = other_ref, held_ref
+        self.far, self.other, self.held = far_ref, other_ref, held_ref
         self.swap_s, self.swap_r = swap_s, swap_r
         self.relays = []
         for j in range(2):
@@ -313,37 +309,41 @@
             seat_of(self.q, 1 - self.f, self.low),
         )
 
-    def turns(self):
-        far = [(j, lax.rem(self.q + k, self.quarter)) for k in range(1, self.quarter) for j in (1, 0)]
-        return far + [(1, self.q), (0, self.q)]
-
-    def send(self, turn):
-        j, i = self.turns()[turn]
-        self.relays[j].over(i, 1 - self.low).start()
-
-    def pass_on(self, turn):
-        j, i = self.turns()[turn]
-        self.relays[j].pass_on(i, self.low)
+    def far_places(self):
+        return [
+            (j, lax.rem(self.q + k, self.quarter)) for k in range(1, self.quarter) for j in (1, 0)
+        ]
 
     def send_far(self):
-        for turn in range(2 * self.quarter - 2):
-            self.send(turn)
+        for j, i in self.far_places():
+            self.relays[j].over(i, 1 - self.low).start()
 
     def pass_far(self):
-        for turn in range(2 * self.quarter - 2):
-            self.pass_on(turn)
+        for j, i in self.far_places():
+            relay = self.relays[j]
+            if self.far is None:
+                relay.pass_on(i, self.low)
+            else:
+                both = relay.part[relay.block(i, self.low)].astype(jnp.float32) + self.far[
+                    j, i
+                ].astype(jnp.float32)
+                relay.across[i] = both.astype(jnp.bfloat16)
+                relay.on(i).start()
+
+    def total(self, j):
+        return self.relays[j].finish(None if self.far is None else [self.q])
 
     def send_near(self):
-        self.send(2 * self.quarter - 2)
-        self.send(2 * self.quarter - 1)
+        for j in (1, 0):
+            self.relays[j].over(self.q, 1 - self.low).start()
 
     def hand_over(self):
-        self.held[...] = self.relays[1].finish().astype(jnp.bfloat16)
+        self.held[...] = self.total(1).astype(jnp.bfloat16)
         self.swap().start()
 
     def finish(self, out_ref):
         cut = self.held.shape[1]
-        out_ref[:, pl.ds(pl.multiple_of(self.f * cut, LANES), cut)] = self.relays[0].finish()
+        out_ref[:, pl.ds(pl.multiple_of(self.f * cut, LANES), cut)] = self.total(0)
         self.swap().wait_recv()
         out_ref[:, pl.ds(pl.multiple_of((1 - self.f) * cut, LANES), cut)] = self.other[...].astype(
             jnp.float32
@@ -366,20 +366,49 @@
 
 def front_kernel(
     count, lines, cuts,
-    normed_ref, packed_ref, expert_ref,
+    x_ref, gain_ref, input_ref, output_ref, select_ref, step_ref, decay_ref, taps_ref, conv_bias_ref,
+    step_bias_ref, skip_ref, expert_ref,
     all_ref, weights_ref, small_ref, ext_ref, sum_ref, act_ref, gate_ref, selected_ref, land_ref,
-    part_ref, partial_ref, total_ref,
+    normed_ref, packed_ref, table_ref, part_ref, partial_ref, total_ref,
     send_w, recv_w, send_up, send_down, recv_hi, send_x, recv_x, send_rs, recv_rs, send_ag, recv_ag,
     *gather_refs,
 ):
     line, own, high, low = place()
     half = count // 2
     gather = Gather(count, expert_ref, land_ref, *gather_refs)
-    rows, width = normed_ref.shape
+    rows, width = x_ref.shape
     shard = packed_ref.shape[0]
     inner = weights_ref.shape[0]
     kernel = cuts.kernel
     partner = 2 * high + 1 - low
+
+    own_shard = output_ref.shape[0]
+    extra = jnp.zeros((shard - own_shard, width), jnp.float32)
+
+    def padded(values):
+        return jnp.concatenate([values.astype(jnp.float32), extra], axis=0).astype(jnp.bfloat16)
+
+    packed_ref[:, :width] = padded(input_ref[0])
+    packed_ref[:, width : 2 * width] = padded(input_ref[1])
+    packed_ref[:, 2 * width : 3 * width] = padded(output_ref[...])
+    table_ref[...] = jnp.zeros_like(table_ref)
+    table_ref[:own_shard, : cuts.picks] = select_ref[...].astype(jnp.float32)
+    picked = table_ref[:LANES, :].T
+    table_ref[...] = jnp.zeros_like(table_ref)
+    table_ref[:LANES, :] = picked
+    for at, ref in (
+        (cuts.step, step_ref),
+        (cuts.decay, decay_ref),
+        (cuts.taps, taps_ref),
+        (cuts.conv_bias, conv_bias_ref),
+        (cuts.step_bias, step_bias_ref),
+        (cuts.skip, skip_ref),
+    ):
+        table_ref[at : at + ref.shape[0], :own_shard] = ref[...].astype(jnp.float32)
+    packed_ref[:, 3 * width :] = table_ref[...].T[:shard].astype(jnp.bfloat16)
+    x = x_ref[...]
+    scale = lax.rsqrt(jnp.mean(x * x, axis=1, keepdims=True) + 1e-05)
+    normed_ref[...] = (x * scale * gain_ref[...]).astype(jnp.bfloat16)
     greet(count, lines)
 
     copies = []
@@ -522,13 +551,13 @@
     gather.finish()
 
 
-def front(count, lines, cuts, normed, packed, expert):
-    rows, width = normed.shape
-    shard, columns = packed.shape
+def front(count, lines, cuts, shard, small, *args):
+    rows, width = args[0].shape
+    expert = args[-1]
+    columns = 3 * width + small
     inner = -(-lines * shard // LANES) * LANES
     length = count * rows
     half = count // 2
-    small = columns - 3 * width
     vmem = pl.BlockSpec(memory_space=pltpu.VMEM)
 
     def f32(*shape):
@@ -537,7 +566,7 @@
     dma = pltpu.SemaphoreType.DMA
     return pl.pallas_call(
         functools.partial(front_kernel, count, lines, cuts),
-        in_specs=[vmem] * 3,
+        in_specs=[vmem] * len(args),
         out_specs=[vmem] * 9,
         out_shape=[
             jax.ShapeDtypeStruct((count, rows, width), jnp.bfloat16),
@@ -551,6 +580,9 @@
             jax.ShapeDtypeStruct((count, expert.shape[0], expert.shape[1] // 2), jnp.bfloat16),
         ],
         scratch_shapes=[
+            pltpu.VMEM((rows, width), jnp.bfloat16),
+            pltpu.VMEM((shard, columns), jnp.bfloat16),
+            pltpu.VMEM((small, LANES), jnp.float32),
             *[pltpu.VMEM((count, cuts.sent, rows), jnp.bfloat16)] * 3,
             dma((lines,)), dma((lines,)), dma((half,)), dma((half,)), dma((half,)), dma((half,)),
             dma((half,)), dma((count,)), dma((count,)), dma((count,)), dma((count,)),
@@ -565,7 +597,7 @@
             transcendentals=length * inner,
         ),
         name="front",
-    )(normed, packed, expert)
+    )(*args)
 
 
 def spread_lanes(values, wide_ref, out_ref):
@@ -775,7 +807,9 @@
     partner = 2 * high + 1 - low
     index = pl.program_id(0)
     now = count - 1 - index
-    scatter = Scatter(count, expert_ref, other_ref, held_ref, swap_s, swap_r, scatter_refs)
+    scatter = Scatter(
+        count, expert_ref, None, other_ref, held_ref, swap_s, swap_r, scatter_refs
+    )
 
     def along(k):
         return remote(
@@ -957,15 +991,15 @@
     def _():
         hand_over(now - 2)
 
+    @pl.when(index == NEAR_AT)
+    def _():
+        scatter.send_near()
+
     @pl.when(index == FAR_AT)
     def _():
         scatter.send_far()
 
-    @pl.when(index == NEAR_AT)
-    def _():
-        scatter.send_near()
-
-    @pl.when(index == count // 2 + PASS_AFTER)
+    @pl.when(index == PASS_AT)
     def _():
         scatter.pass_far()
 
@@ -1091,12 +1125,13 @@
     count, lines, cuts,
     grad_selected_ref, small_ref, weights_ref, ext_ref, sum_ref, grad_act_ref, grad_gate_ref,
     mixer_low_ref, normed_ref, grad_middle_ref, grad_step_ref, rate_total_ref, scan_rows_ref,
-    vectors_ref, expert_ref,
-    summed_ref, shard_ref, totals_ref, expert_out_ref,
+    vectors_ref, expert_ref, far_ref, x_ref, gain_ref, kept_ref,
+    tokens_ref, input_ref, output_ref, select_ref, step_ref, decay_ref, taps_ref, conv_bias_ref,
+    step_bias_ref, skip_ref, totals_ref, expert_out_ref,
     grad_sum_ref, grad_conv_ref, grad_small_ref, ours_ref, theirs_ref,
     send_v, recv_v, send_u, recv_u, other_ref, held_ref, swap_s, swap_r, *refs,
 ):
-    scatter = Scatter(count, expert_ref, other_ref, held_ref, swap_s, swap_r, refs[:6])
+    scatter = Scatter(count, expert_ref, far_ref, other_ref, held_ref, swap_s, swap_r, refs[:6])
     relay = whole_relay("seq", count, refs[6:13])
     spread = whole_relay("dp", lines, refs[13:])
     line, own, _, _ = place()
@@ -1104,9 +1139,11 @@
     width = normed_ref.shape[1]
     rows = length // count
     kernel = cuts.kernel
-    shard = shard_ref.shape[0]
+    shard = spread.part.shape[1]
+    own_shard = output_ref.shape[0]
     greet(count, lines)
-    scatter.send_far()
+    scatter.pass_far()
+    scatter.send_near()
     grad_small_ref[...] = jnp.zeros_like(grad_small_ref)
     grad_sum_ref[length:, :] = jnp.zeros((8, inner), jnp.float32)
     select = small_ref[: cuts.sent, :].astype(jnp.bfloat16)
@@ -1156,8 +1193,6 @@
         return carry
 
     lax.fori_loop(0, count, second, 0)
-    scatter.send_near()
-    scatter.pass_far()
 
     decay = slice(cuts.decay, cuts.decay + cuts.state)
     grad_small_ref[cuts.step : cuts.step + cuts.rank, :] = grad_step_ref[...]
@@ -1223,14 +1258,39 @@
     for d in range(lines):
         spread.pass_on(d // 2, d % 2)
     totals_ref[...] = sum_over(lines, "dp", send_u, recv_u)
-    summed_ref[...] = relay.finish()
-    shard_ref[...] = spread.finish()
+    x = x_ref[...]
+    scale = lax.rsqrt(jnp.mean(x * x, axis=1, keepdims=True) + 1e-05)
+    scaled = gain_ref[...] * relay.finish()
+    tokens_ref[...] = (
+        kept_ref[...]
+        + scale * scaled
+        - x * (scale * scale * scale) * jnp.mean(scaled * x, axis=1, keepdims=True)
+    )
+    total = spread.finish()
+    input_ref[0] = total[:own_shard, :width]
+    input_ref[1] = total[:own_shard, width : 2 * width]
+    output_ref[...] = total[:own_shard, 2 * width : 3 * width]
+    small = total[:, 3 * width :]
+    select_ref[...] = small[:own_shard, : cuts.picks]
+    small = jnp.concatenate(
+        [small, jnp.zeros((LANES - shard, small.shape[1]), jnp.float32)], axis=0
+    ).T
+    for at, ref in (
+        (cuts.step, step_ref),
+        (cuts.decay, decay_ref),
+        (cuts.taps, taps_ref),
+        (cuts.conv_bias, conv_bias_ref),
+        (cuts.step_bias, step_bias_ref),
+        (cuts.skip, skip_ref),
+    ):
+        ref[...] = small[at : at + ref.shape[0], :own_shard]
     scatter.finish(expert_out_ref)
 
 
 def back(
-    count, lines, shard, cuts, grad_selected, small, weights, ext, conv_sum, grad_act, grad_gate,
-    mixer_low, normed, grad_middle, grad_step, rate_total, scan_rows, vectors, expert,
+    count, lines, shard, own_shard, cuts, grad_selected, small, weights, ext, conv_sum, grad_act, grad_gate,
+    mixer_low, normed, grad_middle, grad_step, rate_total, scan_rows, vectors, expert, far,
+    x, gain, kept,
 ):
     length, inner = conv_sum.shape
     width = normed.shape[1]
@@ -1240,16 +1300,29 @@
     dma = pltpu.SemaphoreType.DMA
     args = (
         grad_selected, small, weights, ext, conv_sum, grad_act, grad_gate, mixer_low, normed,
-        grad_middle, grad_step, rate_total, scan_rows, vectors, expert,
+        grad_middle, grad_step, rate_total, scan_rows, vectors, expert, far, x, gain, kept,
     )
     return pl.pallas_call(
         functools.partial(back_kernel, count, lines, cuts),
         in_specs=[vmem] * len(args),
-        out_specs=[vmem] * 4,
+        out_specs=[vmem] * 12,
         out_shape=[
-            jax.ShapeDtypeStruct((rows, width), jnp.float32),
-            jax.ShapeDtypeStruct((shard, columns), jnp.float32),
-            jax.ShapeDtypeStruct(vectors.shape, jnp.float32),
+            *[
+                jax.ShapeDtypeStruct(shape, jnp.float32)
+                for shape in (
+                    (rows, width),
+                    (2, own_shard, width),
+                    (own_shard, width),
+                    (own_shard, cuts.picks),
+                    (cuts.rank, own_shard),
+                    (cuts.state, own_shard),
+                    (cuts.kernel, own_shard),
+                    (1, own_shard),
+                    (1, own_shard),
+                    (1, own_shard),
+                    vectors.shape,
+                )
+            ],
             jax.ShapeDtypeStruct((expert.shape[1], 2 * expert.shape[2]), jnp.float32),
         ],
         scratch_shapes=[
@@ -1278,7 +1351,7 @@
 LAG = 3
 FAR_AT = 0
 NEAR_AT = 2
-PASS_AFTER = 0
+PASS_AT = 4
 SLOTS = 64
 
 
@@ -1293,11 +1366,11 @@
 
 def experts_kernel(
     count, lines, experts,
-    x_ref, mixer_ref, grad_ref, chosen_ref, table_ref, back_table_ref, gain_ref, router_ref,
+    x_ref, mixer_ref, grad_ref, route_ref, gain_ref, router_ref,
     up_ref, down_ref,
-    output_ref, grad_middle_ref, grad_low_ref, vectors_ref, grad_up_ref, grad_down_ref,
-    middle_ref, normed_ref, send_ref, rows_ref, made_ref, got_ref, act_ref, slope_ref, pre_ref,
-    send_sem, recv_sem, home_s, home_r,
+    output_ref, grad_middle_ref, grad_low_ref, vectors_ref, grad_up_ref, grad_down_ref, far_up_ref,
+    table_ref, back_table_ref, middle_ref, normed_ref, send_ref, rows_ref, made_ref, got_ref, act_ref, slope_ref, pre_ref,
+    send_sem, recv_sem, home_s, home_r, far_s, far_r,
 ):
     line, own, _, _ = place()
     q, f, low = square()
@@ -1309,8 +1382,10 @@
             pl.semaphore_signal(
                 barrier, inc=1, device_id=(lax.rem(line + d, lines), where), device_id_type=MESH
             )
-    pl.semaphore_signal(barrier, inc=1, device_id=(line, mate), device_id_type=MESH)
-    pl.semaphore_wait(barrier, 2 * lines - 1)
+    partner = seat_of(q, f, 1 - low)
+    for where in (mate, partner):
+        pl.semaphore_signal(barrier, inc=1, device_id=(line, where), device_id_type=MESH)
+    pl.semaphore_wait(barrier, 2 * lines)
 
     peers = [(j, d) for d in range(lines) for j in (1, 0) if (j, d) != (0, 0)]
 
@@ -1353,7 +1428,27 @@
     normed = (middle * scale * gain).astype(jnp.bfloat16)
     normed_ref[...] = normed
     rows, width = middle.shape
-    slots = table_ref.shape[0] // experts
+    slots = SLOTS
+    lane = lax.broadcasted_iota(jnp.int32, (rows, LANES), 1)
+    route_along = jnp.broadcast_to(route_ref[...].astype(jnp.float32), (rows, rows))
+    route_down = route_along.T[:, :LANES]
+    chosen = (route_down == lane.astype(jnp.float32)).astype(jnp.float32)
+    earlier = (
+        lax.broadcasted_iota(jnp.int32, (rows, rows), 0)
+        > lax.broadcasted_iota(jnp.int32, (rows, rows), 1)
+    ).astype(jnp.bfloat16)
+    before = dot_nn(earlier, chosen.astype(jnp.bfloat16))
+    slot_down = route_down[:, :1] * slots + jnp.sum(before * chosen, axis=1, keepdims=True)
+    slot_along = jnp.broadcast_to(slot_down, (rows, rows)).T[:1, :]
+    table_ref[...] = (
+        jnp.broadcast_to(slot_along, table_ref.shape)
+        == lax.broadcasted_iota(jnp.int32, table_ref.shape, 0).astype(jnp.float32)
+    ).astype(jnp.bfloat16)
+    for e in range(experts):
+        places = lax.broadcasted_iota(jnp.int32, (rows, slots), 1) + e * slots
+        back_table_ref[e] = (
+            jnp.broadcast_to(slot_down, (rows, slots)) == places.astype(jnp.float32)
+        ).astype(jnp.bfloat16)
 
     def dispatch(what, values):
         sent = dot_nn(table_ref[...], values).astype(jnp.bfloat16)
@@ -1364,11 +1459,17 @@
         rows_ref[what, 0, line] = send_ref[what, line // copies]
 
     dispatch(0, normed)
-    lane = lax.broadcasted_iota(jnp.int32, (rows, LANES), 1)
-    logits = jnp.where(lane < experts, outer_cols(normed, router_ref[...]), -jnp.inf)
+    router_f = jnp.concatenate(
+        [
+            router_ref[...].astype(jnp.float32),
+            jnp.zeros((LANES - experts, width), jnp.float32),
+        ],
+        axis=0,
+    )
+    router = router_f.astype(jnp.bfloat16)
+    logits = jnp.where(lane < experts, outer_cols(normed, router), -jnp.inf)
     grown = jnp.exp(logits - jnp.max(logits, axis=1, keepdims=True))
     probs = grown / jnp.sum(grown, axis=1, keepdims=True)
-    chosen = chosen_ref[...]
     gate = jnp.sum(chosen * probs, axis=1, keepdims=True)
     dispatch(1, (gate * grad_ref[...]).astype(jnp.bfloat16))
 
@@ -1436,6 +1537,18 @@
         return carry
 
     lax.fori_loop(0, parts, weigh, 0)
+
+    far_copies = []
+    for k in range(1, count // 4):
+        i = lax.rem(q + k, count // 4)
+        for j in (1, 0):
+            far_copies.append(
+                remote(
+                    grad_up_ref.at[seat_of(i, lax.rem(f + j, 2), 1 - low)], far_up_ref.at[j, i],
+                    far_s.at[j, i], far_r.at[j, i], line, partner,
+                )
+            )
+            far_copies[-1].start()
 
     def home(what):
         for j, d in peers:
@@ -1459,7 +1572,7 @@
     output_ref[...] = middle + gate * picked
     grad_gate = jnp.sum(grad * picked, axis=1, keepdims=True)
     grad_logits = gate * (chosen - probs) * grad_gate
-    grad_normed = home(1) + dot_nn(grad_logits, router_ref[...].astype(jnp.float32), HIGHEST)
+    grad_normed = home(1) + dot_nn(grad_logits, router_f, HIGHEST)
     scaled = gain * grad_normed
     grad_middle = (
         grad
@@ -1477,24 +1590,26 @@
         for j, d in peers:
             out_copy(what, j, d).wait_send()
             home_copy(what, j, d).wait_send()
+    for copy in far_copies:
+        copy.wait()
 
 
 def run_experts(
-    count, lines, experts, x, mixer, grad, chosen, table, back_table, gain, router, up, down
+    count, lines, experts, x, mixer, grad, route, gain, router, up, down
 ):
     rows, width = x.shape
-    slots = table.shape[0] // experts
+    slots = SLOTS
     total = 2 * lines * slots
     hidden = up.shape[1]
     pieces = (count, up.shape[0] // count, hidden)
     vmem = pl.BlockSpec(memory_space=pltpu.VMEM)
     dma = pltpu.SemaphoreType.DMA
-    args = (x, mixer, grad, chosen, table, back_table, gain, router, up, down)
+    args = (x, mixer, grad, route, gain, router, up, down)
     low = jnp.bfloat16
     return pl.pallas_call(
         functools.partial(experts_kernel, count, lines, experts),
         in_specs=[vmem] * len(args),
-        out_specs=[vmem] * 6,
+        out_specs=[vmem] * 7,
         out_shape=[
             jax.ShapeDtypeStruct((rows, width), jnp.float32),
             jax.ShapeDtypeStruct((rows, width), jnp.float32),
@@ -1502,8 +1617,11 @@
             jax.ShapeDtypeStruct((8, width), jnp.float32),
             jax.ShapeDtypeStruct(pieces, low),
             jax.ShapeDtypeStruct(pieces, low),
+            jax.ShapeDtypeStruct((2, count // 4, *pieces[1:]), low),
         ],
         scratch_shapes=[
+            pltpu.VMEM((experts * slots, rows), low),
+            pltpu.VMEM((experts, rows, slots), low),
             pltpu.VMEM((rows, width), jnp.float32),
             pltpu.VMEM((rows, width), low),
             pltpu.VMEM((2, experts, slots, width), low),
@@ -1514,6 +1632,7 @@
             pltpu.VMEM((total, hidden), low),
             pltpu.VMEM((total, hidden), jnp.float32),
             dma((2, 2, lines)), dma((2, 2, lines)), dma((2, 2, lines)), dma((2, 2, lines)),
+            dma((2, count // 4)), dma((2, count // 4)),
         ],
         compiler_params=pltpu.CompilerParams(
             collective_id=4, has_side_effects=True, vmem_limit_bytes=VMEM_LIMIT
@@ -1560,65 +1679,30 @@
 
     x_in = tokens.reshape(rows, width)
     gain_one = mixer_gain.astype(jnp.float32)
-    normed = rms_norm(x_in, gain_one).astype(jnp.bfloat16)
-
-    small = jnp.concatenate(
-        [
-            select_proj,
-            step_proj,
-            decay_log,
-            conv_weight,
-            conv_bias[None, :],
-            step_bias[None, :],
-            skip_gain[None, :],
-        ],
-        axis=0,
-    )
     small_pad = -(-cuts.rows // LANES) * LANES
-    small = jnp.pad(small, ((0, small_pad - cuts.rows), (0, 0)))
-    packed = jnp.concatenate(
-        [input_proj.reshape(2 * width, shard).T, output_proj, small.T], axis=1
-    )
-    packed = jnp.pad(packed, ((0, shard_rows - shard), (0, 0)))
     (normed_all, weights, small_all, conv_ext, conv_sum, conv_act, gate_branch, selected, up_cut) = (
-        front(count, lines, cuts, normed, packed, expert_up)
+        front(
+            count, lines, cuts, shard_rows, small_pad,
+            x_in, gain_one[None], input_proj.transpose(0, 2, 1), output_proj, select_proj.T,
+            step_proj, decay_log, conv_weight, conv_bias[None], step_bias[None], skip_gain[None],
+            expert_up,
+        )
     )
     pre, mixed, mixer_low, priors, end, mixer_out, down_cut = scan_forward(
         count, cuts, width, conv_act, gate_branch, selected, small_all, weights, expert_down.T
     )
 
     experts = router.shape[0]
-    route = routes.reshape(rows)
-    chosen = (route[:, None] == lax.broadcasted_iota(jnp.int32, (rows, LANES), 1)).astype(
-        jnp.float32
-    )
-    earlier = (
-        lax.broadcasted_iota(jnp.int32, (rows, rows), 0)
-        > lax.broadcasted_iota(jnp.int32, (rows, rows), 1)
-    ).astype(jnp.float32)
-    before = jnp.dot(earlier, chosen, precision=HIGHEST)
-    position = jnp.sum(before * chosen, axis=1).astype(jnp.int32)
-    slot = route * SLOTS + position
-    table = (
-        slot[None, :] == lax.broadcasted_iota(jnp.int32, (experts * SLOTS, rows), 0)
-    ).astype(jnp.bfloat16)
-    back_table = (
-        slot[None, :, None]
-        == lax.broadcasted_iota(jnp.int32, (experts, rows, SLOTS), 2)
-        + SLOTS * lax.broadcasted_iota(jnp.int32, (experts, rows, SLOTS), 0)
-    ).astype(jnp.bfloat16)
-    output, grad_middle, grad_middle_low, vectors, grad_up_low, grad_down_low = run_experts(
+    (output, grad_middle, grad_middle_low, vectors, grad_up_low, grad_down_low, far_up) = run_experts(
         count,
         lines,
         experts,
         x_in,
         mixer_out,
         cotangent.reshape(rows, width),
-        chosen,
-        table,
-        back_table,
+        routes.reshape(1, rows),
         expert_gain.astype(jnp.float32)[None],
-        jnp.pad(router, ((0, LANES - experts), (0, 0))),
+        router,
         up_cut.reshape(-1, up_cut.shape[2]),
         down_cut.reshape(-1, down_cut.shape[2]),
     )
@@ -1630,35 +1714,26 @@
             weights, priors, end, grad_down_low,
         )
     )
-    grad_normed, grad_shard, totals, grad_up = back(
-        count, lines, shard_rows, cuts, grad_selected, small_all, weights, conv_ext, conv_sum,
+    (grad_tokens, grad_input, grad_output, grad_select, grad_step, grad_decay, grad_taps,
+     grad_conv_bias, grad_step_bias, grad_skip, totals, grad_up) = back(
+        count, lines, shard_rows, shard, cuts, grad_selected, small_all, weights, conv_ext, conv_sum,
         grad_act, grad_gate_branch, mixer_low, normed_all.reshape(-1, width),
         grad_middle_all.reshape(-1, width), grad_step_w, rate_total, scan_rows, vectors,
-        grad_up_low,
-    )
-    grad_shard = grad_shard[:shard]
-    grad_input_w = grad_shard[:, : 2 * width].T.reshape(2, width, shard)
-    small_shard = grad_shard[:, 3 * width :].T
-    cut = 0
-    small_grads = []
-    for number in (picks, rank, state, kernel, 1, 1, 1):
-        small_grads.append(small_shard[cut : cut + number])
-        cut += number
-    unused_one, pull_one = jax.vjp(lambda v: rms_norm(v, gain_one), x_in)
-    grad_tokens = grad_middle + pull_one(grad_normed)[0]
+        grad_up_low, far_up, x_in, gain_one[None], grad_middle,
+    )
     return (
         output.reshape(tokens.shape),
         grad_tokens.reshape(tokens.shape),
         totals[0] / gain_one,
-        grad_input_w,
-        small_grads[3],
-        small_grads[4].reshape(shard),
-        small_grads[0],
-        small_grads[1],
-        small_grads[5].reshape(shard),
-        small_grads[2],
-        small_grads[6].reshape(shard),
-        grad_shard[:, 2 * width : 3 * width],
+        grad_input.transpose(0, 2, 1),
+        grad_taps,
+        grad_conv_bias.reshape(shard),
+        grad_select.T,
+        grad_step,
+        grad_step_bias.reshape(shard),
+        grad_decay,
+        grad_skip.reshape(shard),
+        grad_output,
         totals[1],
         totals[2 : 2 + experts],
         grad_up,

time: 548 us -> 527 us (0.962)
  other arithmetic: 10.7 us -> 0.61 us
  Pallas kernels: 516 us -> 508 us
    pallas_call x1, Pallas kernels: 125 us -> 116 us  [back(): pl.pallas_call(functools.partial(back_kernel, count, lines, cuts), in_spe...]
    unnamed x35 -> x39, local copies, waits for them, and re-layouts: 8.66 us -> 11.7 us
where the time goes in v6:
time: 527 us
  Pallas kernels  508 us (96%)
  local copies, waits for them, and re-layouts  17.2 us (3%)
    pallas_call x1, Pallas kernels, scan_backward(): pl.pallas_call(functools.partial(scan_backward_kernel, count, cuts), grid...  134 us
    pallas_call x1, Pallas kernels, back(): pl.pallas_call(functools.partial(back_kernel, count, lines, cuts), in_spe...  116 us
    pallas_call x1, Pallas kernels, front(): pl.pallas_call(functools.partial(front_kernel, count, lines, cuts), in_sp...  107 us
    pallas_call x1, Pallas kernels, scan_forward(): pl.pallas_call(functools.partial(scan_forward_kernel, count, cuts), grid=...  78.1 us
    pallas_call x1, Pallas kernels, run_experts(): pl.pallas_call(functools.partial(experts_kernel, count, lines, experts),...  73.7 us
    unnamed x39, local copies, waits for them, and re-layouts  11.7 us

profile of v6, /device:TPU:31, one launch (start us, length us, event | category | flops | bytes accessed | tf_op | source)
XLA Modules:
  0.0 526.9 jit_solution(8815429906639929138)
XLA Ops:
  0.6 1.3 broadcast_in_dim.18.gain_ref
  1.9 1.3 reshape.80.gain_ref
  3.2 106.8 %front.1 = (bf16[8,128,1152]{2,1,0:T(8,128)(2,1)}, bf16[384,3712]{1,0:T(8,128)(2,1)}, f32[256,384]{1,0:T(8,128)}, f32[1032,384]{1,0:T(8,128)}, f32[1024,384]{1,0...) custom-call(f32[128,1152]{1,0:T(8,128)} %bitcast.25, ...), custom_call_target="tpu_custom_call" | custom-call | flops 1811939328 | bytes 7864320 | tf_op jit(solution)/shard_map/front/pallas_call | solution.py:567
  110.0 78.1 %scan_forward.1 = (f32[1024,384]{1,0:T(8,128)}, f32[1024,384]{1,0:T(8,128)}, bf16[1024,384]{1,0:T(8,128)(2,1)}, f32[1024,16,384]{2,1,0:T(8,128)}, f32[16,384]{1,...) custom-call(f32[1024,384]{1,0:T(8,128)} %get-tuple-element.59.act_ref, ...), custom_call_target="tpu_custom_call" | custom-call | flops 50331648 | bytes 34603008 | tf_op jit(solution)/shard_map/scan_forward/pallas_call | solution.py:736
  188.2 73.7 %experts.1 = (f32[128,1152]{1,0:T(8,128)}, f32[128,1152]{1,0:T(8,128)}, bf16[128,1152]{1,0:T(8,128)(2,1)}, f32[8,1152]{1,0:T(8,128)}, bf16[8,144,1536]{2,1,0:T(8...) custom-call(f32[128,1152]{1,0:T(8,128)} %bitcast.26, ...), custom_call_target="tpu_custom_call" | custom-call | flops 10871635968 | bytes 14155776 | tf_op jit(solution)/shard_map/experts/pallas_call | solution.py:1609
  261.9 133.6 %scan_backward.1 = (bf16[1024,384]{1,0:T(8,128)(2,1)}, f32[1024,384]{1,0:T(8,128)}, f32[72,384]{1,0:T(8,128)}, f32[16,384]{1,0:T(8,128)}, f32[8,384]{1,0:T(8,128...) custom-call(bf16[128,1152]{1,0:T(8,128)(2,1)} %get-tuple-element.68.own_ref, ...), custom_call_target="tpu_custom_call" | custom-call | flops 125829120 | bytes 34603008 | tf_op jit(solution)/shard_map/scan_backward/pallas_call | solution.py:1060
  395.6 0.0 copy-start.7
  395.6 0.0 copy-start.3
  395.6 116.1 %back.1 = (f32[128,1152]{1,0:T(8,128)}, f32[2,72,1152]{2,1,0:T(8,128)}, f32[72,1152]{1,0:T(8,128)}, f32[72,104]{1,0:T(8,128)}, f32[72,72]{1,0:T(8,128)}, /*index...) custom-call(bf16[8,112,128]{2,1,0:T(8,128)(2,1)} %get-tuple-element., ...), custom_call_target="tpu_custom_call" | custom-call | flops 4529848320 | bytes 11796480 | tf_op jit(solution)/shard_map/back/pallas_call | solution.py:1305
  511.6 0.0 copy-start.2
  511.6 1.5 slice_reduce_fusion
  513.1 1.4 slice.11
  514.5 0.0 copy-done.7
  514.5 0.6 convert_divide_fusion
  515.1 0.0 copy-done.3
  515.1 0.0 copy-start.9
  515.1 0.0 copy-start.12
  515.1 0.0 copy-start.6
  515.1 0.0 copy-start.5
  515.1 0.0 copy-start.11
  515.1 0.0 copy-start.8
  515.2 0.0 copy-start.10
  515.2 0.0 copy-start.4
  515.2 0.8 copy.46
  516.0 0.0 copy-start.1
  516.0 2.0 copy.47
  518.0 0.0 copy-done.2
  518.0 0.8 copy.48
  518.9 0.0 copy-done.9
  518.9 0.6 copy.49
  519.5 0.0 copy-done.12
  519.5 0.5 copy.50
  520.0 0.0 copy-done.6
  520.0 0.6 copy.51
  520.6 0.0 copy-done.5
  520.6 0.6 copy.52
  521.2 0.0 copy-done.11
  521.2 0.5 copy.53
  521.7 0.0 copy-done.8
  521.7 0.6 copy.54
  522.3 0.0 copy-done.10
  522.3 0.5 copy.55
  522.9 0.0 copy-done.4
  522.9 0.7 copy.56
  523.6 0.0 copy-done.1
  523.6 1.2 copy.57
  524.8 0.9 copy-done
  525.7 1.2 copy.58
  (1 shorter events, 0.0 us)
Async XLA Ops:
  395.6 119.0 %copy-start.7 = (bf16[1152]{0:T(1024)(128)(2,1)S(1)}, bf16[1152]{0:T(1024)(128)(2,1)}, u32[]{:S(2)}) copy-start(bf16[1152]{0:T(1024)(128)(2,1)} %param.20) | copy-start | bytes 6916
  395.6 119.6 %copy-start.3 = (f32[128,1152]{1,0:T(8,128)S(1)}, f32[128,1152]{1,0:T(8,128)}, u32[]{:S(2)}) copy-start(f32[128,1152]{1,0:T(8,128)} %get-tuple-element.67) | copy-start | bytes 1769476
  511.6 6.4 %copy-start.2 = (f32[2,72,1152]{2,1,0:T(8,128)S(1)}, f32[2,72,1152]{2,1,0:T(8,128)}, u32[]{:S(2)}) copy-start(f32[2,72,1152]{2,1,0:T(8,128)} %get-tuple-element.91) | copy-start | bytes 1990660
  515.1 3.8 copy-start.9
  515.1 4.3 copy-start.12
  515.1 4.9 copy-start.6
  515.1 5.5 %copy-start.5 = (f32[72,72]{1,0:T(8,128)S(1)}, f32[72,72]{1,0:T(8,128)}, u32[]{:S(2)}) copy-start(f32[72,72]{1,0:T(8,128)} %get-tuple-element.127) | copy-start | bytes 62212
  515.1 6.1 %copy-start.11 = (f32[1,72]{1,0:T(1,128)S(1)}, f32[1,72]{1,0:T(1,128)}, u32[]{:S(2)}) copy-start(f32[1,72]{1,0:T(1,128)} %get-tuple-element.96) | copy-start | bytes 868
  515.1 6.6 %copy-start.8 = (f32[16,72]{1,0:T(8,128)S(1)}, f32[16,72]{1,0:T(8,128)}, u32[]{:S(2)}) copy-start(f32[16,72]{1,0:T(8,128)} %get-tuple-element.129) | copy-start | bytes 13828
  515.2 7.2 %copy-start.10 = (f32[1,72]{1,0:T(1,128)S(1)}, f32[1,72]{1,0:T(1,128)}, u32[]{:S(2)}) copy-start(f32[1,72]{1,0:T(1,128)} %get-tuple-element.98) | copy-start | bytes 868
  515.2 7.7 %copy-start.4 = (f32[72,1152]{1,0:T(8,128)S(1)}, f32[72,1152]{1,0:T(8,128)}, u32[]{:S(2)}) copy-start(f32[72,1152]{1,0:T(8,128)} %get-tuple-element.131) | copy-start | bytes 995332
  516.0 7.6 %copy-start.1 = (f32[144,3072]{1,0:T(8,128)S(1)}, f32[144,3072]{1,0:T(8,128)}, u32[]{:S(2)}) copy-start(f32[144,3072]{1,0:T(8,128)} %get-tuple-element.134) | copy-start | bytes 5308420
  523.6 2.1 copy-start

commit v7 on v6

--- a/solution.py
+++ b/solution.py
@@ -846,7 +846,7 @@
         rows_ref[...] = jnp.zeros_like(rows_ref)
         stage_ref[...] = jnp.zeros_like(stage_ref)
 
-    @pl.when(index == jnp.maximum(count - 3 - own, 0))
+    @pl.when(index == 0)
     def _():
         for k in range(1, half):
             along(k).start()
@@ -854,7 +854,7 @@
 
     @pl.when(index == 0)
     def _():
-        hand_over(now)
+        hand_over(now - 0)
         hand_over(now - 1)
 
     @pl.when(lax.rem(now, 2) != low)

time: 527 us -> 507 us (0.962)
  Pallas kernels: 508 us -> 487 us
    pallas_call x1, Pallas kernels: 134 us -> 119 us  [scan_backward(): pl.pallas_call(functools.partial(scan_backward_kernel, count, cuts), grid...]
    pallas_call x1, Pallas kernels: 116 us -> 110 us  [back(): pl.pallas_call(functools.partial(back_kernel, count, lines, cuts), in_spe...]
where the time goes in v7:
time: 507 us; the launch traced here: 506 us
  Pallas kernels  487 us (96%)
  local copies, waits for them, and re-layouts  17.2 us (3%)
    pallas_call x1, Pallas kernels, scan_backward(): pl.pallas_call(functools.partial(scan_backward_kernel, count, cuts), grid...  119 us
    pallas_call x1, Pallas kernels, back(): pl.pallas_call(functools.partial(back_kernel, count, lines, cuts), in_spe...  110 us
    pallas_call x1, Pallas kernels, front(): pl.pallas_call(functools.partial(front_kernel, count, lines, cuts), in_sp...  107 us
    pallas_call x1, Pallas kernels, scan_forward(): pl.pallas_call(functools.partial(scan_forward_kernel, count, cuts), grid=...  78.1 us
    pallas_call x1, Pallas kernels, run_experts(): pl.pallas_call(functools.partial(experts_kernel, count, lines, experts),...  73.7 us
    unnamed x39, local copies, waits for them, and re-layouts  11.7 us

profile of v7, /device:TPU:31, one launch (start us, length us, event | category | flops | bytes accessed | tf_op | source)
XLA Modules:
  0.0 505.9 jit_solution(261563849739447343)
XLA Ops:
  0.6 1.3 broadcast_in_dim.18.gain_ref
  1.9 1.3 reshape.80.gain_ref
  3.2 106.8 %front.1 = (bf16[8,128,1152]{2,1,0:T(8,128)(2,1)}, bf16[384,3712]{1,0:T(8,128)(2,1)}, f32[256,384]{1,0:T(8,128)}, f32[1032,384]{1,0:T(8,128)}, f32[1024,384]{1,0...) custom-call(f32[128,1152]{1,0:T(8,128)} %bitcast.25, ...), custom_call_target="tpu_custom_call" | custom-call | flops 1811939328 | bytes 7864320 | tf_op jit(solution)/shard_map/front/pallas_call | solution.py:567
  110.0 78.1 %scan_forward.1 = (f32[1024,384]{1,0:T(8,128)}, f32[1024,384]{1,0:T(8,128)}, bf16[1024,384]{1,0:T(8,128)(2,1)}, f32[1024,16,384]{2,1,0:T(8,128)}, f32[16,384]{1,...) custom-call(f32[1024,384]{1,0:T(8,128)} %get-tuple-element.59.act_ref, ...), custom_call_target="tpu_custom_call" | custom-call | flops 50331648 | bytes 34603008 | tf_op jit(solution)/shard_map/scan_forward/pallas_call | solution.py:736
  188.2 73.7 %experts.1 = (f32[128,1152]{1,0:T(8,128)}, f32[128,1152]{1,0:T(8,128)}, bf16[128,1152]{1,0:T(8,128)(2,1)}, f32[8,1152]{1,0:T(8,128)}, bf16[8,144,1536]{2,1,0:T(8...) custom-call(f32[128,1152]{1,0:T(8,128)} %bitcast.26, ...), custom_call_target="tpu_custom_call" | custom-call | flops 10871635968 | bytes 14155776 | tf_op jit(solution)/shard_map/experts/pallas_call | solution.py:1609
  261.9 119.1 %scan_backward.1 = (bf16[1024,384]{1,0:T(8,128)(2,1)}, f32[1024,384]{1,0:T(8,128)}, f32[72,384]{1,0:T(8,128)}, f32[16,384]{1,0:T(8,128)}, f32[8,384]{1,0:T(8,128...) custom-call(bf16[128,1152]{1,0:T(8,128)(2,1)} %get-tuple-element.68.own_ref, ...), custom_call_target="tpu_custom_call" | custom-call | flops 125829120 | bytes 34603008 | tf_op jit(solution)/shard_map/scan_backward/pallas_call | solution.py:1060
  381.0 0.0 copy-start.7
  381.0 0.0 copy-start.3
  381.0 109.7 %back.1 = (f32[128,1152]{1,0:T(8,128)}, f32[2,72,1152]{2,1,0:T(8,128)}, f32[72,1152]{1,0:T(8,128)}, f32[72,104]{1,0:T(8,128)}, f32[72,72]{1,0:T(8,128)}, /*index...) custom-call(bf16[8,112,128]{2,1,0:T(8,128)(2,1)} %get-tuple-element., ...), custom_call_target="tpu_custom_call" | custom-call | flops 4529848320 | bytes 11796480 | tf_op jit(solution)/shard_map/back/pallas_call | solution.py:1305
  490.7 0.0 copy-start.2
  490.7 1.5 slice_reduce_fusion
  492.1 1.4 slice.11
  493.5 0.0 copy-done.7
  493.5 0.6 convert_divide_fusion
  494.1 0.0 copy-done.3
  494.1 0.0 copy-start.9
  494.1 0.0 copy-start.12
  494.1 0.0 copy-start.5
  494.2 0.0 copy-start.11
  494.2 0.0 copy-start.8
  494.2 0.0 copy-start.10
  494.2 0.0 copy-start.4
  494.2 0.8 copy.46
  495.0 0.0 copy-start.1
  495.0 2.0 copy.47
  497.1 0.0 copy-done.2
  497.1 0.8 copy.48
  497.9 0.0 copy-done.9
  497.9 0.6 copy.49
  498.5 0.0 copy-done.12
  498.5 0.5 copy.50
  499.0 0.0 copy-done.6
  499.0 0.6 copy.51
  499.6 0.0 copy-done.5
  499.6 0.6 copy.52
  500.2 0.0 copy-done.11
  500.2 0.5 copy.53
  500.8 0.0 copy-done.8
  500.8 0.6 copy.54
  501.4 0.0 copy-done.10
  501.4 0.5 copy.55
  501.9 0.0 copy-done.4
  501.9 0.7 copy.56
  502.6 0.0 copy-done.1
  502.6 0.0 copy-start
  502.6 1.2 copy.57
  503.8 0.9 copy-done
  504.7 1.2 copy.58
  (1 shorter events, 0.0 us)
Async XLA Ops:
  381.0 112.6 %copy-start.7 = (bf16[1152]{0:T(1024)(128)(2,1)S(1)}, bf16[1152]{0:T(1024)(128)(2,1)}, u32[]{:S(2)}) copy-start(bf16[1152]{0:T(1024)(128)(2,1)} %param.20) | copy-start | bytes 6916
  381.0 113.2 %copy-start.3 = (f32[128,1152]{1,0:T(8,128)S(1)}, f32[128,1152]{1,0:T(8,128)}, u32[]{:S(2)}) copy-start(f32[128,1152]{1,0:T(8,128)} %get-tuple-element.67) | copy-start | bytes 1769476
  490.7 6.4 %copy-start.2 = (f32[2,72,1152]{2,1,0:T(8,128)S(1)}, f32[2,72,1152]{2,1,0:T(8,128)}, u32[]{:S(2)}) copy-start(f32[2,72,1152]{2,1,0:T(8,128)} %get-tuple-element.91) | copy-start | bytes 1990660
  494.1 3.8 copy-start.9
  494.1 4.3 copy-start.12
  494.1 4.9 copy-start.6
  494.1 5.5 %copy-start.5 = (f32[72,72]{1,0:T(8,128)S(1)}, f32[72,72]{1,0:T(8,128)}, u32[]{:S(2)}) copy-start(f32[72,72]{1,0:T(8,128)} %get-tuple-element.127) | copy-start | bytes 62212
  494.2 6.1 %copy-start.11 = (f32[1,72]{1,0:T(1,128)S(1)}, f32[1,72]{1,0:T(1,128)}, u32[]{:S(2)}) copy-start(f32[1,72]{1,0:T(1,128)} %get-tuple-element.96) | copy-start | bytes 868
  494.2 6.6 %copy-start.8 = (f32[16,72]{1,0:T(8,128)S(1)}, f32[16,72]{1,0:T(8,128)}, u32[]{:S(2)}) copy-start(f32[16,72]{1,0:T(8,128)} %get-tuple-element.129) | copy-start | bytes 13828
  494.2 7.2 %copy-start.10 = (f32[1,72]{1,0:T(1,128)S(1)}, f32[1,72]{1,0:T(1,128)}, u32[]{:S(2)}) copy-start(f32[1,72]{1,0:T(1,128)} %get-tuple-element.98) | copy-start | bytes 868
  494.2 7.7 %copy-start.4 = (f32[72,1152]{1,0:T(8,128)S(1)}, f32[72,1152]{1,0:T(8,128)}, u32[]{:S(2)}) copy-start(f32[72,1152]{1,0:T(8,128)} %get-tuple-element.131) | copy-start | bytes 995332
  495.0 7.6 %copy-start.1 = (f32[144,3072]{1,0:T(8,128)S(1)}, f32[144,3072]{1,0:T(8,128)}, u32[]{:S(2)}) copy-start(f32[144,3072]{1,0:T(8,128)} %get-tuple-element.134) | copy-start | bytes 5308420
  502.6 2.1 copy-start

commit v8 on v7

--- a/solution.py
+++ b/solution.py
@@ -254,6 +254,15 @@
             self.along(j, k).start()
         self.pair(j, 0, self.low).start()
 
+    def arrive(self):
+        for j in range(2):
+            for k in range(1, self.quarter):
+                piece = self.piece(j, k, self.low)
+                remote(
+                    self.land.at[piece], self.land.at[piece], self.line_s.at[j, k],
+                    self.line_r.at[j, k], self.line, piece,
+                ).wait_recv()
+
     def forward(self, j):
         for k in range(1, self.quarter):
             piece = self.piece(j, k, self.low)
@@ -263,15 +272,16 @@
             ).wait_recv()
             self.pair(j, k, self.low).start()
 
-    def finish(self):
+    def finish(self, passed=True):
+        crossed = range(self.quarter) if passed else (0,)
         for j in range(2):
-            for k in range(self.quarter):
+            for k in crossed:
                 self.pair(j, k, 1 - self.low).wait_recv()
         self.swap().wait_send()
         for j in range(2):
             for k in range(1, self.quarter):
                 self.along(j, k).wait_send()
-            for k in range(self.quarter):
+            for k in crossed:
                 self.pair(j, k, self.low).wait_send()
 
 
@@ -719,10 +729,9 @@
     def _():
         for late in range(LAG - 1, -1, -1):
             pass_on(step - late)
-        gather.forward(0)
-        gather.forward(1)
+        gather.arrive()
         summed_ref[...] = relay.finish()
-        gather.finish()
+        gather.finish(False)
         expert_out_ref[...] = land_ref[...]
 
 
@@ -1367,10 +1376,11 @@
 def experts_kernel(
     count, lines, experts,
     x_ref, mixer_ref, grad_ref, route_ref, gain_ref, router_ref,
-    up_ref, down_ref,
+    up_ref, held_ref,
     output_ref, grad_middle_ref, grad_low_ref, vectors_ref, grad_up_ref, grad_down_ref, far_up_ref,
-    table_ref, back_table_ref, middle_ref, normed_ref, send_ref, rows_ref, made_ref, got_ref, act_ref, slope_ref, pre_ref,
+    table_ref, back_table_ref, down_ref, middle_ref, normed_ref, send_ref, rows_ref, made_ref, got_ref, act_ref, slope_ref, pre_ref,
     send_sem, recv_sem, home_s, home_r, far_s, far_r,
+    pass_s, pass_r,
 ):
     line, own, _, _ = place()
     q, f, low = square()
@@ -1386,6 +1396,23 @@
     for where in (mate, partner):
         pl.semaphore_signal(barrier, inc=1, device_id=(line, where), device_id_type=MESH)
     pl.semaphore_wait(barrier, 2 * lines)
+
+    quarter = count // 4
+    piece_rows = held_ref.shape[0] // count
+
+    def piece(j, k, member):
+        at = seat_of(lax.rem(q - k + quarter, quarter), lax.rem(f + j, 2), member)
+        return pl.ds(pl.multiple_of(at * piece_rows, piece_rows), piece_rows)
+
+    def crossing(j, k, member):
+        here = piece(j, k, member)
+        return remote(
+            held_ref.at[here], down_ref.at[here], pass_s.at[j, k], pass_r.at[j, k], line, partner
+        )
+
+    for j in range(2):
+        for k in range(1, quarter):
+            crossing(j, k, low).start()
 
     peers = [(j, d) for d in range(lines) for j in (1, 0) if (j, d) != (0, 0)]
 
@@ -1484,6 +1511,12 @@
     def columns(c):
         return pl.ds(pl.multiple_of(c * chunk, LANES), chunk)
 
+    for j in range(2):
+        for k in range(quarter):
+            here = piece(j, k, low)
+            down_ref[here, :] = held_ref[here, :]
+        here = piece(j, 0, 1 - low)
+        down_ref[here, :] = held_ref[here, :]
     for j, d in peers:
         arrived(0, j, d).wait_recv()
 
@@ -1516,6 +1549,9 @@
 
     for j, d in peers:
         arrived(1, j, d).wait_recv()
+    for j in range(2):
+        for k in range(1, quarter):
+            crossing(j, k, 1 - low).wait_recv()
 
     def fall(c, carry):
         slope_ref[:, columns(c)] = (
@@ -1592,6 +1628,9 @@
             home_copy(what, j, d).wait_send()
     for copy in far_copies:
         copy.wait()
+    for j in range(2):
+        for k in range(1, quarter):
+            crossing(j, k, low).wait_send()
 
 
 def run_experts(
@@ -1622,6 +1661,7 @@
         scratch_shapes=[
             pltpu.VMEM((experts * slots, rows), low),
             pltpu.VMEM((experts, rows, slots), low),
+            pltpu.VMEM(down.shape, low),
             pltpu.VMEM((rows, width), jnp.float32),
             pltpu.VMEM((rows, width), low),
             pltpu.VMEM((2, experts, slots, width), low),
@@ -1632,7 +1672,7 @@
             pltpu.VMEM((total, hidden), low),
             pltpu.VMEM((total, hidden), jnp.float32),
             dma((2, 2, lines)), dma((2, 2, lines)), dma((2, 2, lines)), dma((2, 2, lines)),
-            dma((2, count // 4)), dma((2, count // 4)),
+            dma((2, count // 4)), dma((2, count // 4)), dma((2, count // 4)), dma((2, count // 4)),
         ],
         compiler_params=pltpu.CompilerParams(
             collective_id=4, has_side_effects=True, vmem_limit_bytes=VMEM_LIMIT

time: 507 us -> 503 us (level)
  no operation moved by 1% of the time
where the time goes in v8:
time: 503 us
  Pallas kernels  484 us (96%)
  local copies, waits for them, and re-layouts  17.2 us (3%)
    pallas_call x1, Pallas kernels, scan_backward(): pl.pallas_call(functools.partial(scan_backward_kernel, count, cuts), grid...  121 us
    pallas_call x1, Pallas kernels, back(): pl.pallas_call(functools.partial(back_kernel, count, lines, cuts), in_spe...  108 us
    pallas_call x1, Pallas kernels, front(): pl.pallas_call(functools.partial(front_kernel, count, lines, cuts), in_sp...  107 us
    pallas_call x1, Pallas kernels, run_experts(): pl.pallas_call(functools.partial(experts_kernel, count, lines, experts),...  74.6 us
    pallas_call x1, Pallas kernels, scan_forward(): pl.pallas_call(functools.partial(scan_forward_kernel, count, cuts), grid=...  73.2 us
    unnamed x39, local copies, waits for them, and re-layouts  11.7 us

profile of v8, /device:TPU:31, one launch (start us, length us, event | category | flops | bytes accessed | tf_op | source)
XLA Modules:
  0.0 502.5 jit_solution(8275246777503969699)
XLA Ops:
  0.6 1.3 broadcast_in_dim.18.gain_ref
  1.9 1.3 reshape.80.gain_ref
  3.2 106.8 %front.1 = (bf16[8,128,1152]{2,1,0:T(8,128)(2,1)}, bf16[384,3712]{1,0:T(8,128)(2,1)}, f32[256,384]{1,0:T(8,128)}, f32[1032,384]{1,0:T(8,128)}, f32[1024,384]{1,0...) custom-call(f32[128,1152]{1,0:T(8,128)} %bitcast.25, ...), custom_call_target="tpu_custom_call" | custom-call | flops 1811939328 | bytes 7864320 | tf_op jit(solution)/shard_map/front/pallas_call | solution.py:577
  110.0 73.2 %scan_forward.1 = (f32[1024,384]{1,0:T(8,128)}, f32[1024,384]{1,0:T(8,128)}, bf16[1024,384]{1,0:T(8,128)(2,1)}, f32[1024,16,384]{2,1,0:T(8,128)}, f32[16,384]{1,...) custom-call(f32[1024,384]{1,0:T(8,128)} %get-tuple-element.59.act_ref, ...), custom_call_target="tpu_custom_call" | custom-call | flops 50331648 | bytes 34603008 | tf_op jit(solution)/shard_map/scan_forward/pallas_call | solution.py:745
  183.2 74.6 %experts.1 = (f32[128,1152]{1,0:T(8,128)}, f32[128,1152]{1,0:T(8,128)}, bf16[128,1152]{1,0:T(8,128)(2,1)}, f32[8,1152]{1,0:T(8,128)}, bf16[8,144,1536]{2,1,0:T(8...) custom-call(f32[128,1152]{1,0:T(8,128)} %bitcast.26, ...), custom_call_target="tpu_custom_call" | custom-call | flops 10871635968 | bytes 14155776 | tf_op jit(solution)/shard_map/experts/pallas_call | solution.py:1648
  257.8 121.3 %scan_backward.1 = (bf16[1024,384]{1,0:T(8,128)(2,1)}, f32[1024,384]{1,0:T(8,128)}, f32[72,384]{1,0:T(8,128)}, f32[16,384]{1,0:T(8,128)}, f32[8,384]{1,0:T(8,128...) custom-call(bf16[128,1152]{1,0:T(8,128)(2,1)} %get-tuple-element.68.own_ref, ...), custom_call_target="tpu_custom_call" | custom-call | flops 125829120 | bytes 34603008 | tf_op jit(solution)/shard_map/scan_backward/pallas_call | solution.py:1069
  379.0 0.0 copy-start.7
  379.0 0.0 copy-start.3
  379.1 108.2 %back.1 = (f32[128,1152]{1,0:T(8,128)}, f32[2,72,1152]{2,1,0:T(8,128)}, f32[72,1152]{1,0:T(8,128)}, f32[72,104]{1,0:T(8,128)}, f32[72,72]{1,0:T(8,128)}, /*index...) custom-call(bf16[8,112,128]{2,1,0:T(8,128)(2,1)} %get-tuple-element., ...), custom_call_target="tpu_custom_call" | custom-call | flops 4529848320 | bytes 11796480 | tf_op jit(solution)/shard_map/back/pallas_call | solution.py:1314
  487.3 0.0 copy-start.2
  487.3 1.5 slice_reduce_fusion
  488.8 1.4 slice.11
  490.1 0.0 copy-done.7
  490.1 0.6 convert_divide_fusion
  490.7 0.0 copy-done.3
  490.8 0.0 copy-start.9
  490.8 0.0 copy-start.12
  490.8 0.0 copy-start.6
  490.8 0.0 copy-start.5
  490.8 0.0 copy-start.11
  490.8 0.0 copy-start.8
  490.8 0.0 copy-start.10
  490.8 0.0 copy-start.4
  490.8 0.8 copy.46
  491.6 0.0 copy-start.1
  491.6 2.0 copy.47
  493.7 0.0 copy-done.2
  493.7 0.8 copy.48
  494.5 0.0 copy-done.9
  494.5 0.6 copy.49
  495.1 0.0 copy-done.12
  495.1 0.5 copy.50
  495.6 0.0 copy-done.6
  495.6 0.6 copy.51
  496.2 0.0 copy-done.5
  496.2 0.6 copy.52
  496.9 0.0 copy-done.11
  496.9 0.5 copy.53
  497.4 0.0 copy-done.8
  497.4 0.6 copy.54
  498.0 0.0 copy-done.10
  498.0 0.5 copy.55
  498.5 0.0 copy-done.4
  498.5 0.7 copy.56
  499.2 0.0 copy-done.1
  499.2 1.2 copy.57
  500.4 0.9 copy-done
  501.3 1.2 copy.58
  (1 shorter events, 0.0 us)
Async XLA Ops:
  379.0 111.1 %copy-start.7 = (bf16[1152]{0:T(1024)(128)(2,1)S(1)}, bf16[1152]{0:T(1024)(128)(2,1)}, u32[]{:S(2)}) copy-start(bf16[1152]{0:T(1024)(128)(2,1)} %param.20) | copy-start | bytes 6916
  379.0 111.7 %copy-start.3 = (f32[128,1152]{1,0:T(8,128)S(1)}, f32[128,1152]{1,0:T(8,128)}, u32[]{:S(2)}) copy-start(f32[128,1152]{1,0:T(8,128)} %get-tuple-element.67) | copy-start | bytes 1769476
  487.3 6.4 %copy-start.2 = (f32[2,72,1152]{2,1,0:T(8,128)S(1)}, f32[2,72,1152]{2,1,0:T(8,128)}, u32[]{:S(2)}) copy-start(f32[2,72,1152]{2,1,0:T(8,128)} %get-tuple-element.91) | copy-start | bytes 1990660
  490.8 3.8 copy-start.9
  490.8 4.3 copy-start.12
  490.8 4.9 copy-start.6
  490.8 5.5 %copy-start.5 = (f32[72,72]{1,0:T(8,128)S(1)}, f32[72,72]{1,0:T(8,128)}, u32[]{:S(2)}) copy-start(f32[72,72]{1,0:T(8,128)} %get-tuple-element.127) | copy-start | bytes 62212
  490.8 6.1 %copy-start.11 = (f32[1,72]{1,0:T(1,128)S(1)}, f32[1,72]{1,0:T(1,128)}, u32[]{:S(2)}) copy-start(f32[1,72]{1,0:T(1,128)} %get-tuple-element.96) | copy-start | bytes 868
  490.8 6.6 %copy-start.8 = (f32[16,72]{1,0:T(8,128)S(1)}, f32[16,72]{1,0:T(8,128)}, u32[]{:S(2)}) copy-start(f32[16,72]{1,0:T(8,128)} %get-tuple-element.129) | copy-start | bytes 13828
  490.8 7.2 %copy-start.10 = (f32[1,72]{1,0:T(1,128)S(1)}, f32[1,72]{1,0:T(1,128)}, u32[]{:S(2)}) copy-start(f32[1,72]{1,0:T(1,128)} %get-tuple-element.98) | copy-start | bytes 868
  490.8 7.7 %copy-start.4 = (f32[72,1152]{1,0:T(8,128)S(1)}, f32[72,1152]{1,0:T(8,128)}, u32[]{:S(2)}) copy-start(f32[72,1152]{1,0:T(8,128)} %get-tuple-element.131) | copy-start | bytes 995332
  491.6 7.6 %copy-start.1 = (f32[144,3072]{1,0:T(8,128)S(1)}, f32[144,3072]{1,0:T(8,128)}, u32[]{:S(2)}) copy-start(f32[144,3072]{1,0:T(8,128)} %get-tuple-element.134) | copy-start | bytes 5308420
  499.2 2.1 copy-start

commit v9 on v8

--- a/solution.py
+++ b/solution.py
@@ -1360,7 +1360,7 @@
 LAG = 3
 FAR_AT = 0
 NEAR_AT = 2
-PASS_AT = 4
+PASS_AT = 3
 SLOTS = 64
 
 
@@ -1561,18 +1561,14 @@
 
     lax.fori_loop(0, parts, fall, 0)
     send_home(1, slope_ref, up_ref)
-    send_home(0, act_ref, down_ref)
-
     pieces = grad_up_ref.shape[1]
 
-    def weigh(c, carry):
+    def weigh_up(c, carry):
         up = inner_rows(rows_of(rows_ref, 0), slope_ref[:, columns(c)]).astype(jnp.bfloat16)
-        down = inner_rows(rows_of(rows_ref, 1), act_ref[:, columns(c)]).astype(jnp.bfloat16)
         grad_up_ref[:, :, columns(c)] = up.reshape(count, pieces, chunk)
-        grad_down_ref[:, :, columns(c)] = down.reshape(count, pieces, chunk)
         return carry
 
-    lax.fori_loop(0, parts, weigh, 0)
+    lax.fori_loop(0, parts, weigh_up, 0)
 
     far_copies = []
     for k in range(1, count // 4):
@@ -1585,6 +1581,14 @@
                 )
             )
             far_copies[-1].start()
+
+    send_home(0, act_ref, down_ref)
+    def weigh_down(c, carry):
+        down = inner_rows(rows_of(rows_ref, 1), act_ref[:, columns(c)]).astype(jnp.bfloat16)
+        grad_down_ref[:, :, columns(c)] = down.reshape(count, pieces, chunk)
+        return carry
+
+    lax.fori_loop(0, parts, weigh_down, 0)
 
     def home(what):
         for j, d in peers:

time: 503 us -> 503 us (level)
  no operation moved by 1% of the time
where the time goes in v9:
time: 503 us; the launch traced here: 502 us
  Pallas kernels  484 us (96%)
  local copies, waits for them, and re-layouts  17.2 us (3%)
    pallas_call x1, Pallas kernels, scan_backward(): pl.pallas_call(functools.partial(scan_backward_kernel, count, cuts), grid...  119 us
    pallas_call x1, Pallas kernels, back(): pl.pallas_call(functools.partial(back_kernel, count, lines, cuts), in_spe...  110 us
    pallas_call x1, Pallas kernels, front(): pl.pallas_call(functools.partial(front_kernel, count, lines, cuts), in_sp...  107 us
    pallas_call x1, Pallas kernels, run_experts(): pl.pallas_call(functools.partial(experts_kernel, count, lines, experts),...  74.6 us
    pallas_call x1, Pallas kernels, scan_forward(): pl.pallas_call(functools.partial(scan_forward_kernel, count, cuts), grid=...  73.2 us
    unnamed x39, local copies, waits for them, and re-layouts  11.7 us

profile of v9, /device:TPU:31, one launch (start us, length us, event | category | flops | bytes accessed | tf_op | source)
XLA Modules:
  0.0 502.1 jit_solution(8532453989277542395)
XLA Ops:
  0.6 1.3 broadcast_in_dim.18.gain_ref
  1.9 1.3 reshape.80.gain_ref
  3.2 106.8 %front.1 = (bf16[8,128,1152]{2,1,0:T(8,128)(2,1)}, bf16[384,3712]{1,0:T(8,128)(2,1)}, f32[256,384]{1,0:T(8,128)}, f32[1032,384]{1,0:T(8,128)}, f32[1024,384]{1,0...) custom-call(f32[128,1152]{1,0:T(8,128)} %bitcast.25, ...), custom_call_target="tpu_custom_call" | custom-call | flops 1811939328 | bytes 7864320 | tf_op jit(solution)/shard_map/front/pallas_call | solution.py:577
  110.0 73.2 %scan_forward.1 = (f32[1024,384]{1,0:T(8,128)}, f32[1024,384]{1,0:T(8,128)}, bf16[1024,384]{1,0:T(8,128)(2,1)}, f32[1024,16,384]{2,1,0:T(8,128)}, f32[16,384]{1,...) custom-call(f32[1024,384]{1,0:T(8,128)} %get-tuple-element.59.act_ref, ...), custom_call_target="tpu_custom_call" | custom-call | flops 50331648 | bytes 34603008 | tf_op jit(solution)/shard_map/scan_forward/pallas_call | solution.py:745
  183.2 74.6 %experts.1 = (f32[128,1152]{1,0:T(8,128)}, f32[128,1152]{1,0:T(8,128)}, bf16[128,1152]{1,0:T(8,128)(2,1)}, f32[8,1152]{1,0:T(8,128)}, bf16[8,144,1536]{2,1,0:T(8...) custom-call(f32[128,1152]{1,0:T(8,128)} %bitcast.26, ...), custom_call_target="tpu_custom_call" | custom-call | flops 10871635968 | bytes 14155776 | tf_op jit(solution)/shard_map/experts/pallas_call | solution.py:1652
  257.8 119.2 %scan_backward.1 = (bf16[1024,384]{1,0:T(8,128)(2,1)}, f32[1024,384]{1,0:T(8,128)}, f32[72,384]{1,0:T(8,128)}, f32[16,384]{1,0:T(8,128)}, f32[8,384]{1,0:T(8,128...) custom-call(bf16[128,1152]{1,0:T(8,128)(2,1)} %get-tuple-element.68.own_ref, ...), custom_call_target="tpu_custom_call" | custom-call | flops 125829120 | bytes 34603008 | tf_op jit(solution)/shard_map/scan_backward/pallas_call | solution.py:1069
  377.0 0.0 copy-start.7
  377.0 0.0 copy-start.3
  377.0 109.9 %back.1 = (f32[128,1152]{1,0:T(8,128)}, f32[2,72,1152]{2,1,0:T(8,128)}, f32[72,1152]{1,0:T(8,128)}, f32[72,104]{1,0:T(8,128)}, f32[72,72]{1,0:T(8,128)}, /*index...) custom-call(bf16[8,112,128]{2,1,0:T(8,128)(2,1)} %get-tuple-element., ...), custom_call_target="tpu_custom_call" | custom-call | flops 4529848320 | bytes 11796480 | tf_op jit(solution)/shard_map/back/pallas_call | solution.py:1314
  486.9 0.0 copy-start.2
  486.9 1.5 slice_reduce_fusion
  488.4 1.4 slice.11
  489.7 0.0 copy-done.7
  489.7 0.6 convert_divide_fusion
  490.3 0.0 copy-done.3
  490.3 0.0 copy-start.9
  490.4 0.0 copy-start.12
  490.4 0.0 copy-start.6
  490.4 0.0 copy-start.5
  490.4 0.0 copy-start.11
  490.4 0.0 copy-start.8
  490.4 0.0 copy-start.10
  490.4 0.0 copy-start.4
  490.4 0.8 copy.46
  491.2 0.0 copy-start.1
  491.2 2.0 copy.47
  493.3 0.0 copy-done.2
  493.3 0.8 copy.48
  494.1 0.0 copy-done.9
  494.1 0.6 copy.49
  494.7 0.0 copy-done.12
  494.7 0.5 copy.50
  495.2 0.0 copy-done.6
  495.2 0.6 copy.51
  495.8 0.0 copy-done.5
  495.8 0.6 copy.52
  496.5 0.0 copy-done.11
  496.5 0.5 copy.53
  497.0 0.0 copy-done.8
  497.0 0.6 copy.54
  497.6 0.0 copy-done.10
  497.6 0.5 copy.55
  498.1 0.0 copy-done.4
  498.1 0.7 copy.56
  498.8 0.0 copy-done.1
  498.8 1.2 copy.57
  500.0 0.9 copy-done
  500.9 1.2 copy.58
  (1 shorter events, 0.0 us)
Async XLA Ops:
  377.0 112.8 %copy-start.7 = (bf16[1152]{0:T(1024)(128)(2,1)S(1)}, bf16[1152]{0:T(1024)(128)(2,1)}, u32[]{:S(2)}) copy-start(bf16[1152]{0:T(1024)(128)(2,1)} %param.20) | copy-start | bytes 6916
  377.0 113.4 %copy-start.3 = (f32[128,1152]{1,0:T(8,128)S(1)}, f32[128,1152]{1,0:T(8,128)}, u32[]{:S(2)}) copy-start(f32[128,1152]{1,0:T(8,128)} %get-tuple-element.67) | copy-start | bytes 1769476
  486.9 6.4 %copy-start.2 = (f32[2,72,1152]{2,1,0:T(8,128)S(1)}, f32[2,72,1152]{2,1,0:T(8,128)}, u32[]{:S(2)}) copy-start(f32[2,72,1152]{2,1,0:T(8,128)} %get-tuple-element.91) | copy-start | bytes 1990660
  490.3 3.8 copy-start.9
  490.4 4.3 copy-start.12
  490.4 4.9 copy-start.6
  490.4 5.5 %copy-start.5 = (f32[72,72]{1,0:T(8,128)S(1)}, f32[72,72]{1,0:T(8,128)}, u32[]{:S(2)}) copy-start(f32[72,72]{1,0:T(8,128)} %get-tuple-element.127) | copy-start | bytes 62212
  490.4 6.1 %copy-start.11 = (f32[1,72]{1,0:T(1,128)S(1)}, f32[1,72]{1,0:T(1,128)}, u32[]{:S(2)}) copy-start(f32[1,72]{1,0:T(1,128)} %get-tuple-element.96) | copy-start | bytes 868
  490.4 6.6 %copy-start.8 = (f32[16,72]{1,0:T(8,128)S(1)}, f32[16,72]{1,0:T(8,128)}, u32[]{:S(2)}) copy-start(f32[16,72]{1,0:T(8,128)} %get-tuple-element.129) | copy-start | bytes 13828
  490.4 7.2 %copy-start.10 = (f32[1,72]{1,0:T(1,128)S(1)}, f32[1,72]{1,0:T(1,128)}, u32[]{:S(2)}) copy-start(f32[1,72]{1,0:T(1,128)} %get-tuple-element.98) | copy-start | bytes 868
  490.4 7.7 %copy-start.4 = (f32[72,1152]{1,0:T(8,128)S(1)}, f32[72,1152]{1,0:T(8,128)}, u32[]{:S(2)}) copy-start(f32[72,1152]{1,0:T(8,128)} %get-tuple-element.131) | copy-start | bytes 995332
  491.2 7.6 %copy-start.1 = (f32[144,3072]{1,0:T(8,128)S(1)}, f32[144,3072]{1,0:T(8,128)}, u32[]{:S(2)}) copy-start(f32[144,3072]{1,0:T(8,128)} %get-tuple-element.134) | copy-start | bytes 5308420
  498.8 2.1 copy-start
